TPU v7x, 32 devices: a whole 2x2x4 slice. The times are simulated.
32 devices in a mesh: groups: 2 (over y), slab: 4 (over z), pole: 2 (over x), sub: 2 (over core).
Axes of the slice: x: 2, y: 2, z: 4, core: 2. Of those that a mesh axis runs over, the one named last changes fastest.
Arguments:
- onsite: float32 [8, 2, 128, 128], P(('groups', 'slab')), parts along dimension 0, may hold values from -0.5 to 0.5
- coupling: float32 [8, 2, 128, 128], P(('groups', 'slab')), parts along dimension 0, may hold values from -0.25 to 0.25
- pole_real: float32 [4], P(('pole', 'sub')), may hold values from -2 to 2
- pole_imag: float32 [4], P(('pole', 'sub')), may hold values from 0.1 to 1
- pole_weight: float32 [4, 2], P(('pole', 'sub')), may hold values from -4 to 4
Outputs:
- density: float32 [8, 2, 128, 128], P(('groups', 'slab'), None, ('pole', 'sub')), parts along dimension 0
- energy_density: float32 [8, 2, 128, 128], P(('groups', 'slab'), None, ('pole', 'sub')), parts along dimension 0
There are 2 independent parts, one for each index of `groups`. A program takes and returns all parts, laid end to end along the dimension named above; an argument that names none is the same for every part. Nothing has to cross between parts.
All inputs are finite; a program needn't handle non-finite values.
Results may differ from a plain program's by a relative error of at most 0.0003.
Values sent between devices are 32-bit elements; how exact they have to be, the bound alone decides.
No kernel may reach another device: no remote copies, remote signals or barrier semaphores. Data moves between devices by JAX's collectives and lax.ppermute only.
A program may use at most 128 MiB of HBM per device.

v0:
```python
import functools

import jax
import jax.numpy as jnp
from jax import lax
from jax.experimental import pallas as pl
from jax.experimental.pallas import tpu as pltpu
from jax.sharding import PartitionSpec as P

ROWS = 8
precise = lax.Precision.HIGHEST
f32 = jnp.float32


def row_of(tile, k):
    return jnp.broadcast_to(tile[k : k + 1, :], tile.shape)


def lane_of(tile, k):
    return jnp.broadcast_to(tile[:, k : k + 1], tile.shape)


def sweep_panel(xr, xi, first, lane, subl):
    cols = [(lane_of(xr, first + j), lane_of(xi, first + j)) for j in range(ROWS)]
    for k in range(ROWS):
        tr, ti = cols[k]
        dr, di = row_of(tr, k), row_of(ti, k)
        scale = 1.0 / (dr * dr + di * di)
        rr, ri = dr * scale, -di * scale
        cr, ci = tr - (subl == k).astype(f32), ti
        for j in range(k + 1, ROWS):
            ar, ai = row_of(cols[j][0], k), row_of(cols[j][1], k)
            br, bi = ar * rr - ai * ri, ar * ri + ai * rr
            cols[j] = (cols[j][0] - (cr * br - ci * bi), cols[j][1] - (cr * bi + ci * br))
        ar, ai = row_of(xr, k) + (lane == first + k).astype(f32), row_of(xi, k)
        br, bi = ar * rr - ai * ri, ar * ri + ai * rr
        xr, xi = xr - (cr * br - ci * bi), xi - (cr * bi + ci * br)
    return xr, xi


def invert_into(src, dst):
    order = src.shape[-1]
    count = order // ROWS
    lane = lax.broadcasted_iota(jnp.int32, (ROWS, order), 1)
    subl = lax.broadcasted_iota(jnp.int32, (ROWS, order), 0)
    re = [src[0, ROWS * i : ROWS * i + ROWS, :] for i in range(count)]
    im = [src[1, ROWS * i : ROWS * i + ROWS, :] for i in range(count)]
    for p in range(count):
        first = ROWS * p
        xr, xi = sweep_panel(re[p], im[p], first, lane, subl)
        rows = [(row_of(xr, k), row_of(xi, k)) for k in range(ROWS)]
        inside = (lane >= first) & (lane < first + ROWS)
        for q in range(1, count):
            i = (p + q) % count
            ar, ai = re[i], im[i]
            nr, ni = jnp.where(inside, 0.0, ar), jnp.where(inside, 0.0, ai)
            for k in range(ROWS):
                cr, ci = lane_of(ar, first + k), lane_of(ai, first + k)
                ur, ui = rows[k]
                nr = nr - cr * ur + ci * ui
                ni = ni - cr * ui - ci * ur
            re[i], im[i] = nr, ni
        re[p], im[p] = xr, xi
    for i in range(count):
        dst[0, ROWS * i : ROWS * i + ROWS, :] = re[i]
        dst[1, ROWS * i : ROWS * i + ROWS, :] = im[i]


def dot(a, b):
    return lax.dot_general(a, b, (((1,), (0,)), ((), ())), precision=precise, preferred_element_type=f32)


def product(a, b):
    order = a[0].shape[0]
    whole = dot(jnp.concatenate(a, axis=0), jnp.concatenate(b, axis=1))
    real = whole[:order, :order] - whole[order:, order:]
    imag = whole[:order, order:] + whole[order:, :order]
    return real, imag


def adjoint(a):
    return a[0].T, -a[1].T


def pair(ref, *index):
    return ref[(*index, 0)], ref[(*index, 1)]


def kernel(
    slabs, poles, place, pole, onsite, coupling, *refs
):
    gathered, refs = refs[: 2 * (slabs - 1)], refs[2 * (slabs - 1) :]
    outs, (blocks, links, work, inverses, pivot, greens) = refs[:poles], refs[poles:]
    me, mine, sub = place[0], place[1], place[2]
    half = slabs // 2
    order = onsite.shape[-1]
    blocks[me] = onsite[0]
    links[me] = coupling[0]
    for k in range(1, slabs):
        source = lax.rem(me + slabs - k, slabs)
        for part, ref in ((sub, gathered[2 * k - 2]), (1 - sub, gathered[2 * k - 1])):
            blocks[source, part] = ref[0]
            links[source, part] = ref[1]

    eye = (
        lax.broadcasted_iota(jnp.int32, (order, order), 0)
        == lax.broadcasted_iota(jnp.int32, (order, order), 1)
    ).astype(f32)
    zr, zi = pole[0], pole[1]

    def shifted(j):
        real, imag = pair(blocks, j)
        return 0.5 * (real + real.T) - zr * eye, 0.5 * (imag - imag.T) - zi * eye

    left = me < half

    def where_block(slot, j):
        from_left = left == (slot == 0)
        return from_left, jnp.where(from_left, j, slabs - 1 - j), jnp.where(from_left, j, slabs - j)

    def link(from_left, index):
        real, imag = pair(links, index)
        return (
            jnp.where(from_left, real, real.T),
            jnp.where(from_left, imag, -imag.T),
        )

    def put(ref, value, *index):
        ref[(*index, 0)] = value[0]
        ref[(*index, 1)] = value[1]

    def minus(a, b):
        return a[0] - b[0], a[1] - b[1]

    def level(j, _):
        def side(slot, _):
            from_left, own, joint = where_block(slot, j)

            @pl.when(j < half)
            def _():
                put(work, shifted(own))

            @pl.when((j > 0) & (j < half))
            def _():
                k = link(from_left, joint)
                inner = product(pair(inverses, slot, j - 1), k)
                put(work, minus(pair(work), product(adjoint(k), inner)))

            @pl.when(j == half)
            def _():
                k = link(jnp.logical_not(left), half)
                k = adjoint(k)
                inner = product(k, pair(inverses, 1, half - 1))
                put(work, minus(pair(pivot), product(inner, adjoint(k))))

            @pl.when(slot == 0)
            def _():
                pivot[...] = work[...]

            invert_into(work, inverses.at[slot, j])
            return 0

        return lax.fori_loop(0, jnp.where(j == half, 1, 2), side, 0)

    lax.fori_loop(0, half + 1, level, 0)
    greens[...] = inverses[0, half]
    place_in_chain = jnp.where(left, me, slabs - 1 - me)

    def outward(step, _):
        j = half - 1 - step
        _, _, joint = where_block(0, j)
        k = link(left, joint)
        inverse = pair(inverses, 0, j - 1)
        out = product(inverse, k)
        back = product(adjoint(k), inverse)
        update = product(product(out, pair(greens)), back)
        put(greens, (inverse[0] + update[0], inverse[1] + update[1]))
        return 0

    lax.fori_loop(0, half - 1 - place_in_chain, outward, 0)

    gr, gi = pair(greens)
    wr, wi = pole[2], pole[3]
    rows = order // poles
    for slot, (ur, ui) in enumerate(((wr, wi), (wr * zr - wi * zi, wr * zi + wi * zr))):
        real, imag = ur * gr - ui * gi, ur * gi + ui * gr
        put(work, (0.5 * (imag + imag.T), 0.5 * (real.T - real)))
        for k in range(poles):
            start = pl.multiple_of((mine ^ k) * rows, rows)
            for part in range(2):
                outs[k][slot, part] = work[part, pl.ds(start, rows), :]


def shards(slabs, poles, onsite, coupling, pole_real, pole_imag, pole_weight):
    order = onsite.shape[-1]
    me, sub = lax.axis_index("slab"), lax.axis_index("sub")
    mine = lax.axis_index(("pole", "sub"))
    halves = jnp.stack(
        [
            lax.dynamic_index_in_dim(onsite[0], sub, 0, False),
            lax.dynamic_index_in_dim(coupling[0], sub, 0, False),
        ]
    )
    gathered = []
    for k in range(1, slabs):
        got = lax.ppermute(halves, "slab", [(i, (i + k) % slabs) for i in range(slabs)])
        gathered += [got, lax.ppermute(got, "sub", [(0, 1), (1, 0)])]
    place = jnp.stack([me, mine, sub]).astype(jnp.int32)
    pole = jnp.concatenate([pole_real, pole_imag, pole_weight[0]])
    vmem = pl.BlockSpec(memory_space=pltpu.VMEM)
    smem = pl.BlockSpec(memory_space=pltpu.SMEM)
    half = slabs // 2
    pieces = pl.pallas_call(
        functools.partial(kernel, slabs, poles),
        out_shape=[jax.ShapeDtypeStruct((2, 2, order // poles, order), f32)] * poles,
        in_specs=[smem, smem] + [vmem] * (2 + len(gathered)),
        out_specs=[vmem] * poles,
        scratch_shapes=[
            pltpu.VMEM((slabs, 2, order, order), f32),
            pltpu.VMEM((slabs, 2, order, order), f32),
            pltpu.VMEM((2, order, order), f32),
            pltpu.VMEM((2, half + 1, 2, order, order), f32),
            pltpu.VMEM((2, order, order), f32),
            pltpu.VMEM((2, order, order), f32),
        ],
        compiler_params=pltpu.CompilerParams(vmem_limit_bytes=40 << 20),
    )(place, pole, onsite, coupling, *gathered)
    total = pieces[0]
    for k in range(1, poles):
        total = total + lax.ppermute(pieces[k], ("pole", "sub"), [(i, i ^ k) for i in range(poles)])
    return total[0][None], total[1][None]


def solution(mesh):
    in_specs = (
        P(("groups", "slab"), None, None, None),
        P(("groups", "slab"), None, None, None),
        P(("pole", "sub")),
        P(("pole", "sub")),
        P(("pole", "sub"), None),
    )
    out_specs = (
        P(("groups", "slab"), None, ("pole", "sub"), None),
        P(("groups", "slab"), None, ("pole", "sub"), None),
    )
    body = functools.partial(shards, mesh.shape["slab"], mesh.shape["pole"] * mesh.shape["sub"])
    return jax.shard_map(body, mesh=mesh, in_specs=in_specs, out_specs=out_specs, check_vma=False)
```

profile of v0, /device:TPU:0, one launch (start us, length us, event | category | flops | bytes accessed | tf_op | source)
XLA Modules:
  0.0 69.9 jit_solution(10775593193332837360)
XLA Ops:
  0.6 0.9 %dynamic-slice_bitcast_fusion = (f32[1,128,128]{2,1,0:T(8,128)S(1)}, f32[1,128,128]{2,1,0:T(8,128)S(1)}) fusion(f32[1,2,128,128]{3,2,1,0:T(8,128)} %coupling.1, s32[]{:T(128)S(6)} %select_n.5, f32[1,2,128,128]{3,2,1,0:T(8,128)} %onsite.1), kind=kLoop, calls=%fused_computation.2 | loop fusion | bytes 262148 | tf_op jit(solution)/shard_map/jit(dynamic_index_in_dim)/dynamic_slice | solution.py:201
  1.5 0.0 copy-start
  1.5 0.0 copy-start.1
  1.6 5.1 %collective-permute-start.4 = (f32[2,128,128]{2,1,0:T(8,128)S(1)}, f32[2,128,128]{2,1,0:T(8,128)S(1)}, u32[]{:S(2)}, u32[]{:S(2)}) collective-permute-start(f32[2,128,128]{2,1,0:T(8,128)S(1)} %pad_maximum_fusion), channel_id=1, source_target_pairs={{0,12},{4,0},{8,4},{12,8},{1,13},{5,1},{9,5},{13,9},{2,14},{6,2},{... | collective-permute-start | bytes 393224 | tf_op jit(solution)/shard_map/ppermute | solution.py:206
  6.7 0.0 collective-permute-start.2
  6.7 1.0 %collective-permute-start = (f32[2,128,128]{2,1,0:T(8,128)S(1)}, f32[2,128,128]{2,1,0:T(8,128)S(1)}, u32[]{:S(2)}, u32[]{:S(2)}) collective-permute-start(f32[2,128,128]{2,1,0:T(8,128)S(1)} %pad_maximum_fusion), channel_id=1, source_target_pairs={{0,4},{4,8},{8,12},{12,0},{1,5},{5,9},{9,13},{13,1},{2,6},{6,10},{... | collective-permute-start | bytes 393224 | tf_op jit(solution)/shard_map/ppermute | solution.py:206
  7.7 2.9 %collective-permute-done.4.refs_4_ = f32[2,128,128]{2,1,0:T(8,128)S(1)} collective-permute-done((f32[2,128,128]{2,1,0:T(8,128)S(1)}, f32[2,128,128]{2,1,0:T(8,128)S(1)}, u32[]{:S(2)}, u32[]{:S(2)}) %collective-permute-start.4) | collective-permute-done | bytes 131104 | tf_op jit(solution)/shard_map/ppermute | solution.py:206
  10.6 0.0 collective-permute-start.5
  10.6 7.3 %collective-permute-done.2.refs_2_ = f32[2,128,128]{2,1,0:T(8,128)S(1)} collective-permute-done((f32[2,128,128]{2,1,0:T(8,128)S(1)}, f32[2,128,128]{2,1,0:T(8,128)S(1)}, u32[]{:S(2)}, u32[]{:S(2)}) %collective-permute-start.2) | collective-permute-done | bytes 131104 | tf_op jit(solution)/shard_map/ppermute | solution.py:206
  17.9 0.0 collective-permute-start.3
  17.9 0.5 collective-permute-start.1
  18.4 0.1 pad_add_fusion.place
  19.8 0.0 copy-start.2
  19.8 0.6 copy-done.2
  20.4 0.1 pad_maximum_fusion.1.pole
  20.5 0.0 collective-permute-done.1.refs_1_
  20.5 43.1 %shard_map.68 = (f32[2,2,32,128]{3,2,1,0:T(8,128)S(1)}, f32[2,2,32,128]{3,2,1,0:T(8,128)S(1)}, f32[2,2,32,128]{3,2,1,0:T(8,128)S(1)}, f32[2,2,32,128]{3,2,1,0:T(8,128)S(1)}) custom-call(s32[3]{0:T(128)S(1)} %pad_add_fusion.place, f32[4]{0:T(128)S(1)} %pad_maximum_fusion.1.pole, f32[1,2,128,128]{3,2,1,0:T(8,128)S(1)} %copy-done, ...), custom_call_target="tpu_custom_call" | custom-call | tf_op jit(solution)/shard_map/pallas_call | solution.py:213
  63.6 0.1 collective-permute-start.6
  63.7 1.6 %collective-permute-start.7 = (f32[2,2,32,128]{3,2,1,0:T(8,128)S(1)}, f32[2,2,32,128]{3,2,1,0:T(8,128)S(1)}, u32[]{:S(2)}, u32[]{:S(2)}) collective-permute-start(f32[2,2,32,128]{3,2,1,0:T(8,128)S(1)} %get-tuple-element.8), channel_id=1, source_target_pairs={{0,2},{1,3},{2,0},{3,1},{4,6},{5,7},{6,4},{7,5},{8,10},{9,11},{10,... | collective-permute-start | bytes 196616 | tf_op jit(solution)/shard_map/ppermute | solution.py:230
  65.2 0.3 collective-permute-start.8
  65.5 0.0 collective-permute-done.6
  65.5 2.6 %collective-permute-done.7 = f32[2,2,32,128]{3,2,1,0:T(8,128)S(1)} collective-permute-done((f32[2,2,32,128]{3,2,1,0:T(8,128)S(1)}, f32[2,2,32,128]{3,2,1,0:T(8,128)S(1)}, u32[]{:S(2)}, u32[]{:S(2)}) %collective-permute-start.7) | collective-permute-done | bytes 65568 | tf_op jit(solution)/shard_map/ppermute | solution.py:230
  68.2 1.1 %collective-permute-done.8 = f32[2,2,32,128]{3,2,1,0:T(8,128)S(1)} collective-permute-done((f32[2,2,32,128]{3,2,1,0:T(8,128)S(1)}, f32[2,2,32,128]{3,2,1,0:T(8,128)S(1)}, u32[]{:S(2)}, u32[]{:S(2)}) %collective-permute-start.8) | collective-permute-done | bytes 65568 | tf_op jit(solution)/shard_map/ppermute | solution.py:230
  69.3 0.6 fusion
  (7 shorter events, 0.0 us)
Async XLA Ops:
  1.5 19.0 %copy-start = (f32[1,2,128,128]{3,2,1,0:T(8,128)S(1)}, f32[1,2,128,128]{3,2,1,0:T(8,128)}, u32[]{:S(2)}) copy-start(f32[1,2,128,128]{3,2,1,0:T(8,128)} %onsite.1) | copy-start | bytes 393220
  1.5 19.0 %copy-start.1 = (f32[1,2,128,128]{3,2,1,0:T(8,128)S(1)}, f32[1,2,128,128]{3,2,1,0:T(8,128)}, u32[]{:S(2)}) copy-start(f32[1,2,128,128]{3,2,1,0:T(8,128)} %coupling.1) | copy-start | bytes 393220
  1.6 9.0 %collective-permute-start.4 = (f32[2,128,128]{2,1,0:T(8,128)S(1)}, f32[2,128,128]{2,1,0:T(8,128)S(1)}, u32[]{:S(2)}, u32[]{:S(2)}) collective-permute-start(f32[2,128,128]{2,1,0:T(8,128)S(1)} %pad_maximum_fusion), channel_id=1, source_target_pairs={{0,12},{4,0},{8,4},{12,8},{1,13},{5,1},{9,5},{13,9},{2,14},{6,2},{... | collective-permute-start | bytes 393224 | tf_op jit(solution)/shard_map/ppermute | solution.py:206
  6.7 11.2 %collective-permute-start.2 = (f32[2,128,128]{2,1,0:T(8,128)S(1)}, f32[2,128,128]{2,1,0:T(8,128)S(1)}, u32[]{:S(2)}, u32[]{:S(2)}) collective-permute-start(f32[2,128,128]{2,1,0:T(8,128)S(1)} %pad_maximum_fusion), channel_id=1, source_target_pairs={{0,8},{4,12},{8,0},{12,4},{1,9},{5,13},{9,1},{13,5},{2,10},{6,14},... | collective-permute-start | bytes 393224 | tf_op jit(solution)/shard_map/ppermute | solution.py:206
  6.7 11.2 %collective-permute-start = (f32[2,128,128]{2,1,0:T(8,128)S(1)}, f32[2,128,128]{2,1,0:T(8,128)S(1)}, u32[]{:S(2)}, u32[]{:S(2)}) collective-permute-start(f32[2,128,128]{2,1,0:T(8,128)S(1)} %pad_maximum_fusion), channel_id=1, source_target_pairs={{0,4},{4,8},{8,12},{12,0},{1,5},{5,9},{9,13},{13,1},{2,6},{6,10},{... | collective-permute-start | bytes 393224 | tf_op jit(solution)/shard_map/ppermute | solution.py:206
  10.6 9.9 %collective-permute-start.5 = (f32[2,128,128]{2,1,0:T(8,128)S(1)}, f32[2,128,128]{2,1,0:T(8,128)S(1)}, u32[]{:S(2)}, u32[]{:S(2)}) collective-permute-start(f32[2,128,128]{2,1,0:T(8,128)S(1)} %collective-permute-done.4.refs_4_), channel_id=1, source_target_pairs={{0,1},{1,0},{2,3},{3,2},{4,5},{5,4},{6,7},{7,6},{8,9},{9,8},{10,11... | collective-permute-start | bytes 393224 | tf_op jit(solution)/shard_map/ppermute | solution.py:207
  17.9 2.6 %collective-permute-start.3 = (f32[2,128,128]{2,1,0:T(8,128)S(1)}, f32[2,128,128]{2,1,0:T(8,128)S(1)}, u32[]{:S(2)}, u32[]{:S(2)}) collective-permute-start(f32[2,128,128]{2,1,0:T(8,128)S(1)} %collective-permute-done.2.refs_2_), channel_id=1, source_target_pairs={{0,1},{1,0},{2,3},{3,2},{4,5},{5,4},{6,7},{7,6},{8,9},{9,8},{10,11... | collective-permute-start | bytes 393224 | tf_op jit(solution)/shard_map/ppermute | solution.py:207
  17.9 2.6 %collective-permute-start.1 = (f32[2,128,128]{2,1,0:T(8,128)S(1)}, f32[2,128,128]{2,1,0:T(8,128)S(1)}, u32[]{:S(2)}, u32[]{:S(2)}) collective-permute-start(f32[2,128,128]{2,1,0:T(8,128)S(1)} %collective-permute-done.refs_0_), channel_id=1, source_target_pairs={{0,1},{1,0},{2,3},{3,2},{4,5},{5,4},{6,7},{7,6},{8,9},{9,8},{10,11... | collective-permute-start | bytes 393224 | tf_op jit(solution)/shard_map/ppermute | solution.py:207
  19.8 0.7 copy-start.2
  63.6 1.9 %collective-permute-start.6 = (f32[2,2,32,128]{3,2,1,0:T(8,128)S(1)}, f32[2,2,32,128]{3,2,1,0:T(8,128)S(1)}, u32[]{:S(2)}, u32[]{:S(2)}) collective-permute-start(f32[2,2,32,128]{3,2,1,0:T(8,128)S(1)} %get-tuple-element.7), channel_id=1, source_target_pairs={{0,1},{1,0},{2,3},{3,2},{4,5},{5,4},{6,7},{7,6},{8,9},{9,8},{10,11... | collective-permute-start | bytes 196616 | tf_op jit(solution)/shard_map/ppermute | solution.py:230
  63.7 4.5 %collective-permute-start.7 = (f32[2,2,32,128]{3,2,1,0:T(8,128)S(1)}, f32[2,2,32,128]{3,2,1,0:T(8,128)S(1)}, u32[]{:S(2)}, u32[]{:S(2)}) collective-permute-start(f32[2,2,32,128]{3,2,1,0:T(8,128)S(1)} %get-tuple-element.8), channel_id=1, source_target_pairs={{0,2},{1,3},{2,0},{3,1},{4,6},{5,7},{6,4},{7,5},{8,10},{9,11},{10,... | collective-permute-start | bytes 196616 | tf_op jit(solution)/shard_map/ppermute | solution.py:230
  65.2 4.0 %collective-permute-start.8 = (f32[2,2,32,128]{3,2,1,0:T(8,128)S(1)}, f32[2,2,32,128]{3,2,1,0:T(8,128)S(1)}, u32[]{:S(2)}, u32[]{:S(2)}) collective-permute-start(f32[2,2,32,128]{3,2,1,0:T(8,128)S(1)} %get-tuple-element.9), channel_id=1, source_target_pairs={{0,3},{1,2},{2,1},{3,0},{4,7},{5,6},{6,5},{7,4},{8,11},{9,10},{10,... | collective-permute-start | bytes 196616 | tf_op jit(solution)/shard_map/ppermute | solution.py:230
where the time goes:
time: 70.1 us; the launch traced here: 69.9 us
  Pallas kernels  43.1 us (61%)
  waiting for transfers between devices  13.9 us (20%)
  starting transfers between devices  8.56 us (12%)
  local copies, waits for them, and re-layouts  2.18 us (3%)
  between operations  2.02 us (3%)
    pallas_call x1, Pallas kernels, shards(): pl.pallas_call(functools.partial(kernel, slabs, poles), out_shape=[jax.Sh...  43.1 us
    ppermute x3, waiting for transfers between devices, shards(): lax.ppermute(halves, 'slab', [(i, (i + k) % slabs) for i in range(slabs)])  10.2 us
    ppermute x3, starting transfers between devices, shards(): lax.ppermute(halves, 'slab', [(i, (i + k) % slabs) for i in range(slabs)])  6.11 us
    ppermute x3, waiting for transfers between devices, shards(): lax.ppermute(pieces[k], ('pole', 'sub'), [(i, i ^ k) for i in range(poles)])  3.74 us
    ppermute x3, starting transfers between devices, shards(): lax.ppermute(pieces[k], ('pole', 'sub'), [(i, i ^ k) for i in range(poles)])  1.93 us
  transfers between devices with their start and end apart: 9, of which 4 were waited for; matrix products, arithmetic and copies ran while one was open for 0% of the time, Pallas kernels for 0%

commit v1 on v0

v1 whole, which is shorter than its diff:
```python
import functools

import jax
import jax.numpy as jnp
from jax import lax
from jax.experimental import pallas as pl
from jax.experimental.pallas import tpu as pltpu
from jax.sharding import PartitionSpec as P

ROWS = 8
PANEL = 2 * ROWS
f32, bf16 = jnp.float32, jnp.bfloat16
PARTS = ((0, 0), (0, 1), (1, 0), (1, 1), (0, 2), (2, 0))


def row_of(tile, k):
    return jnp.broadcast_to(tile[k : k + 1, :], tile.shape)


def lane_of(tile, k):
    where = jnp.full(tile.shape, k, jnp.int32)
    return jnp.take_along_axis(tile, where, axis=1, mode="promise_in_bounds")


def sweep(tiles, first, lane, subl):
    tiles = list(tiles)
    columns = [[(lane_of(xr, first + j), lane_of(xi, first + j)) for j in range(ROWS)] for xr, xi in tiles]
    for k in range(ROWS):
        in_row, in_lane = (subl == k).astype(f32), (lane == first + k).astype(f32)
        for s, cols in enumerate(columns):
            xr, xi = tiles[s]
            tr, ti = cols[k]
            dr, di = row_of(tr, k), row_of(ti, k)
            scale = 1.0 / (dr * dr + di * di)
            rr, ri = dr * scale, -di * scale
            cr = tr - in_row
            cr, ci = cr * rr - ti * ri, cr * ri + ti * rr
            for j in range(k + 1, ROWS):
                ar, ai = row_of(cols[j][0], k), row_of(cols[j][1], k)
                cols[j] = (cols[j][0] - (cr * ar - ci * ai), cols[j][1] - (cr * ai + ci * ar))
            ar, ai = row_of(xr, k) + in_lane, row_of(xi, k)
            tiles[s] = (xr - (cr * ar - ci * ai), xi - (cr * ai + ci * ar))
    return tiles


def follow(tile, swept, first, inside):
    ar, ai = tile
    nr, ni = jnp.where(inside, 0.0, ar), jnp.where(inside, 0.0, ai)
    pr = pi = None
    for k in range(ROWS):
        cr, ci = lane_of(ar, first + k), lane_of(ai, first + k)
        ur, ui = row_of(swept[0], k), row_of(swept[1], k)
        tr, ti = cr * ur - ci * ui, cr * ui + ci * ur
        if k % 2 == 0:
            nr, ni = nr - tr, ni - ti
        else:
            pr, pi = (tr, ti) if pr is None else (pr + tr, pi + ti)
    return nr - pr, ni - pi


def split(x):
    parts = [x.astype(bf16)]
    for _ in range(2):
        x = x - parts[-1].astype(f32)
        parts.append(x.astype(bf16))
    return parts


def times(left, right):
    columns = right[0].shape[1]
    lr, li = split(left[0]), split(left[1])
    rr, ri, rn = split(right[0]), split(right[1]), split(-right[1])
    lhs = jnp.concatenate([part for a, _ in PARTS for part in (lr[a], li[a])], axis=1)
    rhs = jnp.concatenate(
        [
            jnp.concatenate(pair, axis=1)
            for _, b in PARTS
            for pair in ((rr[b], ri[b]), (rn[b], rr[b]))
        ],
        axis=0,
    )
    whole = lax.dot_general(lhs, rhs, (((1,), (0,)), ((), ())), preferred_element_type=f32)
    return whole[:, :columns], whole[:, columns:]


def others_follow(tiles, panel, place):
    order = tiles[0][0].shape[1]

    def padded(part):
        rows = jnp.concatenate(part, axis=0)
        above = [jnp.zeros((PANEL * place, order), f32)] if place else []
        below = order - PANEL * (place + 1)
        return jnp.concatenate(above + [rows] + ([jnp.zeros((below, order), f32)] if below else []), axis=0)

    left = [jnp.concatenate(part, axis=0) for part in zip(*tiles)]
    right = [padded(part) for part in zip(*panel)]
    real, imag = times(left, right)
    return [(real[ROWS * t : ROWS * t + ROWS], imag[ROWS * t : ROWS * t + ROWS]) for t in range(len(tiles))]


def invert(systems):
    order = systems[0][0][0].shape[1]
    count, panels = order // ROWS, order // PANEL
    lane = lax.broadcasted_iota(jnp.int32, (ROWS, order), 1)
    subl = lax.broadcasted_iota(jnp.int32, (ROWS, order), 0)
    systems = [list(tiles) for tiles in systems]
    for place in range(panels):
        a, b = 2 * place, 2 * place + 1
        in_a = (lane >= ROWS * a) & (lane < ROWS * a + ROWS)
        in_b = (lane >= ROWS * b) & (lane < ROWS * b + ROWS)
        last = place == panels - 1
        ahead = (b + 1) % count
        first = sweep([tiles[a] for tiles in systems], ROWS * a, lane, subl)
        second = [follow(tiles[b], x, ROWS * a, in_a) for tiles, x in zip(systems, first)]
        if not last:
            soon = [follow(tiles[ahead], x, ROWS * a, in_a) for tiles, x in zip(systems, first)]
        second = sweep(second, ROWS * b, lane, subl)
        if not last:
            soon = [follow(tile, x, ROWS * b, in_b) for tile, x in zip(soon, second)]
        first = [follow(tile, x, ROWS * b, in_b) for tile, x in zip(first, second)]
        rest = [i for i in range(count) if i not in (a, b) and (last or i != ahead)]
        rest.sort(key=lambda i: (i - ahead) % count)
        for s, tiles in enumerate(systems):
            taken = rest + rest[-1:] if len(rest) % 2 else rest
            delta = others_follow([tiles[i] for i in taken], [first[s], second[s]], place)
            for (dr, di), i in zip(delta, rest):
                tiles[i] = (
                    jnp.where(in_a | in_b, 0.0, tiles[i][0]) - dr,
                    jnp.where(in_a | in_b, 0.0, tiles[i][1]) - di,
                )
            tiles[a], tiles[b] = first[s], second[s]
            if not last:
                tiles[ahead] = soon[s]
    return systems


def to_tiles(value):
    count = value[0].shape[0] // ROWS
    return [tuple(part[ROWS * i : ROWS * i + ROWS] for part in value) for i in range(count)]


def from_tiles(tiles):
    return tuple(jnp.concatenate(part, axis=0) for part in zip(*tiles))


def inverses_of(*values):
    return [from_tiles(tiles) for tiles in invert([to_tiles(value) for value in values])]


def adjoint(a):
    return a[0].T, -a[1].T


def plus(a, b):
    return a[0] + b[0], a[1] + b[1]


def minus(a, b):
    return a[0] - b[0], a[1] - b[1]


def get(ref, *index):
    return ref[(*index, 0)], ref[(*index, 1)]


def put(ref, value, *index):
    ref[(*index, 0)], ref[(*index, 1)] = value


def square(order):
    rows = lax.broadcasted_iota(jnp.int32, (order, order), 0)
    columns = lax.broadcasted_iota(jnp.int32, (order, order), 1)
    return rows, columns


def pack(onsite):
    real, imag = 0.5 * (onsite[0] + onsite[0].T), 0.5 * (onsite[1] - onsite[1].T)
    rows, columns = square(real.shape[0])
    return jnp.where(rows <= columns, real, imag)


def unpack_shifted(packed, zr, zi):
    rows, columns = square(packed.shape[0])
    turned = packed.T
    real = jnp.where(rows <= columns, packed, turned)
    imag = jnp.where(rows > columns, packed, -turned)
    return jnp.where(rows == columns, real - zr, real), jnp.where(rows == columns, -zi, imag)


def prepare(place, onsite, coupling, packed, half):
    packed[...] = pack((onsite[0, 0], onsite[0, 1]))
    half[...] = coupling[0, place[2]]


def start_chain(slabs, place, pole, *refs):
    blocks, out, chosen = refs[: slabs // 2], refs[-2], refs[-1]
    me = place[0]
    end = jnp.where(me < slabs // 2, 0, slabs - 1)
    for k, ref in enumerate(blocks):

        @pl.when((me ^ end) == k)
        def _(ref=ref):
            chosen[...] = ref[...]

    (inverse,) = inverses_of(unpack_shifted(chosen[...], pole[0], pole[1]))
    put(out, inverse)


def finish(slabs, poles, place, pole, start, coupling, *refs):
    packed, refs = refs[:slabs], refs[slabs:]
    halves, refs = refs[: 2 * (slabs - 1)], refs[2 * (slabs - 1) :]
    outs, (blocks, links, outward, inward, own, far, work, greens) = refs[:poles], refs[poles:]
    me, mine, sub = place[0], place[1], place[2]
    middle = slabs // 2
    order = start.shape[-1]
    for k in range(slabs):
        blocks[me ^ k] = packed[k][...]
    links[me] = coupling[0]
    for k in range(1, slabs):
        links[me ^ k, sub] = halves[2 * k - 2][...]
        links[me ^ k, 1 - sub] = halves[2 * k - 1][...]
    zr, zi = pole[0], pole[1]
    left = me < middle

    def block(from_left, j):
        return unpack_shifted(blocks[jnp.where(from_left, j, slabs - 1 - j)], zr, zi)

    def link(from_left, j):
        real, imag = get(links, jnp.where(from_left, j, slabs - j))
        return jnp.where(from_left, real, real.T), jnp.where(from_left, imag, -imag.T)

    def reduced(from_left, j, inverse):
        k = link(from_left, j)
        out, back = times(inverse, k), adjoint(k)
        return times(back, out), out, times(back, inverse)

    put(own, (start[0], start[1]), 0)
    right = jnp.logical_not(left)

    def level(j, far_pivot):
        taken, out, back = reduced(left, j, get(own, j - 1))
        put(outward, out, j)
        put(inward, back, j)
        here, there = inverses_of(minus(block(left, j), taken), far_pivot())
        put(own, here, j)
        put(far, there, j - 1)

    def far_pivot(j):
        return minus(block(right, j), reduced(right, j, get(far, j - 1))[0])

    level(1, lambda: block(right, 0))

    def next_level(j, _):
        level(j, lambda: far_pivot(j - 1))
        return 0

    lax.fori_loop(2, middle, next_level, 0)
    taken, out, back = reduced(left, middle, get(own, middle - 1))
    put(outward, out, middle)
    put(inward, back, middle)
    (green,) = inverses_of(minus(far_pivot(middle - 1), taken))
    put(greens, green)

    def retreat(step, _):
        j = middle - step
        update = times(times(get(outward, j), get(greens)), get(inward, j))
        put(greens, plus(get(own, j - 1), update))
        return 0

    lax.fori_loop(0, middle - jnp.where(left, me, slabs - 1 - me), retreat, 0)
    gr, gi = get(greens)
    wr, wi = pole[2], pole[3]
    rows = order // poles
    for slot, (ur, ui) in enumerate(((wr, wi), (wr * zr - wi * zi, wr * zi + wi * zr))):
        real, imag = ur * gr - ui * gi, ur * gi + ui * gr
        put(work, (0.5 * (imag + imag.T), 0.5 * (real.T - real)))
        for k in range(poles):
            begin = pl.multiple_of((mine ^ k) * rows, rows)
            for part in range(2):
                outs[k][slot, part] = work[part, pl.ds(begin, rows), :]


def shards(slabs, poles, onsite, coupling, pole_real, pole_imag, pole_weight):
    order = onsite.shape[-1]
    middle = slabs // 2
    place = jnp.stack(
        [lax.axis_index("slab"), lax.axis_index(("pole", "sub")), lax.axis_index("sub")]
    ).astype(jnp.int32)
    pole = jnp.concatenate([pole_real, pole_imag, pole_weight[0]])
    vmem = pl.BlockSpec(memory_space=pltpu.VMEM)
    smem = pl.BlockSpec(memory_space=pltpu.SMEM)
    params = pltpu.CompilerParams(vmem_limit_bytes=40 << 20)
    square_of = jax.ShapeDtypeStruct((order, order), f32)
    complex_of = jax.ShapeDtypeStruct((2, order, order), f32)

    def scratch(*lead):
        return pltpu.VMEM((*lead, order, order), f32)

    packed, half = pl.pallas_call(
        prepare,
        out_shape=[square_of, square_of],
        in_specs=[smem, vmem, vmem],
        out_specs=[vmem, vmem],
        compiler_params=params,
    )(place, onsite, coupling)

    def swap(value, k):
        return lax.ppermute(value, "slab", [(i, i ^ k) for i in range(slabs)])

    blocks = [packed] + [swap(packed, k) for k in range(1, slabs)]
    halves = []
    for k in range(1, slabs):
        got = swap(half, k)
        halves += [got, lax.ppermute(got, "sub", [(0, 1), (1, 0)])]
    start = pl.pallas_call(
        functools.partial(start_chain, slabs),
        out_shape=complex_of,
        in_specs=[smem, smem] + [vmem] * middle,
        out_specs=vmem,
        scratch_shapes=[scratch()],
        compiler_params=params,
        cost_estimate=pl.CostEstimate(flops=2 * 10**9, bytes_accessed=10**6, transcendentals=0),
    )(place, pole, *blocks[:middle])
    pieces = pl.pallas_call(
        functools.partial(finish, slabs, poles),
        out_shape=[jax.ShapeDtypeStruct((2, 2, order // poles, order), f32)] * poles,
        in_specs=[smem, smem] + [vmem] * (2 + slabs + len(halves)),
        out_specs=[vmem] * poles,
        scratch_shapes=[
            scratch(slabs),
            scratch(slabs, 2),
            scratch(middle + 1, 2),
            scratch(middle + 1, 2),
            scratch(middle, 2),
            scratch(middle, 2),
            scratch(2),
            scratch(2),
        ],
        compiler_params=params,
    )(place, pole, start, coupling, *blocks, *halves)
    total = pieces[0]
    for k in range(1, poles):
        total = total + lax.ppermute(pieces[k], ("pole", "sub"), [(i, i ^ k) for i in range(poles)])
    return total[0][None], total[1][None]


def solution(mesh):
    in_specs = (
        P(("groups", "slab"), None, None, None),
        P(("groups", "slab"), None, None, None),
        P(("pole", "sub")),
        P(("pole", "sub")),
        P(("pole", "sub"), None),
    )
    out_specs = (
        P(("groups", "slab"), None, ("pole", "sub"), None),
        P(("groups", "slab"), None, ("pole", "sub"), None),
    )
    body = functools.partial(shards, mesh.shape["slab"], mesh.shape["pole"] * mesh.shape["sub"])
    return jax.shard_map(body, mesh=mesh, in_specs=in_specs, out_specs=out_specs, check_vma=False)
```

time: 70.1 us -> 44.7 us (0.64)
  Pallas kernels: 43.1 us -> 21 us
  waiting for transfers between devices: 13.9 us -> 5.42 us
  starting transfers between devices: 8.56 us -> 12.8 us
  local copies, waits for them, and re-layouts: 2.18 us -> 3.09 us
    pallas_call x1 -> x3, Pallas kernels: 43.1 us -> 21 us  [the longest x1 14.8 us: shards(): pl.pallas_call(functools.partial(finish, slabs, poles), out_shape=[jax.Sh...]
    ppermute x6 -> x9, waiting for transfers between devices: 10.2 us -> 1.06 us  [the longest x6 1.05 us: swap(): return lax.ppermute(value, 'slab', [(i, i ^ k) for i in range(slabs)])]
    ppermute x6 -> x9, starting transfers between devices: 6.63 us -> 10.7 us  [the longest x6 10.2 us: swap(): return lax.ppermute(value, 'slab', [(i, i ^ k) for i in range(slabs)])]
    unnamed x6 -> x8, local copies, waits for them, and re-layouts: 0.66 us -> 2.46 us
    dynamic_slice x1 -> x0, local copies, waits for them, and re-layouts: 0.89 us -> none  [shards(): lax.dynamic_index_in_dim(coupling[0], sub, 0, False)]
  transfers between devices with their start and end apart: 9 -> 12, of which waited for: 4 -> 3; matrix products, arithmetic and copies ran while one was open for 0% -> 0% of each run, Pallas kernels for 0% -> 13%
where the time goes in v1:
time: 44.7 us; the launch traced here: 44.5 us
  Pallas kernels  21 us (47%)
  starting transfers between devices  12.8 us (29%)
  waiting for transfers between devices  5.42 us (12%)
  local copies, waits for them, and re-layouts  3.09 us (7%)
  between operations  2.03 us (5%)
    pallas_call x1, Pallas kernels, shards(): pl.pallas_call(functools.partial(finish, slabs, poles), out_shape=[jax.Sh...  14.8 us
    ppermute x6, starting transfers between devices, swap(): return lax.ppermute(value, 'slab', [(i, i ^ k) for i in range(slabs)])  10.2 us
    pallas_call x1, Pallas kernels, shards(): pl.pallas_call(functools.partial(start_chain, slabs), out_shape=complex_o...  5.6 us
    ppermute x3, waiting for transfers between devices, shards(): lax.ppermute(pieces[k], ('pole', 'sub'), [(i, i ^ k) for i in range(poles)])  4.37 us
    unnamed x8, local copies, waits for them, and re-layouts  2.46 us
    ppermute x3, starting transfers between devices, shards(): lax.ppermute(pieces[k], ('pole', 'sub'), [(i, i ^ k) for i in range(poles)])  2.07 us
    ppermute x6, waiting for transfers between devices, swap(): return lax.ppermute(value, 'slab', [(i, i ^ k) for i in range(slabs)])  1.05 us
  transfers between devices with their start and end apart: 12, of which 3 were waited for; matrix products, arithmetic and copies ran while one was open for 0% of the time, Pallas kernels for 13%

profile of v1, /device:TPU:0, one launch (start us, length us, event | category | flops | bytes accessed | tf_op | source)
XLA Modules:
  0.0 44.5 jit_solution(7646879945191255031)
XLA Ops:
  0.6 0.1 pad_add_fusion.place
  0.7 0.9 %copy-done = f32[1,2,128,128]{3,2,1,0:T(8,128)S(1)} copy-done((f32[1,2,128,128]{3,2,1,0:T(8,128)S(1)}, f32[1,2,128,128]{3,2,1,0:T(8,128)}, u32[]{:S(2)}) %copy-start) | copy-done | bytes 131096
  1.6 0.9 %copy-done.2 = f32[1,2,128,128]{3,2,1,0:T(8,128)S(1)} copy-done((f32[1,2,128,128]{3,2,1,0:T(8,128)S(1)}, f32[1,2,128,128]{3,2,1,0:T(8,128)}, u32[]{:S(2)}) %copy-start.2) | copy-done | bytes 131096
  2.5 0.6 %shard_map.68 = (f32[128,128]{1,0:T(8,128)S(1)}, f32[128,128]{1,0:T(8,128)S(1)}) custom-call(s32[3]{0:T(128)S(1)} %pad_add_fusion.place, f32[1,2,128,128]{3,2,1,0:T(8,128)S(1)} %copy-done.2, f32[1,2,128,128]{3,2,1,0:T(8,128)S(1)} %copy-done), custom_call_target="tpu_custom_call" | custom-call | tf_op jit(solution)/shard_map/pallas_call | solution.py:299
  3.2 5.1 %collective-permute-start.7 = (f32[128,128]{1,0:T(8,128)S(1)}, f32[128,128]{1,0:T(8,128)S(1)}, u32[]{:S(2)}, u32[]{:S(2)}) collective-permute-start(f32[128,128]{1,0:T(8,128)S(1)} %get-tuple-element.9), channel_id=1, source_target_pairs={{0,12},{4,8},{8,4},{12,0},{1,13},{5,9},{9,5},{13,1},{2,14},{6,10},... | collective-permute-start | bytes 196616 | tf_op jit(solution)/shard_map/ppermute | solution.py:308
  8.3 0.0 collective-permute-start.5
  8.3 0.6 %collective-permute-start.3 = (f32[128,128]{1,0:T(8,128)S(1)}, f32[128,128]{1,0:T(8,128)S(1)}, u32[]{:S(2)}, u32[]{:S(2)}) collective-permute-start(f32[128,128]{1,0:T(8,128)S(1)} %get-tuple-element.9), channel_id=1, source_target_pairs={{0,4},{4,0},{8,12},{12,8},{1,5},{5,1},{9,13},{13,9},{2,6},{6,2},{1... | collective-permute-start | bytes 196616 | tf_op jit(solution)/shard_map/ppermute | solution.py:308
  8.9 3.7 %collective-permute-start.2 = (f32[128,128]{1,0:T(8,128)S(1)}, f32[128,128]{1,0:T(8,128)S(1)}, u32[]{:S(2)}, u32[]{:S(2)}) collective-permute-start(f32[128,128]{1,0:T(8,128)S(1)} %get-tuple-element.8.refs_0_), channel_id=1, source_target_pairs={{0,12},{4,8},{8,4},{12,0},{1,13},{5,9},{9,5},{13,1},{2,14},{6,10},... | collective-permute-start | bytes 196616 | tf_op jit(solution)/shard_map/ppermute | solution.py:308
  12.7 0.0 collective-permute-start
  14.0 0.0 copy-start.3
  14.0 0.6 %copy-done.3 = f32[1,2]{1,0:T(1,128)S(1)} copy-done((f32[1,2]{1,0:T(1,128)S(1)}, f32[1,2]{1,0:T(1,128)}, u32[]{:S(2)}) %copy-start.3) | copy-done | bytes 32
  14.6 0.1 pad_maximum_fusion.pole
  14.7 0.0 collective-permute-done.7.refs_8_
  14.7 0.7 %collective-permute-start.1 = (f32[128,128]{1,0:T(8,128)S(1)}, f32[128,128]{1,0:T(8,128)S(1)}, u32[]{:S(2)}, u32[]{:S(2)}) collective-permute-start(f32[128,128]{1,0:T(8,128)S(1)} %get-tuple-element.8.refs_0_), channel_id=1, source_target_pairs={{0,8},{4,12},{8,0},{12,4},{1,9},{5,13},{9,1},{13,5},{2,10},{6,14},... | collective-permute-start | bytes 196616 | tf_op jit(solution)/shard_map/ppermute | solution.py:308
  15.4 0.0 collective-permute-done.5.refs_6_
  15.4 0.5 %collective-permute-start.6 = (f32[128,128]{1,0:T(8,128)S(1)}, f32[128,128]{1,0:T(8,128)S(1)}, u32[]{:S(2)}, u32[]{:S(2)}) collective-permute-start(f32[128,128]{1,0:T(8,128)S(1)} %collective-permute-done.5.refs_6_), channel_id=1, source_target_pairs={{0,1},{1,0},{2,3},{3,2},{4,5},{5,4},{6,7},{7,6},{8,9},{9,8},{10,11... | collective-permute-start | bytes 196616 | tf_op jit(solution)/shard_map/ppermute | solution.py:314
  15.9 1.0 %collective-permute-done.refs_1_ = f32[128,128]{1,0:T(8,128)S(1)} collective-permute-done((f32[128,128]{1,0:T(8,128)S(1)}, f32[128,128]{1,0:T(8,128)S(1)}, u32[]{:S(2)}, u32[]{:S(2)}) %collective-permute-start) | collective-permute-done | bytes 65568 | tf_op jit(solution)/shard_map/ppermute | solution.py:308
  16.9 5.6 %shard_map.69.start = f32[2,128,128]{2,1,0:T(8,128)S(1)} custom-call(s32[3]{0:T(128)S(1)} %pad_add_fusion.place, f32[4]{0:T(128)S(1)} %pad_maximum_fusion.pole, f32[128,128]{1,0:T(8,128)S(1)} %get-tuple-element.8.refs_0_, f32[128,128]{1,0:T(8,128)S(1)} %collective-permute-done.refs_1_), custom_call_target="tpu_custom_call" | custom-call | flops 2000000000 | bytes 1000000 | tf_op jit(solution)/shard_map/pallas_call | solution.py:315
  22.6 14.8 %shard_map.70 = (f32[2,2,32,128]{3,2,1,0:T(8,128)S(1)}, f32[2,2,32,128]{3,2,1,0:T(8,128)S(1)}, f32[2,2,32,128]{3,2,1,0:T(8,128)S(1)}, f32[2,2,32,128]{3,2,1,0:T(8,128)S(1)}) custom-call(s32[3]{0:T(128)S(1)} %pad_add_fusion.place, f32[4]{0:T(128)S(1)} %pad_maximum_fusion.pole, f32[2,128,128]{2,1,0:T(8,128)S(1)} %shard_map.69.start, ...), custom_call_target="tpu_custom_call" | custom-call | tf_op jit(solution)/shard_map/pallas_call | solution.py:324
  37.4 0.6 %collective-permute-start.9 = (f32[2,2,32,128]{3,2,1,0:T(8,128)S(1)}, f32[2,2,32,128]{3,2,1,0:T(8,128)S(1)}, u32[]{:S(2)}, u32[]{:S(2)}) collective-permute-start(f32[2,2,32,128]{3,2,1,0:T(8,128)S(1)} %get-tuple-element.11), channel_id=1, source_target_pairs={{0,1},{1,0},{2,3},{3,2},{4,5},{5,4},{6,7},{7,6},{8,9},{9,8},{10,11... | collective-permute-start | bytes 196616 | tf_op jit(solution)/shard_map/ppermute | solution.py:343
  38.0 1.5 %collective-permute-start.10 = (f32[2,2,32,128]{3,2,1,0:T(8,128)S(1)}, f32[2,2,32,128]{3,2,1,0:T(8,128)S(1)}, u32[]{:S(2)}, u32[]{:S(2)}) collective-permute-start(f32[2,2,32,128]{3,2,1,0:T(8,128)S(1)} %get-tuple-element.12), channel_id=1, source_target_pairs={{0,2},{1,3},{2,0},{3,1},{4,6},{5,7},{6,4},{7,5},{8,10},{9,11},{10,... | collective-permute-start | bytes 196616 | tf_op jit(solution)/shard_map/ppermute | solution.py:343
  39.5 2.8 %collective-permute-done.10 = f32[2,2,32,128]{3,2,1,0:T(8,128)S(1)} collective-permute-done((f32[2,2,32,128]{3,2,1,0:T(8,128)S(1)}, f32[2,2,32,128]{3,2,1,0:T(8,128)S(1)}, u32[]{:S(2)}, u32[]{:S(2)}) %collective-permute-start.10) | collective-permute-done | bytes 65568 | tf_op jit(solution)/shard_map/ppermute | solution.py:343
  42.3 1.6 %collective-permute-done.11 = f32[2,2,32,128]{3,2,1,0:T(8,128)S(1)} collective-permute-done((f32[2,2,32,128]{3,2,1,0:T(8,128)S(1)}, f32[2,2,32,128]{3,2,1,0:T(8,128)S(1)}, u32[]{:S(2)}, u32[]{:S(2)}) %collective-permute-start.11) | collective-permute-done | bytes 65568 | tf_op jit(solution)/shard_map/ppermute | solution.py:343
  43.9 0.6 %fusion = (f32[1,2,32,128]{3,2,1,0:T(8,128)}, f32[1,2,32,128]{3,2,1,0:T(8,128)}) fusion(f32[2,2,32,128]{3,2,1,0:T(8,128)S(1)} %add_add_fusion), kind=kLoop, calls=%fused_computation.3 | loop fusion | bytes 131072 | tf_op jit(solution)/shard_map/slice | solution.py:344
  (15 shorter events, 0.1 us)
Async XLA Ops:
  0.7 0.9 %copy-start = (f32[1,2,128,128]{3,2,1,0:T(8,128)S(1)}, f32[1,2,128,128]{3,2,1,0:T(8,128)}, u32[]{:S(2)}) copy-start(f32[1,2,128,128]{3,2,1,0:T(8,128)} %coupling.3) | copy-start | bytes 393220
  1.6 0.9 %copy-start.2 = (f32[1,2,128,128]{3,2,1,0:T(8,128)S(1)}, f32[1,2,128,128]{3,2,1,0:T(8,128)}, u32[]{:S(2)}) copy-start(f32[1,2,128,128]{3,2,1,0:T(8,128)} %onsite.1) | copy-start | bytes 393220
  3.2 11.5 %collective-permute-start.7 = (f32[128,128]{1,0:T(8,128)S(1)}, f32[128,128]{1,0:T(8,128)S(1)}, u32[]{:S(2)}, u32[]{:S(2)}) collective-permute-start(f32[128,128]{1,0:T(8,128)S(1)} %get-tuple-element.9), channel_id=1, source_target_pairs={{0,12},{4,8},{8,4},{12,0},{1,13},{5,9},{9,5},{13,1},{2,14},{6,10},... | collective-permute-start | bytes 196616 | tf_op jit(solution)/shard_map/ppermute | solution.py:308
  8.3 7.1 %collective-permute-start.5 = (f32[128,128]{1,0:T(8,128)S(1)}, f32[128,128]{1,0:T(8,128)S(1)}, u32[]{:S(2)}, u32[]{:S(2)}) collective-permute-start(f32[128,128]{1,0:T(8,128)S(1)} %get-tuple-element.9), channel_id=1, source_target_pairs={{0,8},{4,12},{8,0},{12,4},{1,9},{5,13},{9,1},{13,5},{2,10},{6,14},... | collective-permute-start | bytes 196616 | tf_op jit(solution)/shard_map/ppermute | solution.py:308
  8.3 7.1 %collective-permute-start.3 = (f32[128,128]{1,0:T(8,128)S(1)}, f32[128,128]{1,0:T(8,128)S(1)}, u32[]{:S(2)}, u32[]{:S(2)}) collective-permute-start(f32[128,128]{1,0:T(8,128)S(1)} %get-tuple-element.9), channel_id=1, source_target_pairs={{0,4},{4,0},{8,12},{12,8},{1,5},{5,1},{9,13},{13,9},{2,6},{6,2},{1... | collective-permute-start | bytes 196616 | tf_op jit(solution)/shard_map/ppermute | solution.py:308
  8.9 13.6 %collective-permute-start.2 = (f32[128,128]{1,0:T(8,128)S(1)}, f32[128,128]{1,0:T(8,128)S(1)}, u32[]{:S(2)}, u32[]{:S(2)}) collective-permute-start(f32[128,128]{1,0:T(8,128)S(1)} %get-tuple-element.8.refs_0_), channel_id=1, source_target_pairs={{0,12},{4,8},{8,4},{12,0},{1,13},{5,9},{9,5},{13,1},{2,14},{6,10},... | collective-permute-start | bytes 196616 | tf_op jit(solution)/shard_map/ppermute | solution.py:308
  12.7 4.3 %collective-permute-start = (f32[128,128]{1,0:T(8,128)S(1)}, f32[128,128]{1,0:T(8,128)S(1)}, u32[]{:S(2)}, u32[]{:S(2)}) collective-permute-start(f32[128,128]{1,0:T(8,128)S(1)} %get-tuple-element.8.refs_0_), channel_id=1, source_target_pairs={{0,4},{4,0},{8,12},{12,8},{1,5},{5,1},{9,13},{13,9},{2,6},{6,2},{1... | collective-permute-start | bytes 196616 | tf_op jit(solution)/shard_map/ppermute | solution.py:308
  14.0 0.7 %copy-start.3 = (f32[1,2]{1,0:T(1,128)S(1)}, f32[1,2]{1,0:T(1,128)}, u32[]{:S(2)}) copy-start(f32[1,2]{1,0:T(1,128)} %param.9) | copy-start | bytes 28
  14.7 7.9 %copy-start.1 = (f32[1,2,128,128]{3,2,1,0:T(8,128)S(1)}, f32[1,2,128,128]{3,2,1,0:T(8,128)}, u32[]{:S(2)}) copy-start(f32[1,2,128,128]{3,2,1,0:T(8,128)} %coupling.3) | copy-start | bytes 393220
  14.7 7.8 %collective-permute-start.1 = (f32[128,128]{1,0:T(8,128)S(1)}, f32[128,128]{1,0:T(8,128)S(1)}, u32[]{:S(2)}, u32[]{:S(2)}) collective-permute-start(f32[128,128]{1,0:T(8,128)S(1)} %get-tuple-element.8.refs_0_), channel_id=1, source_target_pairs={{0,8},{4,12},{8,0},{12,4},{1,9},{5,13},{9,1},{13,5},{2,10},{6,14},... | collective-permute-start | bytes 196616 | tf_op jit(solution)/shard_map/ppermute | solution.py:308
  15.4 7.2 %collective-permute-start.8 = (f32[128,128]{1,0:T(8,128)S(1)}, f32[128,128]{1,0:T(8,128)S(1)}, u32[]{:S(2)}, u32[]{:S(2)}) collective-permute-start(f32[128,128]{1,0:T(8,128)S(1)} %collective-permute-done.7.refs_8_), channel_id=1, source_target_pairs={{0,1},{1,0},{2,3},{3,2},{4,5},{5,4},{6,7},{7,6},{8,9},{9,8},{10,11... | collective-permute-start | bytes 196616 | tf_op jit(solution)/shard_map/ppermute | solution.py:314
  15.4 7.2 %collective-permute-start.6 = (f32[128,128]{1,0:T(8,128)S(1)}, f32[128,128]{1,0:T(8,128)S(1)}, u32[]{:S(2)}, u32[]{:S(2)}) collective-permute-start(f32[128,128]{1,0:T(8,128)S(1)} %collective-permute-done.5.refs_6_), channel_id=1, source_target_pairs={{0,1},{1,0},{2,3},{3,2},{4,5},{5,4},{6,7},{7,6},{8,9},{9,8},{10,11... | collective-permute-start | bytes 196616 | tf_op jit(solution)/shard_map/ppermute | solution.py:314
  16.9 5.7 %collective-permute-start.4 = (f32[128,128]{1,0:T(8,128)S(1)}, f32[128,128]{1,0:T(8,128)S(1)}, u32[]{:S(2)}, u32[]{:S(2)}) collective-permute-start(f32[128,128]{1,0:T(8,128)S(1)} %collective-permute-done.3.refs_4_), channel_id=1, source_target_pairs={{0,1},{1,0},{2,3},{3,2},{4,5},{5,4},{6,7},{7,6},{8,9},{9,8},{10,11... | collective-permute-start | bytes 196616 | tf_op jit(solution)/shard_map/ppermute | solution.py:314
  37.4 2.1 %collective-permute-start.9 = (f32[2,2,32,128]{3,2,1,0:T(8,128)S(1)}, f32[2,2,32,128]{3,2,1,0:T(8,128)S(1)}, u32[]{:S(2)}, u32[]{:S(2)}) collective-permute-start(f32[2,2,32,128]{3,2,1,0:T(8,128)S(1)} %get-tuple-element.11), channel_id=1, source_target_pairs={{0,1},{1,0},{2,3},{3,2},{4,5},{5,4},{6,7},{7,6},{8,9},{9,8},{10,11... | collective-permute-start | bytes 196616 | tf_op jit(solution)/shard_map/ppermute | solution.py:343
  38.0 4.3 %collective-permute-start.10 = (f32[2,2,32,128]{3,2,1,0:T(8,128)S(1)}, f32[2,2,32,128]{3,2,1,0:T(8,128)S(1)}, u32[]{:S(2)}, u32[]{:S(2)}) collective-permute-start(f32[2,2,32,128]{3,2,1,0:T(8,128)S(1)} %get-tuple-element.12), channel_id=1, source_target_pairs={{0,2},{1,3},{2,0},{3,1},{4,6},{5,7},{6,4},{7,5},{8,10},{9,11},{10,... | collective-permute-start | bytes 196616 | tf_op jit(solution)/shard_map/ppermute | solution.py:343
  39.5 4.4 %collective-permute-start.11 = (f32[2,2,32,128]{3,2,1,0:T(8,128)S(1)}, f32[2,2,32,128]{3,2,1,0:T(8,128)S(1)}, u32[]{:S(2)}, u32[]{:S(2)}) collective-permute-start(f32[2,2,32,128]{3,2,1,0:T(8,128)S(1)} %get-tuple-element.13), channel_id=1, source_target_pairs={{0,3},{1,2},{2,1},{3,0},{4,7},{5,6},{6,5},{7,4},{8,11},{9,10},{10,... | collective-permute-start | bytes 196616 | tf_op jit(solution)/shard_map/ppermute | solution.py:343

commit v2 on v1

--- a/solution.py
+++ b/solution.py
@@ -187,74 +187,101 @@
     return jnp.where(rows == columns, real - zr, real), jnp.where(rows == columns, -zi, imag)
 
 
-def prepare(place, onsite, coupling, packed, half):
+def prepare(pole_real, pole_imag, pole_weight, onsite, packed, pole):
     packed[...] = pack((onsite[0, 0], onsite[0, 1]))
-    half[...] = coupling[0, place[2]]
-
-
-def start_chain(slabs, place, pole, *refs):
+    scalars = (pole_real[0], pole_imag[0], pole_weight[0, 0], pole_weight[0, 1])
+    for row, value in enumerate(scalars):
+        pole[row : row + 1, :] = jnp.full((1, pole.shape[1]), value, f32)
+
+
+def scalars_of(pole):
+    return [pole[row : row + 1, :] for row in range(4)]
+
+
+def chain_end(slabs, me):
+    return jnp.where(me < slabs // 2, 0, slabs - 1)
+
+
+def start_chain(slabs, pole, *refs):
     blocks, out, chosen = refs[: slabs // 2], refs[-2], refs[-1]
-    me = place[0]
-    end = jnp.where(me < slabs // 2, 0, slabs - 1)
+    me = lax.axis_index("slab")
+    distance = me ^ chain_end(slabs, me)
+    zr, zi, _, _ = scalars_of(pole)
     for k, ref in enumerate(blocks):
 
-        @pl.when((me ^ end) == k)
+        @pl.when(distance == k)
         def _(ref=ref):
             chosen[...] = ref[...]
 
-    (inverse,) = inverses_of(unpack_shifted(chosen[...], pole[0], pole[1]))
+    (inverse,) = inverses_of(unpack_shifted(chosen[...], zr, zi))
     put(out, inverse)
 
 
-def finish(slabs, poles, place, pole, start, coupling, *refs):
+def chain(slabs, left, blocks, links, zr, zi):
+    def block(from_left, j):
+        return unpack_shifted(blocks[jnp.where(from_left, j, slabs - 1 - j)], zr, zi)
+
+    def link(from_left, j):
+        real, imag = get(links, jnp.where(from_left, j, slabs - j))
+        return jnp.where(from_left, real, real.T), jnp.where(from_left, imag, -imag.T)
+
+    def reduced(from_left, j, inverse):
+        k = link(from_left, j)
+        out, back = times(inverse, k), adjoint(k)
+        return times(back, out), out, times(back, inverse)
+
+    return block, reduced
+
+
+def advance(slabs, pole, start, *refs):
     packed, refs = refs[:slabs], refs[slabs:]
-    halves, refs = refs[: 2 * (slabs - 1)], refs[2 * (slabs - 1) :]
+    near, (here, there, outward, inward, blocks, links) = refs[: slabs // 2], refs[slabs // 2 :]
+    me = lax.axis_index("slab")
+    left = me < slabs // 2
+    zr, zi, _, _ = scalars_of(pole)
+    for k in range(slabs):
+        blocks[me ^ k] = packed[k][...]
+    for k in range(slabs // 2):
+        links[me ^ k] = near[k][0]
+    block, reduced = chain(slabs, left, blocks, links, zr, zi)
+    taken, out, back = reduced(left, 1, get(start))
+    put(outward, out)
+    put(inward, back)
+    own, far = inverses_of(minus(block(left, 1), taken), block(jnp.logical_not(left), 0))
+    put(here, own)
+    put(there, far)
+
+
+def finish(slabs, poles, pole, start, here, there, outward_1, inward_1, *refs):
+    packed, couplings, refs = refs[:slabs], refs[slabs : 2 * slabs], refs[2 * slabs :]
     outs, (blocks, links, outward, inward, own, far, work, greens) = refs[:poles], refs[poles:]
-    me, mine, sub = place[0], place[1], place[2]
+    me, mine = lax.axis_index("slab"), lax.axis_index(("pole", "sub"))
     middle = slabs // 2
     order = start.shape[-1]
     for k in range(slabs):
         blocks[me ^ k] = packed[k][...]
-    links[me] = coupling[0]
-    for k in range(1, slabs):
-        links[me ^ k, sub] = halves[2 * k - 2][...]
-        links[me ^ k, 1 - sub] = halves[2 * k - 1][...]
-    zr, zi = pole[0], pole[1]
+        links[me ^ k] = couplings[k][0]
+    zr, zi, wr, wi = scalars_of(pole)
     left = me < middle
-
-    def block(from_left, j):
-        return unpack_shifted(blocks[jnp.where(from_left, j, slabs - 1 - j)], zr, zi)
-
-    def link(from_left, j):
-        real, imag = get(links, jnp.where(from_left, j, slabs - j))
-        return jnp.where(from_left, real, real.T), jnp.where(from_left, imag, -imag.T)
-
-    def reduced(from_left, j, inverse):
-        k = link(from_left, j)
-        out, back = times(inverse, k), adjoint(k)
-        return times(back, out), out, times(back, inverse)
-
-    put(own, (start[0], start[1]), 0)
     right = jnp.logical_not(left)
-
-    def level(j, far_pivot):
+    block, reduced = chain(slabs, left, blocks, links, zr, zi)
+    own[0], own[1], far[0] = start[...], here[...], there[...]
+    outward[1], inward[1] = outward_1[...], inward_1[...]
+
+    def far_pivot(j):
+        return minus(block(right, j), reduced(right, j, get(far, j - 1))[0])
+
+    def level(j, _):
         taken, out, back = reduced(left, j, get(own, j - 1))
         put(outward, out, j)
         put(inward, back, j)
-        here, there = inverses_of(minus(block(left, j), taken), far_pivot())
-        put(own, here, j)
-        put(far, there, j - 1)
-
-    def far_pivot(j):
-        return minus(block(right, j), reduced(right, j, get(far, j - 1))[0])
-
-    level(1, lambda: block(right, 0))
-
-    def next_level(j, _):
-        level(j, lambda: far_pivot(j - 1))
+        one, two = inverses_of(minus(block(left, j), taken), far_pivot(j - 1))
+        put(own, one, j)
+        put(far, two, j - 1)
         return 0
 
-    lax.fori_loop(2, middle, next_level, 0)
+    if middle > 2:
+        lax.fori_loop(2, middle, level, 0)
     taken, out, back = reduced(left, middle, get(own, middle - 1))
     put(outward, out, middle)
     put(inward, back, middle)
@@ -269,7 +296,6 @@
 
     lax.fori_loop(0, middle - jnp.where(left, me, slabs - 1 - me), retreat, 0)
     gr, gi = get(greens)
-    wr, wi = pole[2], pole[3]
     rows = order // poles
     for slot, (ur, ui) in enumerate(((wr, wi), (wr * zr - wi * zi, wr * zi + wi * zr))):
         real, imag = ur * gr - ui * gi, ur * gi + ui * gr
@@ -283,10 +309,6 @@
 def shards(slabs, poles, onsite, coupling, pole_real, pole_imag, pole_weight):
     order = onsite.shape[-1]
     middle = slabs // 2
-    place = jnp.stack(
-        [lax.axis_index("slab"), lax.axis_index(("pole", "sub")), lax.axis_index("sub")]
-    ).astype(jnp.int32)
-    pole = jnp.concatenate([pole_real, pole_imag, pole_weight[0]])
     vmem = pl.BlockSpec(memory_space=pltpu.VMEM)
     smem = pl.BlockSpec(memory_space=pltpu.SMEM)
     params = pltpu.CompilerParams(vmem_limit_bytes=40 << 20)
@@ -296,35 +318,46 @@
     def scratch(*lead):
         return pltpu.VMEM((*lead, order, order), f32)
 
-    packed, half = pl.pallas_call(
+    def cost(inversions):
+        return pl.CostEstimate(
+            flops=inversions * 25 * 10**8, bytes_accessed=inversions * 10**6, transcendentals=0
+        )
+
+    packed, pole = pl.pallas_call(
         prepare,
-        out_shape=[square_of, square_of],
-        in_specs=[smem, vmem, vmem],
+        out_shape=[square_of, jax.ShapeDtypeStruct((ROWS, order), f32)],
+        in_specs=[smem, smem, smem, vmem],
         out_specs=[vmem, vmem],
         compiler_params=params,
-    )(place, onsite, coupling)
+    )(pole_real, pole_imag, pole_weight, onsite)
 
     def swap(value, k):
         return lax.ppermute(value, "slab", [(i, i ^ k) for i in range(slabs)])
 
     blocks = [packed] + [swap(packed, k) for k in range(1, slabs)]
-    halves = []
-    for k in range(1, slabs):
-        got = swap(half, k)
-        halves += [got, lax.ppermute(got, "sub", [(0, 1), (1, 0)])]
+    links = [coupling] + [swap(coupling, k) for k in range(1, slabs)]
     start = pl.pallas_call(
         functools.partial(start_chain, slabs),
         out_shape=complex_of,
-        in_specs=[smem, smem] + [vmem] * middle,
+        in_specs=[vmem] * (1 + middle),
         out_specs=vmem,
         scratch_shapes=[scratch()],
         compiler_params=params,
-        cost_estimate=pl.CostEstimate(flops=2 * 10**9, bytes_accessed=10**6, transcendentals=0),
-    )(place, pole, *blocks[:middle])
+        cost_estimate=cost(2),
+    )(pole, *blocks[:middle])
+    second = pl.pallas_call(
+        functools.partial(advance, slabs),
+        out_shape=[complex_of] * 4,
+        in_specs=[vmem] * (2 + slabs + middle),
+        out_specs=[vmem] * 4,
+        scratch_shapes=[scratch(slabs), scratch(slabs, 2)],
+        compiler_params=params,
+        cost_estimate=cost(2),
+    )(pole, start, *blocks, *links[:middle])
     pieces = pl.pallas_call(
         functools.partial(finish, slabs, poles),
         out_shape=[jax.ShapeDtypeStruct((2, 2, order // poles, order), f32)] * poles,
-        in_specs=[smem, smem] + [vmem] * (2 + slabs + len(halves)),
+        in_specs=[vmem] * (6 + 2 * slabs),
         out_specs=[vmem] * poles,
         scratch_shapes=[
             scratch(slabs),
@@ -337,7 +370,8 @@
             scratch(2),
         ],
         compiler_params=params,
-    )(place, pole, start, coupling, *blocks, *halves)
+        cost_estimate=cost(2),
+    )(pole, start, *second, *blocks, *links)
     total = pieces[0]
     for k in range(1, poles):
         total = total + lax.ppermute(pieces[k], ("pole", "sub"), [(i, i ^ k) for i in range(poles)])

time: 44.7 us -> 39.9 us (0.89)
  waiting for transfers between devices: 5.42 us -> 3.76 us
  local copies, waits for them, and re-layouts: 3.09 us -> 1.54 us
  starting transfers between devices: 12.8 us -> 12 us
  Pallas kernels: 21 us -> 20.3 us
    pallas_call x1, Pallas kernels: 14.8 us -> 7.86 us  [shards(): pl.pallas_call(functools.partial(finish, slabs, poles), out_shape=[jax.Sh...]
    pallas_call x1 -> x2, Pallas kernels: 0.64 us -> 7.41 us  [the longest x1 6.77 us: shards(): pl.pallas_call(functools.partial(advance, slabs), out_shape=[complex_of]...]
    unnamed x8 -> x6, local copies, waits for them, and re-layouts: 2.46 us -> 0.91 us
    ppermute x6, waiting for transfers between devices: 1.05 us -> 0.02 us  [swap(): return lax.ppermute(value, 'slab', [(i, i ^ k) for i in range(slabs)])]
    ppermute x3, waiting for transfers between devices: 4.37 us -> 3.74 us  [shards(): lax.ppermute(pieces[k], ('pole', 'sub'), [(i, i ^ k) for i in range(poles)])]
    pallas_call x1, Pallas kernels: 5.6 us -> 5.05 us  [shards(): pl.pallas_call(functools.partial(start_chain, slabs), out_shape=complex_o...]
    ppermute x3 -> x0, starting transfers between devices: 0.51 us -> none  [shards(): halves += [got, lax.ppermute(got, 'sub', [(0, 1), (1, 0)])]]
  transfers between devices with their start and end apart: 12 -> 9, of which waited for: 3 -> 2; matrix products, arithmetic and copies ran while one was open for 0% -> 0% of each run, Pallas kernels for 13% -> 30%
where the time goes in v2:
time: 39.9 us; the launch traced here: 39.7 us
  Pallas kernels  20.3 us (51%)
  starting transfers between devices  12 us (30%)
  waiting for transfers between devices  3.76 us (9%)
  between operations  2.05 us (5%)
  local copies, waits for them, and re-layouts  1.54 us (4%)
    ppermute x6, starting transfers between devices, swap(): return lax.ppermute(value, 'slab', [(i, i ^ k) for i in range(slabs)])  10.1 us
    pallas_call x1, Pallas kernels, shards(): pl.pallas_call(functools.partial(finish, slabs, poles), out_shape=[jax.Sh...  7.86 us
    pallas_call x1, Pallas kernels, shards(): pl.pallas_call(functools.partial(advance, slabs), out_shape=[complex_of]...  6.77 us
    pallas_call x1, Pallas kernels, shards(): pl.pallas_call(functools.partial(start_chain, slabs), out_shape=complex_o...  5.05 us
    ppermute x3, waiting for transfers between devices, shards(): lax.ppermute(pieces[k], ('pole', 'sub'), [(i, i ^ k) for i in range(poles)])  3.74 us
    ppermute x3, starting transfers between devices, shards(): lax.ppermute(pieces[k], ('pole', 'sub'), [(i, i ^ k) for i in range(poles)])  1.93 us
    unnamed x6, local copies, waits for them, and re-layouts  0.91 us
  transfers between devices with their start and end apart: 9, of which 2 were waited for; matrix products, arithmetic and copies ran while one was open for 0% of the time, Pallas kernels for 30%

profile of v2, /device:TPU:0, one launch (start us, length us, event | category | flops | bytes accessed | tf_op | source)
XLA Modules:
  0.0 39.7 jit_solution(5661194554163383676)
XLA Ops:
  2.0 0.9 %copy-done = f32[1,2,128,128]{3,2,1,0:T(8,128)S(1)} copy-done((f32[1,2,128,128]{3,2,1,0:T(8,128)S(1)}, f32[1,2,128,128]{3,2,1,0:T(8,128)}, u32[]{:S(2)}) %copy-start) | copy-done | bytes 131096
  2.9 0.6 %shard_map.68 = (f32[128,128]{1,0:T(8,128)S(1)}, f32[8,128]{1,0:T(8,128)S(1)}) custom-call(f32[1]{0:T(128)S(6)} %copy.7.pole_real, f32[1]{0:T(128)S(6)} %copy.8.pole_imag, f32[1,2]{1,0:T(1,128)S(1)} %copy-done.1, f32[1,2,128,128]{3,2,1,0:T(8,128)S(1)} %copy-done), custom_call_target="tpu_custom_call" | custom-call | tf_op jit(solution)/shard_map/pallas_call | solution.py:326
  3.5 3.1 %collective-permute-start = (f32[128,128]{1,0:T(8,128)S(1)}, f32[128,128]{1,0:T(8,128)S(1)}, u32[]{:S(2)}, u32[]{:S(2)}) collective-permute-start(f32[128,128]{1,0:T(8,128)S(1)} %get-tuple-element.13.refs_0_), channel_id=1, source_target_pairs={{0,4},{4,0},{8,12},{12,8},{1,5},{5,1},{9,13},{13,9},{2,6},{6,2},{1... | collective-permute-start | bytes 196616 | tf_op jit(solution)/shard_map/ppermute | solution.py:335
  6.6 2.5 %collective-permute-start.2 = (f32[128,128]{1,0:T(8,128)S(1)}, f32[128,128]{1,0:T(8,128)S(1)}, u32[]{:S(2)}, u32[]{:S(2)}) collective-permute-start(f32[128,128]{1,0:T(8,128)S(1)} %get-tuple-element.13.refs_0_), channel_id=1, source_target_pairs={{0,12},{4,8},{8,4},{12,0},{1,13},{5,9},{9,5},{13,1},{2,14},{6,10},... | collective-permute-start | bytes 196616 | tf_op jit(solution)/shard_map/ppermute | solution.py:335
  9.1 0.1 collective-permute-start.1
  9.2 2.8 %collective-permute-start.4 = (f32[1,2,128,128]{3,2,1,0:T(8,128)S(1)}, f32[1,2,128,128]{3,2,1,0:T(8,128)S(1)}, u32[]{:S(2)}, u32[]{:S(2)}) collective-permute-start(f32[1,2,128,128]{3,2,1,0:T(8,128)S(1)} %copy-done.2), channel_id=1, source_target_pairs={{0,8},{4,12},{8,0},{12,4},{1,9},{5,13},{9,1},{13,5},{2,10},{6,14},... | collective-permute-start | bytes 393224 | tf_op jit(solution)/shard_map/ppermute | solution.py:335
  12.0 0.7 %collective-permute-start.3 = (f32[1,2,128,128]{3,2,1,0:T(8,128)S(1)}, f32[1,2,128,128]{3,2,1,0:T(8,128)S(1)}, u32[]{:S(2)}, u32[]{:S(2)}) collective-permute-start(f32[1,2,128,128]{3,2,1,0:T(8,128)S(1)} %copy-done.2), channel_id=1, source_target_pairs={{0,4},{4,0},{8,12},{12,8},{1,5},{5,1},{9,13},{13,9},{2,6},{6,2},{1... | collective-permute-start | bytes 393224 | tf_op jit(solution)/shard_map/ppermute | solution.py:335
  12.7 0.0 collective-permute-done.refs_1_
  12.7 0.9 %collective-permute-start.5 = (f32[1,2,128,128]{3,2,1,0:T(8,128)S(1)}, f32[1,2,128,128]{3,2,1,0:T(8,128)S(1)}, u32[]{:S(2)}, u32[]{:S(2)}) collective-permute-start(f32[1,2,128,128]{3,2,1,0:T(8,128)S(1)} %copy-done.2), channel_id=1, source_target_pairs={{0,12},{4,8},{8,4},{12,0},{1,13},{5,9},{9,5},{13,1},{2,14},{6,10},... | collective-permute-start | bytes 393224 | tf_op jit(solution)/shard_map/ppermute | solution.py:335
  13.6 5.0 %shard_map.69.start = f32[2,128,128]{2,1,0:T(8,128)S(1)} custom-call(f32[8,128]{1,0:T(8,128)S(1)} %get-tuple-element.12.pole, f32[128,128]{1,0:T(8,128)S(1)} %get-tuple-element.13.refs_0_, f32[128,128]{1,0:T(8,128)S(1)} %collective-permute-done.refs_1_), custom_call_target="tpu_custom_call" | custom-call | flops 5000000000 | bytes 2000000 | tf_op jit(solution)/shard_map/pallas_call | solution.py:339
  18.6 0.0 collective-permute-done.2.refs_3_
  18.7 0.0 collective-permute-done.1.refs_2_
  18.7 0.0 collective-permute-done.3.refs_5_
  18.7 6.8 %shard_map.70 = (f32[2,128,128]{2,1,0:T(8,128)S(1)}, f32[2,128,128]{2,1,0:T(8,128)S(1)}, f32[2,128,128]{2,1,0:T(8,128)S(1)}, f32[2,128,128]{2,1,0:T(8,128)S(1)}) custom-call(f32[8,128]{1,0:T(8,128)S(1)} %get-tuple-element.12.pole, f32[2,128,128]{2,1,0:T(8,128)S(1)} %shard_map.69.start, f32[128,128]{1,0:T(8,128)S(1)} %get-tuple-element.13.refs_0_, ...), custom_call_target="tpu_custom_call" | custom-call | flops 5000000000 | bytes 2000000 | tf_op jit(solution)/shard_map/pallas_call | solution.py:348
  25.4 0.0 collective-permute-done.4.refs_6_
  25.5 0.0 collective-permute-done.5.refs_7_
  25.5 7.9 %shard_map.71 = (f32[2,2,32,128]{3,2,1,0:T(8,128)S(1)}, f32[2,2,32,128]{3,2,1,0:T(8,128)S(1)}, f32[2,2,32,128]{3,2,1,0:T(8,128)S(1)}, f32[2,2,32,128]{3,2,1,0:T(8,128)S(1)}) custom-call(f32[8,128]{1,0:T(8,128)S(1)} %get-tuple-element.12.pole, f32[2,128,128]{2,1,0:T(8,128)S(1)} %shard_map.69.start, f32[2,128,128]{2,1,0:T(8,128)S(1)} %get-tuple-element.14.here, ...), custom_call_target="tpu_custom_call" | custom-call | flops 5000000000 | bytes 2000000 | tf_op jit(solution)/shard_map/pallas_call | solution.py:357
  33.3 0.1 collective-permute-start.6
  33.4 1.6 %collective-permute-start.7 = (f32[2,2,32,128]{3,2,1,0:T(8,128)S(1)}, f32[2,2,32,128]{3,2,1,0:T(8,128)S(1)}, u32[]{:S(2)}, u32[]{:S(2)}) collective-permute-start(f32[2,2,32,128]{3,2,1,0:T(8,128)S(1)} %get-tuple-element.20), channel_id=1, source_target_pairs={{0,2},{1,3},{2,0},{3,1},{4,6},{5,7},{6,4},{7,5},{8,10},{9,11},{10,... | collective-permute-start | bytes 196616 | tf_op jit(solution)/shard_map/ppermute | solution.py:377
  35.0 0.3 collective-permute-start.8
  35.3 0.0 collective-permute-done.6
  35.3 2.6 %collective-permute-done.7 = f32[2,2,32,128]{3,2,1,0:T(8,128)S(1)} collective-permute-done((f32[2,2,32,128]{3,2,1,0:T(8,128)S(1)}, f32[2,2,32,128]{3,2,1,0:T(8,128)S(1)}, u32[]{:S(2)}, u32[]{:S(2)}) %collective-permute-start.7) | collective-permute-done | bytes 65568 | tf_op jit(solution)/shard_map/ppermute | solution.py:377
  37.9 1.1 %collective-permute-done.8 = f32[2,2,32,128]{3,2,1,0:T(8,128)S(1)} collective-permute-done((f32[2,2,32,128]{3,2,1,0:T(8,128)S(1)}, f32[2,2,32,128]{3,2,1,0:T(8,128)S(1)}, u32[]{:S(2)}, u32[]{:S(2)}) %collective-permute-start.8) | collective-permute-done | bytes 65568 | tf_op jit(solution)/shard_map/ppermute | solution.py:377
  39.0 0.6 %fusion = (f32[1,2,32,128]{3,2,1,0:T(8,128)}, f32[1,2,32,128]{3,2,1,0:T(8,128)}) fusion(f32[2,2,32,128]{3,2,1,0:T(8,128)S(1)} %add_add_fusion), kind=kLoop, calls=%fused_computation.1 | loop fusion | bytes 131072 | tf_op jit(solution)/shard_map/slice | solution.py:378
  (6 shorter events, 0.0 us)
Async XLA Ops:
  1.3 0.7 %copy-start.1 = (f32[1,2]{1,0:T(1,128)S(1)}, f32[1,2]{1,0:T(1,128)}, u32[]{:S(2)}) copy-start(f32[1,2]{1,0:T(1,128)} %pole_weight.1) | copy-start | bytes 28
  2.0 0.9 %copy-start = (f32[1,2,128,128]{3,2,1,0:T(8,128)S(1)}, f32[1,2,128,128]{3,2,1,0:T(8,128)}, u32[]{:S(2)}) copy-start(f32[1,2,128,128]{3,2,1,0:T(8,128)} %onsite.1) | copy-start | bytes 393220
  2.9 6.3 %copy-start.2 = (f32[1,2,128,128]{3,2,1,0:T(8,128)S(1)}, f32[1,2,128,128]{3,2,1,0:T(8,128)}, u32[]{:S(2)}) copy-start(f32[1,2,128,128]{3,2,1,0:T(8,128)} %refs_4_.3) | copy-start | bytes 393220
  3.5 9.2 %collective-permute-start = (f32[128,128]{1,0:T(8,128)S(1)}, f32[128,128]{1,0:T(8,128)S(1)}, u32[]{:S(2)}, u32[]{:S(2)}) collective-permute-start(f32[128,128]{1,0:T(8,128)S(1)} %get-tuple-element.13.refs_0_), channel_id=1, source_target_pairs={{0,4},{4,0},{8,12},{12,8},{1,5},{5,1},{9,13},{13,9},{2,6},{6,2},{1... | collective-permute-start | bytes 196616 | tf_op jit(solution)/shard_map/ppermute | solution.py:335
  6.6 12.0 %collective-permute-start.2 = (f32[128,128]{1,0:T(8,128)S(1)}, f32[128,128]{1,0:T(8,128)S(1)}, u32[]{:S(2)}, u32[]{:S(2)}) collective-permute-start(f32[128,128]{1,0:T(8,128)S(1)} %get-tuple-element.13.refs_0_), channel_id=1, source_target_pairs={{0,12},{4,8},{8,4},{12,0},{1,13},{5,9},{9,5},{13,1},{2,14},{6,10},... | collective-permute-start | bytes 196616 | tf_op jit(solution)/shard_map/ppermute | solution.py:335
  9.1 9.6 %collective-permute-start.1 = (f32[128,128]{1,0:T(8,128)S(1)}, f32[128,128]{1,0:T(8,128)S(1)}, u32[]{:S(2)}, u32[]{:S(2)}) collective-permute-start(f32[128,128]{1,0:T(8,128)S(1)} %get-tuple-element.13.refs_0_), channel_id=1, source_target_pairs={{0,8},{4,12},{8,0},{12,4},{1,9},{5,13},{9,1},{13,5},{2,10},{6,14},... | collective-permute-start | bytes 196616 | tf_op jit(solution)/shard_map/ppermute | solution.py:335
  9.2 16.3 %collective-permute-start.4 = (f32[1,2,128,128]{3,2,1,0:T(8,128)S(1)}, f32[1,2,128,128]{3,2,1,0:T(8,128)S(1)}, u32[]{:S(2)}, u32[]{:S(2)}) collective-permute-start(f32[1,2,128,128]{3,2,1,0:T(8,128)S(1)} %copy-done.2), channel_id=1, source_target_pairs={{0,8},{4,12},{8,0},{12,4},{1,9},{5,13},{9,1},{13,5},{2,10},{6,14},... | collective-permute-start | bytes 393224 | tf_op jit(solution)/shard_map/ppermute | solution.py:335
  12.0 6.7 %collective-permute-start.3 = (f32[1,2,128,128]{3,2,1,0:T(8,128)S(1)}, f32[1,2,128,128]{3,2,1,0:T(8,128)S(1)}, u32[]{:S(2)}, u32[]{:S(2)}) collective-permute-start(f32[1,2,128,128]{3,2,1,0:T(8,128)S(1)} %copy-done.2), channel_id=1, source_target_pairs={{0,4},{4,0},{8,12},{12,8},{1,5},{5,1},{9,13},{13,9},{2,6},{6,2},{1... | collective-permute-start | bytes 393224 | tf_op jit(solution)/shard_map/ppermute | solution.py:335
  12.7 12.8 %collective-permute-start.5 = (f32[1,2,128,128]{3,2,1,0:T(8,128)S(1)}, f32[1,2,128,128]{3,2,1,0:T(8,128)S(1)}, u32[]{:S(2)}, u32[]{:S(2)}) collective-permute-start(f32[1,2,128,128]{3,2,1,0:T(8,128)S(1)} %copy-done.2), channel_id=1, source_target_pairs={{0,12},{4,8},{8,4},{12,0},{1,13},{5,9},{9,5},{13,1},{2,14},{6,10},... | collective-permute-start | bytes 393224 | tf_op jit(solution)/shard_map/ppermute | solution.py:335
  33.3 1.9 %collective-permute-start.6 = (f32[2,2,32,128]{3,2,1,0:T(8,128)S(1)}, f32[2,2,32,128]{3,2,1,0:T(8,128)S(1)}, u32[]{:S(2)}, u32[]{:S(2)}) collective-permute-start(f32[2,2,32,128]{3,2,1,0:T(8,128)S(1)} %get-tuple-element.19), channel_id=1, source_target_pairs={{0,1},{1,0},{2,3},{3,2},{4,5},{5,4},{6,7},{7,6},{8,9},{9,8},{10,11... | collective-permute-start | bytes 196616 | tf_op jit(solution)/shard_map/ppermute | solution.py:377
  33.4 4.5 %collective-permute-start.7 = (f32[2,2,32,128]{3,2,1,0:T(8,128)S(1)}, f32[2,2,32,128]{3,2,1,0:T(8,128)S(1)}, u32[]{:S(2)}, u32[]{:S(2)}) collective-permute-start(f32[2,2,32,128]{3,2,1,0:T(8,128)S(1)} %get-tuple-element.20), channel_id=1, source_target_pairs={{0,2},{1,3},{2,0},{3,1},{4,6},{5,7},{6,4},{7,5},{8,10},{9,11},{10,... | collective-permute-start | bytes 196616 | tf_op jit(solution)/shard_map/ppermute | solution.py:377
  35.0 4.0 %collective-permute-start.8 = (f32[2,2,32,128]{3,2,1,0:T(8,128)S(1)}, f32[2,2,32,128]{3,2,1,0:T(8,128)S(1)}, u32[]{:S(2)}, u32[]{:S(2)}) collective-permute-start(f32[2,2,32,128]{3,2,1,0:T(8,128)S(1)} %get-tuple-element.21), channel_id=1, source_target_pairs={{0,3},{1,2},{2,1},{3,0},{4,7},{5,6},{6,5},{7,4},{8,11},{9,10},{10,... | collective-permute-start | bytes 196616 | tf_op jit(solution)/shard_map/ppermute | solution.py:377

commit v3 on v2

v3 whole, which is shorter than its diff:
```python
import functools

import jax
import jax.numpy as jnp
from jax import lax
from jax.experimental import pallas as pl
from jax.experimental.pallas import tpu as pltpu
from jax.sharding import PartitionSpec as P

ROWS = 8
PANEL = 2 * ROWS
f32, bf16 = jnp.float32, jnp.bfloat16
PARTS = ((0, 0), (0, 1), (1, 0), (1, 1), (0, 2), (2, 0))


def row_of(tile, k):
    return jnp.broadcast_to(tile[k : k + 1, :], tile.shape)


def lane_of(tile, k):
    where = jnp.full(tile.shape, k, jnp.int32)
    return jnp.take_along_axis(tile, where, axis=1, mode="promise_in_bounds")


def plus(a, b):
    return a[0] + b[0], a[1] + b[1]


def minus(a, b):
    return a[0] - b[0], a[1] - b[1]


def complex_times(a, b):
    return a[0] * b[0] - a[1] * b[1], a[0] * b[1] + a[1] * b[0]


def sweep_double(tiles, first, lane, subl):
    tiles = list(tiles)
    columns = [[(lane_of(xr, first + j), lane_of(xi, first + j)) for j in range(ROWS)] for xr, xi in tiles]
    for k in range(0, ROWS, 2):
        for s, cols in enumerate(columns):

            def entries(pair):
                return [(row_of(pair[0], i), row_of(pair[1], i)) for i in (k, k + 1)]

            (a, c), (b, d) = entries(cols[k]), entries(cols[k + 1])
            det = minus(complex_times(a, d), complex_times(b, c))
            scale = 1.0 / (det[0] * det[0] + det[1] * det[1])
            over = det[0] * scale, -det[1] * scale
            one = cols[k][0] - (subl == k).astype(f32), cols[k][1]
            two = cols[k + 1][0] - (subl == k + 1).astype(f32), cols[k + 1][1]
            one, two = (
                minus(complex_times(one, d), complex_times(two, c)),
                minus(complex_times(two, a), complex_times(one, b)),
            )
            for j in range(k + 2, min(k + 4, ROWS)):
                upper, lower = entries(cols[j])
                taken = plus(complex_times(one, upper), complex_times(two, lower))
                cols[j] = minus(cols[j], complex_times(taken, over))
            one, two = complex_times(one, over), complex_times(two, over)
            for j in range(k + 4, ROWS):
                upper, lower = entries(cols[j])
                cols[j] = minus(cols[j], plus(complex_times(one, upper), complex_times(two, lower)))
            upper, lower = entries(tiles[s])
            upper = upper[0] + (lane == first + k).astype(f32), upper[1]
            lower = lower[0] + (lane == first + k + 1).astype(f32), lower[1]
            tiles[s] = minus(tiles[s], plus(complex_times(one, upper), complex_times(two, lower)))
    return tiles


def sweep_single(tiles, first, lane, subl):
    tiles = list(tiles)
    columns = [[(lane_of(xr, first + j), lane_of(xi, first + j)) for j in range(ROWS)] for xr, xi in tiles]
    for k in range(ROWS):
        in_row, in_lane = (subl == k).astype(f32), (lane == first + k).astype(f32)
        for s, cols in enumerate(columns):
            xr, xi = tiles[s]
            tr, ti = cols[k]
            dr, di = row_of(tr, k), row_of(ti, k)
            scale = 1.0 / (dr * dr + di * di)
            rr, ri = dr * scale, -di * scale
            cr = tr - in_row
            cr, ci = cr * rr - ti * ri, cr * ri + ti * rr
            for j in range(k + 1, ROWS):
                ar, ai = row_of(cols[j][0], k), row_of(cols[j][1], k)
                cols[j] = (cols[j][0] - (cr * ar - ci * ai), cols[j][1] - (cr * ai + ci * ar))
            ar, ai = row_of(xr, k) + in_lane, row_of(xi, k)
            tiles[s] = (xr - (cr * ar - ci * ai), xi - (cr * ai + ci * ar))
    return tiles


def follow(tile, swept, first, inside):
    ar, ai = tile
    nr, ni = jnp.where(inside, 0.0, ar), jnp.where(inside, 0.0, ai)
    pr = pi = None
    for k in range(ROWS):
        cr, ci = lane_of(ar, first + k), lane_of(ai, first + k)
        ur, ui = row_of(swept[0], k), row_of(swept[1], k)
        tr, ti = cr * ur - ci * ui, cr * ui + ci * ur
        if k % 2 == 0:
            nr, ni = nr - tr, ni - ti
        else:
            pr, pi = (tr, ti) if pr is None else (pr + tr, pi + ti)
    return nr - pr, ni - pi


def split(x):
    parts = [x.astype(bf16)]
    for _ in range(2):
        x = x - parts[-1].astype(f32)
        parts.append(x.astype(bf16))
    return parts


def multiply(left, right, columns):
    lhs = jnp.concatenate([part for a, _ in PARTS for part in (left[0][a], left[1][a])], axis=1)
    rhs = jnp.concatenate(
        [
            jnp.concatenate(pair, axis=1)
            for _, b in PARTS
            for pair in ((right[0][b], right[1][b]), (-right[1][b], right[0][b]))
        ],
        axis=0,
    )
    whole = lax.dot_general(lhs, rhs, (((1,), (0,)), ((), ())), preferred_element_type=f32)
    return whole[:, :columns], whole[:, columns:]


def times(left, right):
    columns = right[0].shape[1]
    return multiply([split(part) for part in left], [split(part) for part in right], columns)


def others_follow(tiles, panel, place):
    order = tiles[0][0].shape[1]

    def padded(rows):
        above, below = PANEL * place, order - PANEL * (place + 1)
        parts = [jnp.zeros((above, order), bf16)] if above else []
        parts += [rows]
        parts += [jnp.zeros((below, order), bf16)] if below else []
        return jnp.concatenate(parts, axis=0)

    left = [split(jnp.concatenate(part, axis=0)) for part in zip(*tiles)]
    right = [[padded(rows) for rows in split(jnp.concatenate(part, axis=0))] for part in zip(*panel)]
    real, imag = multiply(left, right, order)
    return [(real[ROWS * t : ROWS * t + ROWS], imag[ROWS * t : ROWS * t + ROWS]) for t in range(len(tiles))]


def invert(systems):
    order = systems[0][0][0].shape[1]
    count, panels = order // ROWS, order // PANEL
    lane = lax.broadcasted_iota(jnp.int32, (ROWS, order), 1)
    subl = lax.broadcasted_iota(jnp.int32, (ROWS, order), 0)
    systems = [list(tiles) for tiles in systems]
    sweep = sweep_double if len(systems) == 1 else sweep_single
    for place in range(panels):
        a, b = 2 * place, 2 * place + 1
        in_a = (lane >= ROWS * a) & (lane < ROWS * a + ROWS)
        in_b = (lane >= ROWS * b) & (lane < ROWS * b + ROWS)
        soon = [] if place == panels - 1 else [b + 1, b + 2]
        first = sweep([tiles[a] for tiles in systems], ROWS * a, lane, subl)
        second = [follow(tiles[b], x, ROWS * a, in_a) for tiles, x in zip(systems, first)]
        ahead = [[follow(tiles[i], x, ROWS * a, in_a) for i in soon] for tiles, x in zip(systems, first)]
        second = sweep(second, ROWS * b, lane, subl)
        ahead = [[follow(tile, x, ROWS * b, in_b) for tile in pair] for pair, x in zip(ahead, second)]
        first = [follow(tile, x, ROWS * b, in_b) for tile, x in zip(first, second)]
        rest = [i for i in range(count) if i not in (a, b, *soon)]
        rest.sort(key=lambda i: (i - b) % count)
        for s, tiles in enumerate(systems):
            delta = others_follow([tiles[i] for i in rest], [first[s], second[s]], place)
            for (dr, di), i in zip(delta, rest):
                tiles[i] = (
                    jnp.where(in_a | in_b, 0.0, tiles[i][0]) - dr,
                    jnp.where(in_a | in_b, 0.0, tiles[i][1]) - di,
                )
            tiles[a], tiles[b] = first[s], second[s]
            for i, tile in zip(soon, ahead[s]):
                tiles[i] = tile
    return systems


def to_tiles(value):
    count = value[0].shape[0] // ROWS
    return [tuple(part[ROWS * i : ROWS * i + ROWS] for part in value) for i in range(count)]


def from_tiles(tiles):
    return tuple(jnp.concatenate(part, axis=0) for part in zip(*tiles))


def inverses_of(*values):
    return [from_tiles(tiles) for tiles in invert([to_tiles(value) for value in values])]


def adjoint(a):
    return a[0].T, -a[1].T


def get(ref, *index):
    return ref[(*index, 0)], ref[(*index, 1)]


def put(ref, value, *index):
    ref[(*index, 0)], ref[(*index, 1)] = value


def square(order):
    rows = lax.broadcasted_iota(jnp.int32, (order, order), 0)
    columns = lax.broadcasted_iota(jnp.int32, (order, order), 1)
    return rows, columns


def hermitian(onsite):
    return 0.5 * (onsite[0] + onsite[0].T), 0.5 * (onsite[1] - onsite[1].T)


def pack(block):
    rows, columns = square(block[0].shape[0])
    return jnp.where(rows <= columns, *block)


def unpack(packed):
    rows, columns = square(packed.shape[0])
    turned = packed.T
    imag = jnp.where(rows > columns, packed, jnp.where(rows < columns, -turned, 0.0))
    return jnp.where(rows <= columns, packed, turned), imag


def shifted(block, zr, zi):
    rows, columns = square(block[0].shape[0])
    return jnp.where(rows == columns, block[0] - zr, block[0]), jnp.where(rows == columns, -zi, block[1])


def prepare(onsite, packed):
    packed[...] = pack(hermitian(get(onsite, 0)))


def spread_scalars(pole_real, pole_imag, pole_weight, pole):
    width = pole.shape[1]
    pole[0:1, :] = jnp.broadcast_to(pole_real[...].reshape(1, 1), (1, width))
    pole[1:2, :] = jnp.broadcast_to(pole_imag[...].reshape(1, 1), (1, width))
    pole[2:3, :] = jnp.broadcast_to(pole_weight[:, 0:1], (1, width))
    pole[3:4, :] = jnp.broadcast_to(pole_weight[:, 1:2], (1, width))


def scalars_of(pole):
    return [pole[row : row + 1, :] for row in range(4)]


def turned_if(turn, value):
    return jnp.where(turn, value[0].T, value[0]), jnp.where(turn, -value[1].T, value[1])


def start_chain(slabs, pole, *refs):
    near, out, chosen = refs[: slabs // 2], refs[-2], refs[-1]
    me = lax.axis_index("slab")
    distance = me ^ jnp.where(me < slabs // 2, 0, slabs - 1)
    zr, zi, _, _ = scalars_of(pole)
    for k, ref in enumerate(near):

        @pl.when(distance == k)
        def _(ref=ref):
            chosen[...] = ref[...]

    (inverse,) = inverses_of(shifted(unpack(chosen[...]), zr, zi))
    put(out, inverse)


def chain(slabs, me, blocks, links, zr, zi):
    left = me < slabs // 2

    def block(own, j):
        index = jnp.where(left == own, j, slabs - 1 - j)
        return shifted(unpack(blocks[index]), zr, zi)

    def reduced(own, j, inverse):
        from_left = left == own
        k = turned_if(jnp.logical_not(from_left), get(links, jnp.where(from_left, j, slabs - j)))
        out, back = times(inverse, k), adjoint(k)
        return times(back, out), out, back

    return block, reduced


def fill_near(me, target, refs):
    for k, ref in enumerate(refs):
        target[me ^ k] = ref[...] if ref.ndim == target.ndim - 1 else ref[0]


def fill_far(me, target, refs):
    middle, core = target.shape[0] // 2, lax.axis_index("sub")
    for i, ref in enumerate(refs):
        mask = middle + i - i % 2 + jnp.where(i % 2 == 0, core, 1 - core)
        target[me ^ mask] = ref[...] if ref.ndim == target.ndim - 1 else ref[0]


def advance(slabs, pole, start, *refs):
    middle = slabs // 2
    block_refs, link_refs, refs = refs[:slabs], refs[slabs : slabs + middle], refs[slabs + middle :]
    here, there, outward, inward, blocks, links = refs
    me = lax.axis_index("slab")
    zr, zi, _, _ = scalars_of(pole)
    fill_near(me, blocks, block_refs[:middle])
    fill_far(me, blocks, block_refs[middle:])
    fill_near(me, links, link_refs)
    block, reduced = chain(slabs, me, blocks, links, zr, zi)
    inverse = get(start)
    taken, out, back = reduced(True, 1, inverse)
    put(outward, out)
    put(inward, times(back, inverse))
    own, other = inverses_of(minus(block(True, 1), taken), block(False, 0))
    put(here, own)
    put(there, other)


def finish(slabs, poles, pole, start, second, end, outward_1, inward_1, *refs):
    middle = slabs // 2
    block_refs, link_refs, refs = refs[:slabs], refs[slabs : 2 * slabs], refs[2 * slabs :]
    outs, (blocks, links, outward, inward, own, other, work) = refs[:poles], refs[poles:]
    me, mine = lax.axis_index("slab"), lax.axis_index(("pole", "sub"))
    order = start.shape[-1]
    fill_near(me, blocks, block_refs[:middle])
    fill_far(me, blocks, block_refs[middle:])
    fill_near(me, links, link_refs[:middle])
    fill_far(me, links, link_refs[middle:])
    zr, zi, wr, wi = scalars_of(pole)
    block, reduced = chain(slabs, me, blocks, links, zr, zi)
    own[0], own[1], other[0] = start[...], second[...], end[...]
    outward[1], inward[1] = outward_1[...], inward_1[...]

    def other_pivot(j):
        return minus(block(False, j), reduced(False, j, get(other, j - 1))[0])

    def level(j, _):
        inverse = get(own, j - 1)
        taken, out, back = reduced(True, j, inverse)
        one, two = inverses_of(minus(block(True, j), taken), other_pivot(j - 1))
        put(outward, out, j)
        put(inward, times(back, inverse), j)
        put(own, one, j)
        put(other, two, j - 1)
        return 0

    def wider(j, found):
        base, out, back = found
        near_out, near_back = get(outward, j), get(inward, j)
        base = plus(get(own, j - 1), times(times(near_out, base), near_back))
        return base, times(near_out, out), times(back, near_back)

    if middle > 2:
        lax.fori_loop(2, middle, level, 0)
    inverse = get(own, middle - 1)
    taken, out, back = reduced(True, middle, inverse)
    steps = middle - 1 - jnp.where(me < middle, me, slabs - 1 - me)
    found = inverse, out, times(back, inverse)
    if middle == 2:
        further = wider(1, found)
        found = jax.tree.map(lambda new, old: jnp.where(steps > 0, new, old), further, found)
    else:
        found = lax.fori_loop(0, steps, lambda step, found: wider(middle - 1 - step, found), found)
    (green,) = inverses_of(minus(other_pivot(middle - 1), taken))
    gr, gi = plus(found[0], times(times(found[1], green), found[2]))
    gr_t, gi_t = gr.T, gi.T
    even, odd = (0.5 * (gr + gr_t), 0.5 * (gi + gi_t)), (0.5 * (gr_t - gr), 0.5 * (gi_t - gi))
    rows = order // poles
    for slot, (ur, ui) in enumerate(((wr, wi), (wr * zr - wi * zi, wr * zi + wi * zr))):
        put(work, (ur * even[1] + ui * even[0], ur * odd[0] - ui * odd[1]), slot)
    for k in range(poles):
        begin = pl.multiple_of((mine ^ k) * rows, rows)
        outs[k][...] = work[:, :, pl.ds(begin, rows), :]


def shards(slabs, poles, onsite, coupling, pole_real, pole_imag, pole_weight):
    order = onsite.shape[-1]
    middle = slabs // 2
    vmem = pl.BlockSpec(memory_space=pltpu.VMEM)
    params = pltpu.CompilerParams(vmem_limit_bytes=40 << 20)
    square_of = jax.ShapeDtypeStruct((order, order), f32)
    complex_of = jax.ShapeDtypeStruct((2, order, order), f32)

    def scratch(*lead):
        return pltpu.VMEM((*lead, order, order), f32)

    def cost(inversions):
        return pl.CostEstimate(
            flops=inversions * 25 * 10**8, bytes_accessed=inversions * 10**6, transcendentals=0
        )

    def swap(value, k):
        return lax.ppermute(value, "slab", [(i, i ^ k) for i in range(slabs)])

    packed = pl.pallas_call(
        prepare, out_shape=square_of, in_specs=[vmem], out_specs=vmem, compiler_params=params
    )(onsite)
    pole = pl.pallas_call(
        spread_scalars,
        out_shape=jax.ShapeDtypeStruct((ROWS, order), f32),
        in_specs=[vmem] * 3,
        out_specs=vmem,
        compiler_params=params,
    )(pole_real, pole_imag, pole_weight)

    def far_swap(value, k):
        pairs = [(2 * i + c, 2 * (i ^ (k + c)) + c) for i in range(slabs) for c in range(2)]
        return lax.ppermute(value, ("slab", "sub"), pairs)

    near_blocks = [packed] + [swap(packed, k) for k in range(1, middle)]
    far_blocks = [far_swap(packed, k) for k in range(middle, slabs, 2)]
    near_links = [coupling] + [swap(coupling, k) for k in range(1, middle)]
    far_links = [far_swap(coupling, k) for k in range(middle, slabs, 2)]
    start = pl.pallas_call(
        functools.partial(start_chain, slabs),
        out_shape=complex_of,
        in_specs=[vmem] * (1 + middle),
        out_specs=vmem,
        scratch_shapes=[scratch()],
        compiler_params=params,
        cost_estimate=cost(2),
    )(pole, *near_blocks)

    def both(values):
        pairs = []
        for value in values:
            mine, _ = lax.optimization_barrier((value, start))
            pairs += [value, lax.ppermute(mine, "sub", [(0, 1), (1, 0)])]
        return pairs

    blocks, links = near_blocks + both(far_blocks), near_links + both(far_links)
    second = pl.pallas_call(
        functools.partial(advance, slabs),
        out_shape=[complex_of] * 4,
        in_specs=[vmem] * (2 + slabs + middle),
        out_specs=[vmem] * 4,
        scratch_shapes=[scratch(slabs), scratch(slabs, 2)],
        compiler_params=params,
        cost_estimate=cost(2),
    )(pole, start, *blocks, *near_links)
    pieces = pl.pallas_call(
        functools.partial(finish, slabs, poles),
        out_shape=[jax.ShapeDtypeStruct((2, 2, order // poles, order), f32)] * poles,
        in_specs=[vmem] * (6 + 2 * slabs),
        out_specs=[vmem] * poles,
        scratch_shapes=[
            scratch(slabs),
            scratch(slabs, 2),
            scratch(middle + 1, 2),
            scratch(middle + 1, 2),
            scratch(middle, 2),
            scratch(middle, 2),
            scratch(2, 2),
        ],
        compiler_params=params,
        cost_estimate=cost(2),
    )(pole, start, *second, *blocks, *links)
    total = pieces[0]
    for k in range(1, poles):
        total = total + lax.ppermute(pieces[k], ("pole", "sub"), [(i, i ^ k) for i in range(poles)])
    return total[0][None], total[1][None]


def solution(mesh):
    in_specs = (
        P(("groups", "slab"), None, None, None),
        P(("groups", "slab"), None, None, None),
        P(("pole", "sub")),
        P(("pole", "sub")),
        P(("pole", "sub"), None),
    )
    out_specs = (
        P(("groups", "slab"), None, ("pole", "sub"), None),
        P(("groups", "slab"), None, ("pole", "sub"), None),
    )
    body = functools.partial(shards, mesh.shape["slab"], mesh.shape["pole"] * mesh.shape["sub"])
    return jax.shard_map(body, mesh=mesh, in_specs=in_specs, out_specs=out_specs, check_vma=False)
```

time: 39.9 us -> 37.4 us (0.937)
  starting transfers between devices: 12 us -> 8.55 us
  waiting for transfers between devices: 3.76 us -> 7.09 us
  Pallas kernels: 20.3 us -> 18 us
    ppermute x6 -> x2, starting transfers between devices: 10.1 us -> 3.54 us  [swap(): return lax.ppermute(value, 'slab', [(i, i ^ k) for i in range(slabs)])]
    ppermute x0 -> x4, starting transfers between devices: none -> 2.94 us  [the longest x2 2.87 us: far_swap(): return lax.ppermute(value, ('slab', 'sub'), pairs)]
    ppermute x0 -> x4, waiting for transfers between devices: none -> 2.72 us  [the longest x2 2.71 us: far_swap(): return lax.ppermute(value, ('slab', 'sub'), pairs)]
    pallas_call x1, Pallas kernels: 7.86 us -> 7.02 us  [shards(): pl.pallas_call(functools.partial(finish, slabs, poles), out_shape=[jax.Sh...]
    ppermute x3, waiting for transfers between devices: 3.74 us -> 4.37 us  [shards(): lax.ppermute(pieces[k], ('pole', 'sub'), [(i, i ^ k) for i in range(poles)])]
    pallas_call x1, Pallas kernels: 5.05 us -> 4.42 us  [shards(): pl.pallas_call(functools.partial(start_chain, slabs), out_shape=complex_o...]
    pallas_call x1 -> x2, Pallas kernels: 0.64 us -> 0.18 us  [the longest x1 0.1 us: shards(): pl.pallas_call(prepare, out_shape=square_of, in_specs=[vmem], out_specs=v...]
  transfers between devices with their start and end apart: 9 -> 9, of which waited for: 2 -> 3; matrix products, arithmetic and copies ran while one was open for 0% -> 0% of each run, Pallas kernels for 30% -> 29%
where the time goes in v3:
time: 37.4 us; the launch traced here: 37.2 us
  Pallas kernels  18 us (48%)
  starting transfers between devices  8.55 us (23%)
  waiting for transfers between devices  7.09 us (19%)
  between operations  2.03 us (5%)
  local copies, waits for them, and re-layouts  1.54 us (4%)
    pallas_call x1, Pallas kernels, shards(): pl.pallas_call(functools.partial(finish, slabs, poles), out_shape=[jax.Sh...  7.02 us
    pallas_call x1, Pallas kernels, shards(): pl.pallas_call(functools.partial(advance, slabs), out_shape=[complex_of]...  6.39 us
    pallas_call x1, Pallas kernels, shards(): pl.pallas_call(functools.partial(start_chain, slabs), out_shape=complex_o...  4.42 us
    ppermute x3, waiting for transfers between devices, shards(): lax.ppermute(pieces[k], ('pole', 'sub'), [(i, i ^ k) for i in range(poles)])  4.37 us
    ppermute x2, starting transfers between devices, swap(): return lax.ppermute(value, 'slab', [(i, i ^ k) for i in range(slabs)])  3.54 us
    ppermute x2, starting transfers between devices, far_swap(): return lax.ppermute(value, ('slab', 'sub'), pairs)  2.87 us
    ppermute x2, waiting for transfers between devices, far_swap(): return lax.ppermute(value, ('slab', 'sub'), pairs)  2.71 us
    ppermute x3, starting transfers between devices, shards(): lax.ppermute(pieces[k], ('pole', 'sub'), [(i, i ^ k) for i in range(poles)])  2.07 us
  transfers between devices with their start and end apart: 9, of which 3 were waited for; matrix products, arithmetic and copies ran while one was open for 0% of the time, Pallas kernels for 29%

profile of v3, /device:TPU:0, one launch (start us, length us, event | category | flops | bytes accessed | tf_op | source)
XLA Modules:
  0.0 37.2 jit_solution(9584405759763193416)
XLA Ops:
  0.6 0.9 %copy-done = f32[1,2,128,128]{3,2,1,0:T(8,128)S(1)} copy-done((f32[1,2,128,128]{3,2,1,0:T(8,128)S(1)}, f32[1,2,128,128]{3,2,1,0:T(8,128)}, u32[]{:S(2)}) %copy-start) | copy-done | bytes 131096
  1.5 0.1 shard_map.69.refs_0_
  1.6 3.1 %collective-permute-start = (f32[128,128]{1,0:T(8,128)S(1)}, f32[128,128]{1,0:T(8,128)S(1)}, u32[]{:S(2)}, u32[]{:S(2)}) collective-permute-start(f32[128,128]{1,0:T(8,128)S(1)} %shard_map.69.refs_0_), channel_id=1, source_target_pairs={{0,4},{4,0},{8,12},{12,8},{1,5},{5,1},{9,13},{13,9},{2,6},{6,2},{1... | collective-permute-start | bytes 196616 | tf_op jit(solution)/shard_map/ppermute | solution.py:391
  4.7 2.6 %collective-permute-start.1 = (f32[128,128]{1,0:T(8,128)S(1)}, f32[128,128]{1,0:T(8,128)S(1)}, u32[]{:S(2)}, u32[]{:S(2)}) collective-permute-start(f32[128,128]{1,0:T(8,128)S(1)} %shard_map.69.refs_0_), channel_id=1, source_target_pairs={{0,8},{1,13},{4,12},{5,9},{8,0},{9,5},{12,4},{13,1},{2,10},{3,15},... | collective-permute-start | bytes 196616 | tf_op jit(solution)/shard_map/ppermute | solution.py:406
  7.3 0.4 %collective-permute-start.3 = (f32[1,2,128,128]{3,2,1,0:T(8,128)S(1)}, f32[1,2,128,128]{3,2,1,0:T(8,128)S(1)}, u32[]{:S(2)}, u32[]{:S(2)}) collective-permute-start(f32[1,2,128,128]{3,2,1,0:T(8,128)S(1)} %copy-done.2), channel_id=1, source_target_pairs={{0,4},{4,0},{8,12},{12,8},{1,5},{5,1},{9,13},{13,9},{2,6},{6,2},{1... | collective-permute-start | bytes 393224 | tf_op jit(solution)/shard_map/ppermute | solution.py:391
  7.8 0.3 collective-permute-start.4
  8.7 0.0 copy-start.1
  9.4 0.1 shard_map.68.pole
  9.5 4.4 %shard_map.70.start = f32[2,128,128]{2,1,0:T(8,128)S(1)} custom-call(f32[8,128]{1,0:T(8,128)S(1)} %shard_map.68.pole, f32[128,128]{1,0:T(8,128)S(1)} %shard_map.69.refs_0_, f32[128,128]{1,0:T(8,128)S(1)} %collective-permute-done.refs_1_), custom_call_target="tpu_custom_call" | custom-call | flops 5000000000 | bytes 2000000 | tf_op jit(solution)/shard_map/pallas_call | solution.py:412
  13.9 0.1 collective-permute-start.2
  14.0 2.7 %collective-permute-done.4.refs_6_ = f32[1,2,128,128]{3,2,1,0:T(8,128)S(1)} collective-permute-done((f32[1,2,128,128]{3,2,1,0:T(8,128)S(1)}, f32[1,2,128,128]{3,2,1,0:T(8,128)S(1)}, u32[]{:S(2)}, u32[]{:S(2)}) %collective-permute-start.4) | collective-permute-done | bytes 131104 | tf_op jit(solution)/shard_map/ppermute | solution.py:406
  16.7 0.0 collective-permute-start.5
  16.7 0.0 collective-permute-done.2.refs_3_
  16.7 0.0 collective-permute-done.3.refs_5_
  16.7 6.4 %shard_map.71 = (f32[2,128,128]{2,1,0:T(8,128)S(1)}, f32[2,128,128]{2,1,0:T(8,128)S(1)}, f32[2,128,128]{2,1,0:T(8,128)S(1)}, f32[2,128,128]{2,1,0:T(8,128)S(1)}) custom-call(f32[8,128]{1,0:T(8,128)S(1)} %shard_map.68.pole, f32[2,128,128]{2,1,0:T(8,128)S(1)} %shard_map.70.start, f32[128,128]{1,0:T(8,128)S(1)} %shard_map.69.refs_0_, ...), custom_call_target="tpu_custom_call" | custom-call | flops 5000000000 | bytes 2000000 | tf_op jit(solution)/shard_map/pallas_call | solution.py:430
  23.1 0.0 collective-permute-done.5.refs_7_
  23.1 7.0 %shard_map.72 = (f32[2,2,32,128]{3,2,1,0:T(8,128)S(1)}, f32[2,2,32,128]{3,2,1,0:T(8,128)S(1)}, f32[2,2,32,128]{3,2,1,0:T(8,128)S(1)}, f32[2,2,32,128]{3,2,1,0:T(8,128)S(1)}) custom-call(f32[8,128]{1,0:T(8,128)S(1)} %shard_map.68.pole, f32[2,128,128]{2,1,0:T(8,128)S(1)} %shard_map.70.start, f32[2,128,128]{2,1,0:T(8,128)S(1)} %get-tuple-element.13.second, ...), custom_call_target="tpu_custom_call" | custom-call | flops 5000000000 | bytes 2000000 | tf_op jit(solution)/shard_map/pallas_call | solution.py:439
  30.1 0.6 %collective-permute-start.6 = (f32[2,2,32,128]{3,2,1,0:T(8,128)S(1)}, f32[2,2,32,128]{3,2,1,0:T(8,128)S(1)}, u32[]{:S(2)}, u32[]{:S(2)}) collective-permute-start(f32[2,2,32,128]{3,2,1,0:T(8,128)S(1)} %get-tuple-element.19), channel_id=1, source_target_pairs={{0,1},{1,0},{2,3},{3,2},{4,5},{5,4},{6,7},{7,6},{8,9},{9,8},{10,11... | collective-permute-start | bytes 196616 | tf_op jit(solution)/shard_map/ppermute | solution.py:458
  30.7 1.5 %collective-permute-start.7 = (f32[2,2,32,128]{3,2,1,0:T(8,128)S(1)}, f32[2,2,32,128]{3,2,1,0:T(8,128)S(1)}, u32[]{:S(2)}, u32[]{:S(2)}) collective-permute-start(f32[2,2,32,128]{3,2,1,0:T(8,128)S(1)} %get-tuple-element.20), channel_id=1, source_target_pairs={{0,2},{1,3},{2,0},{3,1},{4,6},{5,7},{6,4},{7,5},{8,10},{9,11},{10,... | collective-permute-start | bytes 196616 | tf_op jit(solution)/shard_map/ppermute | solution.py:458
  32.2 0.0 collective-permute-start.8
  32.2 0.0 collective-permute-done.6
  32.2 2.8 %collective-permute-done.7 = f32[2,2,32,128]{3,2,1,0:T(8,128)S(1)} collective-permute-done((f32[2,2,32,128]{3,2,1,0:T(8,128)S(1)}, f32[2,2,32,128]{3,2,1,0:T(8,128)S(1)}, u32[]{:S(2)}, u32[]{:S(2)}) %collective-permute-start.7) | collective-permute-done | bytes 65568 | tf_op jit(solution)/shard_map/ppermute | solution.py:458
  35.0 1.6 %collective-permute-done.8 = f32[2,2,32,128]{3,2,1,0:T(8,128)S(1)} collective-permute-done((f32[2,2,32,128]{3,2,1,0:T(8,128)S(1)}, f32[2,2,32,128]{3,2,1,0:T(8,128)S(1)}, u32[]{:S(2)}, u32[]{:S(2)}) %collective-permute-start.8) | collective-permute-done | bytes 65568 | tf_op jit(solution)/shard_map/ppermute | solution.py:458
  36.6 0.6 %fusion = (f32[1,2,32,128]{3,2,1,0:T(8,128)}, f32[1,2,32,128]{3,2,1,0:T(8,128)}) fusion(f32[2,2,32,128]{3,2,1,0:T(8,128)S(1)} %add_add_fusion), kind=kLoop, calls=%fused_computation.1 | loop fusion | bytes 131072 | tf_op jit(solution)/shard_map/slice | solution.py:459
  (7 shorter events, 0.0 us)
Async XLA Ops:
  0.6 0.9 %copy-start = (f32[1,2,128,128]{3,2,1,0:T(8,128)S(1)}, f32[1,2,128,128]{3,2,1,0:T(8,128)}, u32[]{:S(2)}) copy-start(f32[1,2,128,128]{3,2,1,0:T(8,128)} %onsite.1) | copy-start | bytes 393220
  1.5 5.8 %copy-start.2 = (f32[1,2,128,128]{3,2,1,0:T(8,128)S(1)}, f32[1,2,128,128]{3,2,1,0:T(8,128)}, u32[]{:S(2)}) copy-start(f32[1,2,128,128]{3,2,1,0:T(8,128)} %refs_4_.3) | copy-start | bytes 393220
  1.6 7.8 %collective-permute-start = (f32[128,128]{1,0:T(8,128)S(1)}, f32[128,128]{1,0:T(8,128)S(1)}, u32[]{:S(2)}, u32[]{:S(2)}) collective-permute-start(f32[128,128]{1,0:T(8,128)S(1)} %shard_map.69.refs_0_), channel_id=1, source_target_pairs={{0,4},{4,0},{8,12},{12,8},{1,5},{5,1},{9,13},{13,9},{2,6},{6,2},{1... | collective-permute-start | bytes 196616 | tf_op jit(solution)/shard_map/ppermute | solution.py:391
  4.7 9.2 %collective-permute-start.1 = (f32[128,128]{1,0:T(8,128)S(1)}, f32[128,128]{1,0:T(8,128)S(1)}, u32[]{:S(2)}, u32[]{:S(2)}) collective-permute-start(f32[128,128]{1,0:T(8,128)S(1)} %shard_map.69.refs_0_), channel_id=1, source_target_pairs={{0,8},{1,13},{4,12},{5,9},{8,0},{9,5},{12,4},{13,1},{2,10},{3,15},... | collective-permute-start | bytes 196616 | tf_op jit(solution)/shard_map/ppermute | solution.py:406
  7.3 9.4 %collective-permute-start.3 = (f32[1,2,128,128]{3,2,1,0:T(8,128)S(1)}, f32[1,2,128,128]{3,2,1,0:T(8,128)S(1)}, u32[]{:S(2)}, u32[]{:S(2)}) collective-permute-start(f32[1,2,128,128]{3,2,1,0:T(8,128)S(1)} %copy-done.2), channel_id=1, source_target_pairs={{0,4},{4,0},{8,12},{12,8},{1,5},{5,1},{9,13},{13,9},{2,6},{6,2},{1... | collective-permute-start | bytes 393224 | tf_op jit(solution)/shard_map/ppermute | solution.py:391
  7.8 8.9 %collective-permute-start.4 = (f32[1,2,128,128]{3,2,1,0:T(8,128)S(1)}, f32[1,2,128,128]{3,2,1,0:T(8,128)S(1)}, u32[]{:S(2)}, u32[]{:S(2)}) collective-permute-start(f32[1,2,128,128]{3,2,1,0:T(8,128)S(1)} %copy-done.2), channel_id=1, source_target_pairs={{0,8},{1,13},{4,12},{5,9},{8,0},{9,5},{12,4},{13,1},{2,10},{3,15},... | collective-permute-start | bytes 393224 | tf_op jit(solution)/shard_map/ppermute | solution.py:406
  8.7 0.7 %copy-start.1 = (f32[1,2]{1,0:T(1,128)S(1)}, f32[1,2]{1,0:T(1,128)}, u32[]{:S(2)}) copy-start(f32[1,2]{1,0:T(1,128)} %pole_weight.1) | copy-start | bytes 28
  13.9 2.8 %collective-permute-start.2 = (f32[128,128]{1,0:T(8,128)S(1)}, f32[128,128]{1,0:T(8,128)S(1)}, u32[]{:S(2)}, u32[]{:S(2)}) collective-permute-start(f32[128,128]{1,0:T(8,128)S(1)} %collective-permute-done.1.refs_2_), channel_id=1, source_target_pairs={{0,1},{1,0},{2,3},{3,2},{4,5},{5,4},{6,7},{7,6},{8,9},{9,8},{10,11... | collective-permute-start | bytes 196616 | tf_op jit(solution)/shard_map/ppermute | solution.py:426
  16.7 6.4 %collective-permute-start.5 = (f32[1,2,128,128]{3,2,1,0:T(8,128)S(1)}, f32[1,2,128,128]{3,2,1,0:T(8,128)S(1)}, u32[]{:S(2)}, u32[]{:S(2)}) collective-permute-start(f32[1,2,128,128]{3,2,1,0:T(8,128)S(1)} %collective-permute-done.4.refs_6_), channel_id=1, source_target_pairs={{0,1},{1,0},{2,3},{3,2},{4,5},{5,4},{6,7},{7,6},{8,9},{9,8},{10,11... | collective-permute-start | bytes 393224 | tf_op jit(solution)/shard_map/ppermute | solution.py:426
  30.1 2.1 %collective-permute-start.6 = (f32[2,2,32,128]{3,2,1,0:T(8,128)S(1)}, f32[2,2,32,128]{3,2,1,0:T(8,128)S(1)}, u32[]{:S(2)}, u32[]{:S(2)}) collective-permute-start(f32[2,2,32,128]{3,2,1,0:T(8,128)S(1)} %get-tuple-element.19), channel_id=1, source_target_pairs={{0,1},{1,0},{2,3},{3,2},{4,5},{5,4},{6,7},{7,6},{8,9},{9,8},{10,11... | collective-permute-start | bytes 196616 | tf_op jit(solution)/shard_map/ppermute | solution.py:458
  30.7 4.3 %collective-permute-start.7 = (f32[2,2,32,128]{3,2,1,0:T(8,128)S(1)}, f32[2,2,32,128]{3,2,1,0:T(8,128)S(1)}, u32[]{:S(2)}, u32[]{:S(2)}) collective-permute-start(f32[2,2,32,128]{3,2,1,0:T(8,128)S(1)} %get-tuple-element.20), channel_id=1, source_target_pairs={{0,2},{1,3},{2,0},{3,1},{4,6},{5,7},{6,4},{7,5},{8,10},{9,11},{10,... | collective-permute-start | bytes 196616 | tf_op jit(solution)/shard_map/ppermute | solution.py:458
  32.2 4.4 %collective-permute-start.8 = (f32[2,2,32,128]{3,2,1,0:T(8,128)S(1)}, f32[2,2,32,128]{3,2,1,0:T(8,128)S(1)}, u32[]{:S(2)}, u32[]{:S(2)}) collective-permute-start(f32[2,2,32,128]{3,2,1,0:T(8,128)S(1)} %get-tuple-element.21), channel_id=1, source_target_pairs={{0,3},{1,2},{2,1},{3,0},{4,7},{5,6},{6,5},{7,4},{8,11},{9,10},{10,... | collective-permute-start | bytes 196616 | tf_op jit(solution)/shard_map/ppermute | solution.py:458

commit v4 on v3

--- a/solution.py
+++ b/solution.py
@@ -10,7 +10,7 @@
 ROWS = 8
 PANEL = 2 * ROWS
 f32, bf16 = jnp.float32, jnp.bfloat16
-PARTS = ((0, 0), (0, 1), (1, 0), (1, 1), (0, 2), (2, 0))
+PARTS = ((0, 0), (1, 0), (0, 1), (1, 1), (0, 2), (2, 0))
 
 
 def row_of(tile, k):
@@ -34,9 +34,9 @@
     return a[0] * b[0] - a[1] * b[1], a[0] * b[1] + a[1] * b[0]
 
 
-def sweep_double(tiles, first, lane, subl):
+def sweep_double(tiles, columns, first, lane, subl):
     tiles = list(tiles)
-    columns = [[(lane_of(xr, first + j), lane_of(xi, first + j)) for j in range(ROWS)] for xr, xi in tiles]
+    columns = [list(cols) for cols in columns]
     for k in range(0, ROWS, 2):
         for s, cols in enumerate(columns):
 
@@ -68,9 +68,9 @@
     return tiles
 
 
-def sweep_single(tiles, first, lane, subl):
+def sweep_single(tiles, columns, first, lane, subl):
     tiles = list(tiles)
-    columns = [[(lane_of(xr, first + j), lane_of(xi, first + j)) for j in range(ROWS)] for xr, xi in tiles]
+    columns = [list(cols) for cols in columns]
     for k in range(ROWS):
         in_row, in_lane = (subl == k).astype(f32), (lane == first + k).astype(f32)
         for s, cols in enumerate(columns):
@@ -89,19 +89,30 @@
     return tiles
 
 
-def follow(tile, swept, first, inside):
-    ar, ai = tile
-    nr, ni = jnp.where(inside, 0.0, ar), jnp.where(inside, 0.0, ai)
+def spread(tiles, first):
+    return [
+        [(lane_of(xr, first + k), lane_of(xi, first + k)) for k in range(ROWS)] for xr, xi in tiles
+    ]
+
+
+def follow(tile, columns, swept, inside):
+    nr, ni = jnp.where(inside, 0.0, tile[0]), jnp.where(inside, 0.0, tile[1])
     pr = pi = None
-    for k in range(ROWS):
-        cr, ci = lane_of(ar, first + k), lane_of(ai, first + k)
-        ur, ui = row_of(swept[0], k), row_of(swept[1], k)
-        tr, ti = cr * ur - ci * ui, cr * ui + ci * ur
+    for k, column in enumerate(columns):
+        tr, ti = complex_times(column, (row_of(swept[0], k), row_of(swept[1], k)))
         if k % 2 == 0:
             nr, ni = nr - tr, ni - ti
         else:
             pr, pi = (tr, ti) if pr is None else (pr + tr, pi + ti)
     return nr - pr, ni - pi
+
+
+def follow_all(tiles, columns, swept, inside, after=None):
+    if after is None or len(tiles) > 1:
+        masks = [inside] * len(tiles)
+    else:
+        masks = [inside & (tile[1] == tile[1]) for tile in after]
+    return [follow(*args) for args in zip(tiles, columns, swept, masks)]
 
 
 def split(x):
@@ -113,17 +124,18 @@
 
 
 def multiply(left, right, columns):
-    lhs = jnp.concatenate([part for a, _ in PARTS for part in (left[0][a], left[1][a])], axis=1)
+    rows = left[0][0].shape[0]
+    lhs = jnp.concatenate(
+        [jnp.concatenate((left[0][a], left[1][a]), axis=0) for a, _ in PARTS], axis=1
+    )
     rhs = jnp.concatenate(
-        [
-            jnp.concatenate(pair, axis=1)
-            for _, b in PARTS
-            for pair in ((right[0][b], right[1][b]), (-right[1][b], right[0][b]))
-        ],
-        axis=0,
+        [jnp.concatenate((right[0][b], right[1][b]), axis=1) for _, b in PARTS], axis=0
     )
     whole = lax.dot_general(lhs, rhs, (((1,), (0,)), ((), ())), preferred_element_type=f32)
-    return whole[:, :columns], whole[:, columns:]
+    return (
+        whole[:rows, :columns] - whole[rows:, columns:],
+        whole[:rows, columns:] + whole[rows:, :columns],
+    )
 
 
 def times(left, right):
@@ -147,7 +159,7 @@
     return [(real[ROWS * t : ROWS * t + ROWS], imag[ROWS * t : ROWS * t + ROWS]) for t in range(len(tiles))]
 
 
-def invert(systems):
+def invert(systems, asides):
     order = systems[0][0][0].shape[1]
     count, panels = order // ROWS, order // PANEL
     lane = lax.broadcasted_iota(jnp.int32, (ROWS, order), 1)
@@ -159,12 +171,24 @@
         in_a = (lane >= ROWS * a) & (lane < ROWS * a + ROWS)
         in_b = (lane >= ROWS * b) & (lane < ROWS * b + ROWS)
         soon = [] if place == panels - 1 else [b + 1, b + 2]
-        first = sweep([tiles[a] for tiles in systems], ROWS * a, lane, subl)
-        second = [follow(tiles[b], x, ROWS * a, in_a) for tiles, x in zip(systems, first)]
-        ahead = [[follow(tiles[i], x, ROWS * a, in_a) for i in soon] for tiles, x in zip(systems, first)]
-        second = sweep(second, ROWS * b, lane, subl)
-        ahead = [[follow(tile, x, ROWS * b, in_b) for tile in pair] for pair, x in zip(ahead, second)]
-        first = [follow(tile, x, ROWS * b, in_b) for tile, x in zip(first, second)]
+        nexts = [[tiles[i] for tiles in systems] for i in soon]
+        second = [tiles[b] for tiles in systems]
+        if place == 0:
+            columns = spread([tiles[a] for tiles in systems], ROWS * a)
+        second_columns = spread(second, ROWS * a)
+        next_columns = [spread(tiles, ROWS * a) for tiles in nexts]
+        first = sweep([tiles[a] for tiles in systems], columns, ROWS * a, lane, subl)
+        second = follow_all(second, second_columns, first, in_a)
+        columns = spread(second, ROWS * b)
+        nexts = [follow_all(tiles, cols, first, in_a, second) for tiles, cols in zip(nexts, next_columns)]
+        next_columns = [spread(tiles, ROWS * b) for tiles in nexts]
+        first_columns = spread(first, ROWS * b)
+        second = sweep(second, columns, ROWS * b, lane, subl)
+        for i, cols in enumerate(next_columns):
+            nexts[i] = follow_all(nexts[i], cols, second, in_b, nexts[0] if i else None)
+            if i == 0:
+                columns = spread(nexts[0], ROWS * (b + 1))
+        first = follow_all(first, first_columns, second, in_b, nexts[0] if nexts else None)
         rest = [i for i in range(count) if i not in (a, b, *soon)]
         rest.sort(key=lambda i: (i - b) % count)
         for s, tiles in enumerate(systems):
@@ -175,8 +199,10 @@
                     jnp.where(in_a | in_b, 0.0, tiles[i][1]) - di,
                 )
             tiles[a], tiles[b] = first[s], second[s]
-            for i, tile in zip(soon, ahead[s]):
-                tiles[i] = tile
+            for i, tile in zip(soon, nexts):
+                tiles[i] = tile[s]
+        if place < len(asides):
+            asides[place]()
     return systems
 
 
@@ -189,8 +215,8 @@
     return tuple(jnp.concatenate(part, axis=0) for part in zip(*tiles))
 
 
-def inverses_of(*values):
-    return [from_tiles(tiles) for tiles in invert([to_tiles(value) for value in values])]
+def inverses_of(*values, asides=()):
+    return [from_tiles(tiles) for tiles in invert([to_tiles(value) for value in values], asides)]
 
 
 def adjoint(a):
@@ -353,13 +379,31 @@
     inverse = get(own, middle - 1)
     taken, out, back = reduced(True, middle, inverse)
     steps = middle - 1 - jnp.where(me < middle, me, slabs - 1 - me)
-    found = inverse, out, times(back, inverse)
+    pivot = minus(other_pivot(middle - 1), taken)
     if middle == 2:
-        further = wider(1, found)
-        found = jax.tree.map(lambda new, old: jnp.where(steps > 0, new, old), further, found)
+        made = {}
+
+        def aside(name, make):
+            return lambda: made.update({name: make()})
+
+        near_out, near_back = get(outward, 1), get(inward, 1)
+        asides = [
+            aside("back", lambda: times(back, inverse)),
+            aside("half", lambda: times(near_out, inverse)),
+            aside("further_out", lambda: times(near_out, out)),
+            aside("base", lambda: plus(get(own, 0), times(made["half"], near_back))),
+            aside("further_back", lambda: times(made["back"], near_back)),
+        ]
+        (green,) = inverses_of(pivot, asides=asides)
+        found = jax.tree.map(
+            lambda new, old: jnp.where(steps > 0, new, old),
+            (made["base"], made["further_out"], made["further_back"]),
+            (inverse, out, made["back"]),
+        )
     else:
+        found = inverse, out, times(back, inverse)
         found = lax.fori_loop(0, steps, lambda step, found: wider(middle - 1 - step, found), found)
-    (green,) = inverses_of(minus(other_pivot(middle - 1), taken))
+        (green,) = inverses_of(pivot)
     gr, gi = plus(found[0], times(times(found[1], green), found[2]))
     gr_t, gi_t = gr.T, gi.T
     even, odd = (0.5 * (gr + gr_t), 0.5 * (gi + gi_t)), (0.5 * (gr_t - gr), 0.5 * (gi_t - gi))
@@ -419,14 +463,14 @@
         cost_estimate=cost(2),
     )(pole, *near_blocks)
 
-    def both(values):
+    def both(values, after):
         pairs = []
         for value in values:
-            mine, _ = lax.optimization_barrier((value, start))
+            mine, _ = lax.optimization_barrier((value, after))
             pairs += [value, lax.ppermute(mine, "sub", [(0, 1), (1, 0)])]
         return pairs
 
-    blocks, links = near_blocks + both(far_blocks), near_links + both(far_links)
+    blocks = near_blocks + both(far_blocks, start)
     second = pl.pallas_call(
         functools.partial(advance, slabs),
         out_shape=[complex_of] * 4,
@@ -434,8 +478,9 @@
         out_specs=[vmem] * 4,
         scratch_shapes=[scratch(slabs), scratch(slabs, 2)],
         compiler_params=params,
-        cost_estimate=cost(2),
+        cost_estimate=pl.CostEstimate(flops=1000, bytes_accessed=1000, transcendentals=0),
     )(pole, start, *blocks, *near_links)
+    links = near_links + both(far_links, second[0])
     pieces = pl.pallas_call(
         functools.partial(finish, slabs, poles),
         out_shape=[jax.ShapeDtypeStruct((2, 2, order // poles, order), f32)] * poles,

time: 37.4 us -> 36.1 us (0.965)
  Pallas kernels: 18 us -> 16.7 us
    ppermute x2, waiting for transfers between devices: 2.71 us -> 0.01 us  [far_swap(): return lax.ppermute(value, ('slab', 'sub'), pairs)]
    ppermute x2, waiting for transfers between devices: 0.01 us -> 2.58 us  [both(): pairs += [value, lax.ppermute(mine, 'sub', [(0, 1), (1, 0)])]]
    pallas_call x1, Pallas kernels: 7.02 us -> 6.09 us  [shards(): pl.pallas_call(functools.partial(finish, slabs, poles), out_shape=[jax.Sh...]
    ppermute x2, waiting for transfers between devices: 0.01 us -> 0.82 us  [swap(): return lax.ppermute(value, 'slab', [(i, i ^ k) for i in range(slabs)])]
    ppermute x3, waiting for transfers between devices: 4.37 us -> 3.94 us  [shards(): lax.ppermute(pieces[k], ('pole', 'sub'), [(i, i ^ k) for i in range(poles)])]
  transfers between devices with their start and end apart: 9 -> 9, of which waited for: 3 -> 5; matrix products, arithmetic and copies ran while one was open for 0% -> 0% of each run, Pallas kernels for 29% -> 29%
where the time goes in v4:
time: 36.1 us; the launch traced here: 35.9 us
  Pallas kernels  16.7 us (46%)
  starting transfers between devices  8.2 us (23%)
  waiting for transfers between devices  7.34 us (20%)
  between operations  2.04 us (6%)
  local copies, waits for them, and re-layouts  1.57 us (4%)
    pallas_call x1, Pallas kernels, shards(): pl.pallas_call(functools.partial(advance, slabs), out_shape=[complex_of]...  6.27 us
    pallas_call x1, Pallas kernels, shards(): pl.pallas_call(functools.partial(finish, slabs, poles), out_shape=[jax.Sh...  6.09 us
    pallas_call x1, Pallas kernels, shards(): pl.pallas_call(functools.partial(start_chain, slabs), out_shape=complex_o...  4.18 us
    ppermute x3, waiting for transfers between devices, shards(): lax.ppermute(pieces[k], ('pole', 'sub'), [(i, i ^ k) for i in range(poles)])  3.94 us
    ppermute x2, starting transfers between devices, swap(): return lax.ppermute(value, 'slab', [(i, i ^ k) for i in range(slabs)])  3.54 us
    ppermute x2, starting transfers between devices, far_swap(): return lax.ppermute(value, ('slab', 'sub'), pairs)  2.59 us
    ppermute x2, waiting for transfers between devices, both(): pairs += [value, lax.ppermute(mine, 'sub', [(0, 1), (1, 0)])]  2.58 us
    ppermute x3, starting transfers between devices, shards(): lax.ppermute(pieces[k], ('pole', 'sub'), [(i, i ^ k) for i in range(poles)])  1.93 us
  transfers between devices with their start and end apart: 9, of which 5 were waited for; matrix products, arithmetic and copies ran while one was open for 0% of the time, Pallas kernels for 29%

profile of v4, /device:TPU:0, one launch (start us, length us, event | category | flops | bytes accessed | tf_op | source)
XLA Modules:
  0.0 35.9 jit_solution(2131379473575563104)
XLA Ops:
  0.6 0.9 %copy-done.1 = f32[1,2,128,128]{3,2,1,0:T(8,128)S(1)} copy-done((f32[1,2,128,128]{3,2,1,0:T(8,128)S(1)}, f32[1,2,128,128]{3,2,1,0:T(8,128)}, u32[]{:S(2)}) %copy-start.1) | copy-done | bytes 131096
  1.6 0.1 shard_map.69.refs_0_
  1.7 3.1 %collective-permute-start = (f32[128,128]{1,0:T(8,128)S(1)}, f32[128,128]{1,0:T(8,128)S(1)}, u32[]{:S(2)}, u32[]{:S(2)}) collective-permute-start(f32[128,128]{1,0:T(8,128)S(1)} %shard_map.69.refs_0_), channel_id=1, source_target_pairs={{0,4},{4,0},{8,12},{12,8},{1,5},{5,1},{9,13},{13,9},{2,6},{6,2},{1... | collective-permute-start | bytes 196616 | tf_op jit(solution)/shard_map/ppermute | solution.py:435
  4.8 2.6 %collective-permute-start.1 = (f32[128,128]{1,0:T(8,128)S(1)}, f32[128,128]{1,0:T(8,128)S(1)}, u32[]{:S(2)}, u32[]{:S(2)}) collective-permute-start(f32[128,128]{1,0:T(8,128)S(1)} %shard_map.69.refs_0_), channel_id=1, source_target_pairs={{0,8},{1,13},{4,12},{5,9},{8,0},{9,5},{12,4},{13,1},{2,10},{3,15},... | collective-permute-start | bytes 196616 | tf_op jit(solution)/shard_map/ppermute | solution.py:450
  7.4 0.4 %collective-permute-start.3 = (f32[1,2,128,128]{3,2,1,0:T(8,128)S(1)}, f32[1,2,128,128]{3,2,1,0:T(8,128)S(1)}, u32[]{:S(2)}, u32[]{:S(2)}) collective-permute-start(f32[1,2,128,128]{3,2,1,0:T(8,128)S(1)} %copy-done), channel_id=1, source_target_pairs={{0,4},{4,0},{8,12},{12,8},{1,5},{5,1},{9,13},{13,9},{2,6},{6,2},{1... | collective-permute-start | bytes 393224 | tf_op jit(solution)/shard_map/ppermute | solution.py:435
  7.8 0.0 collective-permute-start.4
  8.5 0.0 copy-start.2
  9.2 0.1 shard_map.68.pole
  9.2 0.0 collective-permute-done.refs_1_
  9.2 4.2 %shard_map.70.start = f32[2,128,128]{2,1,0:T(8,128)S(1)} custom-call(f32[8,128]{1,0:T(8,128)S(1)} %shard_map.68.pole, f32[128,128]{1,0:T(8,128)S(1)} %shard_map.69.refs_0_, f32[128,128]{1,0:T(8,128)S(1)} %collective-permute-done.refs_1_), custom_call_target="tpu_custom_call" | custom-call | flops 5000000000 | bytes 2000000 | tf_op jit(solution)/shard_map/pallas_call | solution.py:456
  13.4 0.0 collective-permute-done.1.refs_2_
  13.4 0.1 collective-permute-start.2
  13.5 1.2 %collective-permute-done.2.refs_3_ = f32[128,128]{1,0:T(8,128)S(1)} collective-permute-done((f32[128,128]{1,0:T(8,128)S(1)}, f32[128,128]{1,0:T(8,128)S(1)}, u32[]{:S(2)}, u32[]{:S(2)}) %collective-permute-start.2) | collective-permute-done | bytes 65568 | tf_op jit(solution)/shard_map/ppermute | solution.py:470
  14.8 0.8 %collective-permute-done.3.refs_5_ = f32[1,2,128,128]{3,2,1,0:T(8,128)S(1)} collective-permute-done((f32[1,2,128,128]{3,2,1,0:T(8,128)S(1)}, f32[1,2,128,128]{3,2,1,0:T(8,128)S(1)}, u32[]{:S(2)}, u32[]{:S(2)}) %collective-permute-start.3) | collective-permute-done | bytes 131104 | tf_op jit(solution)/shard_map/ppermute | solution.py:435
  15.6 6.3 %shard_map.71 = (f32[2,128,128]{2,1,0:T(8,128)S(1)}, f32[2,128,128]{2,1,0:T(8,128)S(1)}, f32[2,128,128]{2,1,0:T(8,128)S(1)}, f32[2,128,128]{2,1,0:T(8,128)S(1)}) custom-call(f32[8,128]{1,0:T(8,128)S(1)} %shard_map.68.pole, f32[2,128,128]{2,1,0:T(8,128)S(1)} %shard_map.70.start, f32[128,128]{1,0:T(8,128)S(1)} %shard_map.69.refs_0_, ...), custom_call_target="tpu_custom_call" | custom-call | flops 1000 | bytes 1000 | tf_op jit(solution)/shard_map/pallas_call | solution.py:474
  21.9 0.1 collective-permute-start.5
  21.9 1.3 %collective-permute-done.5.refs_7_ = f32[1,2,128,128]{3,2,1,0:T(8,128)S(1)} collective-permute-done((f32[1,2,128,128]{3,2,1,0:T(8,128)S(1)}, f32[1,2,128,128]{3,2,1,0:T(8,128)S(1)}, u32[]{:S(2)}, u32[]{:S(2)}) %collective-permute-start.5) | collective-permute-done | bytes 131104 | tf_op jit(solution)/shard_map/ppermute | solution.py:470
  23.3 6.1 %shard_map.72 = (f32[2,2,32,128]{3,2,1,0:T(8,128)S(1)}, f32[2,2,32,128]{3,2,1,0:T(8,128)S(1)}, f32[2,2,32,128]{3,2,1,0:T(8,128)S(1)}, f32[2,2,32,128]{3,2,1,0:T(8,128)S(1)}) custom-call(f32[8,128]{1,0:T(8,128)S(1)} %shard_map.68.pole, f32[2,128,128]{2,1,0:T(8,128)S(1)} %shard_map.70.start, f32[2,128,128]{2,1,0:T(8,128)S(1)} %get-tuple-element.13.second, ...), custom_call_target="tpu_custom_call" | custom-call | flops 5000000000 | bytes 2000000 | tf_op jit(solution)/shard_map/pallas_call | solution.py:484
  29.4 0.2 collective-permute-start.6
  29.6 1.5 %collective-permute-start.7 = (f32[2,2,32,128]{3,2,1,0:T(8,128)S(1)}, f32[2,2,32,128]{3,2,1,0:T(8,128)S(1)}, u32[]{:S(2)}, u32[]{:S(2)}) collective-permute-start(f32[2,2,32,128]{3,2,1,0:T(8,128)S(1)} %get-tuple-element.20), channel_id=1, source_target_pairs={{0,2},{1,3},{2,0},{3,1},{4,6},{5,7},{6,4},{7,5},{8,10},{9,11},{10,... | collective-permute-start | bytes 196616 | tf_op jit(solution)/shard_map/ppermute | solution.py:503
  31.1 0.2 collective-permute-start.8
  31.3 2.6 %collective-permute-done.7 = f32[2,2,32,128]{3,2,1,0:T(8,128)S(1)} collective-permute-done((f32[2,2,32,128]{3,2,1,0:T(8,128)S(1)}, f32[2,2,32,128]{3,2,1,0:T(8,128)S(1)}, u32[]{:S(2)}, u32[]{:S(2)}) %collective-permute-start.7) | collective-permute-done | bytes 65568 | tf_op jit(solution)/shard_map/ppermute | solution.py:503
  33.9 1.3 %collective-permute-done.8 = f32[2,2,32,128]{3,2,1,0:T(8,128)S(1)} collective-permute-done((f32[2,2,32,128]{3,2,1,0:T(8,128)S(1)}, f32[2,2,32,128]{3,2,1,0:T(8,128)S(1)}, u32[]{:S(2)}, u32[]{:S(2)}) %collective-permute-start.8) | collective-permute-done | bytes 65568 | tf_op jit(solution)/shard_map/ppermute | solution.py:503
  35.3 0.6 %fusion = (f32[1,2,32,128]{3,2,1,0:T(8,128)}, f32[1,2,32,128]{3,2,1,0:T(8,128)}) fusion(f32[2,2,32,128]{3,2,1,0:T(8,128)S(1)} %add_add_fusion), kind=kLoop, calls=%fused_computation.1 | loop fusion | bytes 131072 | tf_op jit(solution)/shard_map/slice | solution.py:504
  (7 shorter events, 0.0 us)
Async XLA Ops:
  0.6 6.7 %copy-start = (f32[1,2,128,128]{3,2,1,0:T(8,128)S(1)}, f32[1,2,128,128]{3,2,1,0:T(8,128)}, u32[]{:S(2)}) copy-start(f32[1,2,128,128]{3,2,1,0:T(8,128)} %refs_4_.3) | copy-start | bytes 393220
  0.6 0.9 %copy-start.1 = (f32[1,2,128,128]{3,2,1,0:T(8,128)S(1)}, f32[1,2,128,128]{3,2,1,0:T(8,128)}, u32[]{:S(2)}) copy-start(f32[1,2,128,128]{3,2,1,0:T(8,128)} %onsite.1) | copy-start | bytes 393220
  1.7 7.5 %collective-permute-start = (f32[128,128]{1,0:T(8,128)S(1)}, f32[128,128]{1,0:T(8,128)S(1)}, u32[]{:S(2)}, u32[]{:S(2)}) collective-permute-start(f32[128,128]{1,0:T(8,128)S(1)} %shard_map.69.refs_0_), channel_id=1, source_target_pairs={{0,4},{4,0},{8,12},{12,8},{1,5},{5,1},{9,13},{13,9},{2,6},{6,2},{1... | collective-permute-start | bytes 196616 | tf_op jit(solution)/shard_map/ppermute | solution.py:435
  4.8 8.6 %collective-permute-start.1 = (f32[128,128]{1,0:T(8,128)S(1)}, f32[128,128]{1,0:T(8,128)S(1)}, u32[]{:S(2)}, u32[]{:S(2)}) collective-permute-start(f32[128,128]{1,0:T(8,128)S(1)} %shard_map.69.refs_0_), channel_id=1, source_target_pairs={{0,8},{1,13},{4,12},{5,9},{8,0},{9,5},{12,4},{13,1},{2,10},{3,15},... | collective-permute-start | bytes 196616 | tf_op jit(solution)/shard_map/ppermute | solution.py:450
  7.4 8.2 %collective-permute-start.3 = (f32[1,2,128,128]{3,2,1,0:T(8,128)S(1)}, f32[1,2,128,128]{3,2,1,0:T(8,128)S(1)}, u32[]{:S(2)}, u32[]{:S(2)}) collective-permute-start(f32[1,2,128,128]{3,2,1,0:T(8,128)S(1)} %copy-done), channel_id=1, source_target_pairs={{0,4},{4,0},{8,12},{12,8},{1,5},{5,1},{9,13},{13,9},{2,6},{6,2},{1... | collective-permute-start | bytes 393224 | tf_op jit(solution)/shard_map/ppermute | solution.py:435
  7.8 14.0 %collective-permute-start.4 = (f32[1,2,128,128]{3,2,1,0:T(8,128)S(1)}, f32[1,2,128,128]{3,2,1,0:T(8,128)S(1)}, u32[]{:S(2)}, u32[]{:S(2)}) collective-permute-start(f32[1,2,128,128]{3,2,1,0:T(8,128)S(1)} %copy-done), channel_id=1, source_target_pairs={{0,8},{1,13},{4,12},{5,9},{8,0},{9,5},{12,4},{13,1},{2,10},{3,15},... | collective-permute-start | bytes 393224 | tf_op jit(solution)/shard_map/ppermute | solution.py:450
  8.5 0.7 %copy-start.2 = (f32[1,2]{1,0:T(1,128)S(1)}, f32[1,2]{1,0:T(1,128)}, u32[]{:S(2)}) copy-start(f32[1,2]{1,0:T(1,128)} %pole_weight.1) | copy-start | bytes 28
  13.4 1.3 %collective-permute-start.2 = (f32[128,128]{1,0:T(8,128)S(1)}, f32[128,128]{1,0:T(8,128)S(1)}, u32[]{:S(2)}, u32[]{:S(2)}) collective-permute-start(f32[128,128]{1,0:T(8,128)S(1)} %collective-permute-done.1.refs_2_), channel_id=1, source_target_pairs={{0,1},{1,0},{2,3},{3,2},{4,5},{5,4},{6,7},{7,6},{8,9},{9,8},{10,11... | collective-permute-start | bytes 196616 | tf_op jit(solution)/shard_map/ppermute | solution.py:470
  21.9 1.4 %collective-permute-start.5 = (f32[1,2,128,128]{3,2,1,0:T(8,128)S(1)}, f32[1,2,128,128]{3,2,1,0:T(8,128)S(1)}, u32[]{:S(2)}, u32[]{:S(2)}) collective-permute-start(f32[1,2,128,128]{3,2,1,0:T(8,128)S(1)} %collective-permute-done.4.refs_6_), channel_id=1, source_target_pairs={{0,1},{1,0},{2,3},{3,2},{4,5},{5,4},{6,7},{7,6},{8,9},{9,8},{10,11... | collective-permute-start | bytes 393224 | tf_op jit(solution)/shard_map/ppermute | solution.py:470
  29.4 1.9 %collective-permute-start.6 = (f32[2,2,32,128]{3,2,1,0:T(8,128)S(1)}, f32[2,2,32,128]{3,2,1,0:T(8,128)S(1)}, u32[]{:S(2)}, u32[]{:S(2)}) collective-permute-start(f32[2,2,32,128]{3,2,1,0:T(8,128)S(1)} %get-tuple-element.19), channel_id=1, source_target_pairs={{0,1},{1,0},{2,3},{3,2},{4,5},{5,4},{6,7},{7,6},{8,9},{9,8},{10,11... | collective-permute-start | bytes 196616 | tf_op jit(solution)/shard_map/ppermute | solution.py:503
  29.6 4.4 %collective-permute-start.7 = (f32[2,2,32,128]{3,2,1,0:T(8,128)S(1)}, f32[2,2,32,128]{3,2,1,0:T(8,128)S(1)}, u32[]{:S(2)}, u32[]{:S(2)}) collective-permute-start(f32[2,2,32,128]{3,2,1,0:T(8,128)S(1)} %get-tuple-element.20), channel_id=1, source_target_pairs={{0,2},{1,3},{2,0},{3,1},{4,6},{5,7},{6,4},{7,5},{8,10},{9,11},{10,... | collective-permute-start | bytes 196616 | tf_op jit(solution)/shard_map/ppermute | solution.py:503
  31.1 4.1 %collective-permute-start.8 = (f32[2,2,32,128]{3,2,1,0:T(8,128)S(1)}, f32[2,2,32,128]{3,2,1,0:T(8,128)S(1)}, u32[]{:S(2)}, u32[]{:S(2)}) collective-permute-start(f32[2,2,32,128]{3,2,1,0:T(8,128)S(1)} %get-tuple-element.21), channel_id=1, source_target_pairs={{0,3},{1,2},{2,1},{3,0},{4,7},{5,6},{6,5},{7,4},{8,11},{9,10},{10,... | collective-permute-start | bytes 196616 | tf_op jit(solution)/shard_map/ppermute | solution.py:503

commit v5 on v4

--- a/solution.py
+++ b/solution.py
@@ -53,12 +53,12 @@
                 minus(complex_times(one, d), complex_times(two, c)),
                 minus(complex_times(two, a), complex_times(one, b)),
             )
-            for j in range(k + 2, min(k + 4, ROWS)):
+            for j in range(k + 2, min(k + 3, ROWS)):
                 upper, lower = entries(cols[j])
                 taken = plus(complex_times(one, upper), complex_times(two, lower))
                 cols[j] = minus(cols[j], complex_times(taken, over))
             one, two = complex_times(one, over), complex_times(two, over)
-            for j in range(k + 4, ROWS):
+            for j in range(k + 3, ROWS):
                 upper, lower = entries(cols[j])
                 cols[j] = minus(cols[j], plus(complex_times(one, upper), complex_times(two, lower)))
             upper, lower = entries(tiles[s])
@@ -270,6 +270,10 @@
     pole[3:4, :] = jnp.broadcast_to(pole_weight[:, 1:2], (1, width))
 
 
+def halve(coupling, half):
+    half[...] = coupling[0, lax.axis_index("sub")]
+
+
 def scalars_of(pole):
     return [pole[row : row + 1, :] for row in range(4)]
 
@@ -314,6 +318,13 @@
         target[me ^ k] = ref[...] if ref.ndim == target.ndim - 1 else ref[0]
 
 
+def fill_links(me, target, own, halves):
+    core = lax.axis_index("sub")
+    target[me] = own[0]
+    for i, ref in enumerate(halves):
+        target[me ^ (1 + i // 2), core if i % 2 == 0 else 1 - core] = ref[...]
+
+
 def fill_far(me, target, refs):
     middle, core = target.shape[0] // 2, lax.axis_index("sub")
     for i, ref in enumerate(refs):
@@ -321,35 +332,47 @@
         target[me ^ mask] = ref[...] if ref.ndim == target.ndim - 1 else ref[0]
 
 
-def advance(slabs, pole, start, *refs):
+def couple(slabs, pole, start, *refs):
     middle = slabs // 2
-    block_refs, link_refs, refs = refs[:slabs], refs[slabs : slabs + middle], refs[slabs + middle :]
-    here, there, outward, inward, blocks, links = refs
+    block_refs, own, refs = refs[:middle], refs[middle], refs[middle + 1 :]
+    halves, refs = refs[: 2 * middle - 2], refs[2 * middle - 2 :]
+    pivot, outward, inward, blocks, links = refs
     me = lax.axis_index("slab")
     zr, zi, _, _ = scalars_of(pole)
-    fill_near(me, blocks, block_refs[:middle])
-    fill_far(me, blocks, block_refs[middle:])
-    fill_near(me, links, link_refs)
+    fill_near(me, blocks, block_refs)
+    fill_links(me, links, own, halves)
     block, reduced = chain(slabs, me, blocks, links, zr, zi)
     inverse = get(start)
     taken, out, back = reduced(True, 1, inverse)
+    put(pivot, minus(block(True, 1), taken))
     put(outward, out)
     put(inward, times(back, inverse))
-    own, other = inverses_of(minus(block(True, 1), taken), block(False, 0))
+
+
+def advance(slabs, pole, pivot, *refs):
+    middle = slabs // 2
+    block_refs, (here, there, blocks) = refs[:middle], refs[middle:]
+    me = lax.axis_index("slab")
+    zr, zi, _, _ = scalars_of(pole)
+    fill_far(me, blocks, block_refs)
+    block, _ = chain(slabs, me, blocks, None, zr, zi)
+    own, other = inverses_of(get(pivot), block(False, 0))
     put(here, own)
     put(there, other)
 
 
 def finish(slabs, poles, pole, start, second, end, outward_1, inward_1, *refs):
     middle = slabs // 2
-    block_refs, link_refs, refs = refs[:slabs], refs[slabs : 2 * slabs], refs[2 * slabs :]
+    block_refs, coupling, refs = refs[:slabs], refs[slabs], refs[slabs + 1 :]
+    halves, refs = refs[: 2 * middle - 2], refs[2 * middle - 2 :]
+    far_refs, refs = refs[:middle], refs[middle:]
     outs, (blocks, links, outward, inward, own, other, work) = refs[:poles], refs[poles:]
     me, mine = lax.axis_index("slab"), lax.axis_index(("pole", "sub"))
     order = start.shape[-1]
     fill_near(me, blocks, block_refs[:middle])
     fill_far(me, blocks, block_refs[middle:])
-    fill_near(me, links, link_refs[:middle])
-    fill_far(me, links, link_refs[middle:])
+    fill_links(me, links, coupling, halves)
+    fill_far(me, links, far_refs)
     zr, zi, wr, wi = scalars_of(pole)
     block, reduced = chain(slabs, me, blocks, links, zr, zi)
     own[0], own[1], other[0] = start[...], second[...], end[...]
@@ -434,6 +457,10 @@
     def swap(value, k):
         return lax.ppermute(value, "slab", [(i, i ^ k) for i in range(slabs)])
 
+    half = pl.pallas_call(
+        halve, out_shape=square_of, in_specs=[vmem], out_specs=vmem, compiler_params=params
+    )(coupling)
+    near_links = [swap(half, k) for k in range(1, middle)]
     packed = pl.pallas_call(
         prepare, out_shape=square_of, in_specs=[vmem], out_specs=vmem, compiler_params=params
     )(onsite)
@@ -451,7 +478,6 @@
 
     near_blocks = [packed] + [swap(packed, k) for k in range(1, middle)]
     far_blocks = [far_swap(packed, k) for k in range(middle, slabs, 2)]
-    near_links = [coupling] + [swap(coupling, k) for k in range(1, middle)]
     far_links = [far_swap(coupling, k) for k in range(middle, slabs, 2)]
     start = pl.pallas_call(
         functools.partial(start_chain, slabs),
@@ -470,21 +496,32 @@
             pairs += [value, lax.ppermute(mine, "sub", [(0, 1), (1, 0)])]
         return pairs
 
-    blocks = near_blocks + both(far_blocks, start)
-    second = pl.pallas_call(
-        functools.partial(advance, slabs),
-        out_shape=[complex_of] * 4,
-        in_specs=[vmem] * (2 + slabs + middle),
-        out_specs=[vmem] * 4,
+    far_blocks = both(far_blocks, start)
+    near_links = both(near_links, start)
+    pivot, *factors = pl.pallas_call(
+        functools.partial(couple, slabs),
+        out_shape=[complex_of] * 3,
+        in_specs=[vmem] * (1 + 3 * middle),
+        out_specs=[vmem] * 3,
         scratch_shapes=[scratch(slabs), scratch(slabs, 2)],
         compiler_params=params,
         cost_estimate=pl.CostEstimate(flops=1000, bytes_accessed=1000, transcendentals=0),
-    )(pole, start, *blocks, *near_links)
-    links = near_links + both(far_links, second[0])
+    )(pole, start, *near_blocks, coupling, *near_links)
+    far_links = both(far_links, pivot)
+    second = pl.pallas_call(
+        functools.partial(advance, slabs),
+        out_shape=[complex_of] * 2,
+        in_specs=[vmem] * (2 + middle),
+        out_specs=[vmem] * 2,
+        scratch_shapes=[scratch(slabs)],
+        compiler_params=params,
+        cost_estimate=cost(2),
+    )(pole, pivot, *far_blocks)
+    blocks, links = near_blocks + far_blocks, [coupling] + near_links + far_links
     pieces = pl.pallas_call(
         functools.partial(finish, slabs, poles),
         out_shape=[jax.ShapeDtypeStruct((2, 2, order // poles, order), f32)] * poles,
-        in_specs=[vmem] * (6 + 2 * slabs),
+        in_specs=[vmem] * (5 + 2 * slabs + middle),
         out_specs=[vmem] * poles,
         scratch_shapes=[
             scratch(slabs),
@@ -497,7 +534,7 @@
         ],
         compiler_params=params,
         cost_estimate=cost(2),
-    )(pole, start, *second, *blocks, *links)
+    )(pole, start, *second, *factors, *blocks, *links)
     total = pieces[0]
     for k in range(1, poles):
         total = total + lax.ppermute(pieces[k], ("pole", "sub"), [(i, i ^ k) for i in range(poles)])

time: 36.1 us -> 35.3 us (0.978)
  waiting for transfers between devices: 7.34 us -> 6.8 us
  Pallas kernels: 16.7 us -> 16.3 us
    ppermute x2 -> x3, waiting for transfers between devices: 2.58 us -> 0.18 us  [both(): pairs += [value, lax.ppermute(mine, 'sub', [(0, 1), (1, 0)])]]
    ppermute x2, waiting for transfers between devices: 0.01 us -> 2.25 us  [far_swap(): return lax.ppermute(value, ('slab', 'sub'), pairs)]
    pallas_call x1, Pallas kernels: 6.27 us -> 5.28 us  [shards(): pl.pallas_call(functools.partial(advance, slabs), out_shape=[complex_of]...]
    ppermute x2, waiting for transfers between devices: 0.82 us -> 0.01 us  [swap(): return lax.ppermute(value, 'slab', [(i, i ^ k) for i in range(slabs)])]
    pallas_call x0 -> x2, Pallas kernels: none -> 0.74 us  [the longest x1 0.73 us: shards(): pl.pallas_call(functools.partial(couple, slabs), out_shape=[complex_of] *...]
    ppermute x3, waiting for transfers between devices: 3.94 us -> 4.37 us  [shards(): lax.ppermute(pieces[k], ('pole', 'sub'), [(i, i ^ k) for i in range(poles)])]
  transfers between devices with their start and end apart: 9 -> 10, of which waited for: 5 -> 5; matrix products, arithmetic and copies ran while one was open for 0% -> 0% of each run, Pallas kernels for 29% -> 29%
where the time goes in v5:
time: 35.3 us; the launch traced here: 35.1 us
  Pallas kernels  16.3 us (46%)
  starting transfers between devices  8.34 us (24%)
  waiting for transfers between devices  6.8 us (19%)
  between operations  2.05 us (6%)
  local copies, waits for them, and re-layouts  1.57 us (4%)
    pallas_call x1, Pallas kernels, shards(): pl.pallas_call(functools.partial(finish, slabs, poles), out_shape=[jax.Sh...  6.03 us
    pallas_call x1, Pallas kernels, shards(): pl.pallas_call(functools.partial(advance, slabs), out_shape=[complex_of]...  5.28 us
    ppermute x3, waiting for transfers between devices, shards(): lax.ppermute(pieces[k], ('pole', 'sub'), [(i, i ^ k) for i in range(poles)])  4.37 us
    pallas_call x1, Pallas kernels, shards(): pl.pallas_call(functools.partial(start_chain, slabs), out_shape=complex_o...  4.1 us
    ppermute x2, starting transfers between devices, swap(): return lax.ppermute(value, 'slab', [(i, i ^ k) for i in range(slabs)])  3.27 us
    ppermute x2, starting transfers between devices, far_swap(): return lax.ppermute(value, ('slab', 'sub'), pairs)  2.92 us
    ppermute x2, waiting for transfers between devices, far_swap(): return lax.ppermute(value, ('slab', 'sub'), pairs)  2.25 us
    ppermute x3, starting transfers between devices, shards(): lax.ppermute(pieces[k], ('pole', 'sub'), [(i, i ^ k) for i in range(poles)])  2.06 us
  transfers between devices with their start and end apart: 10, of which 5 were waited for; matrix products, arithmetic and copies ran while one was open for 0% of the time, Pallas kernels for 29%

profile of v5, /device:TPU:0, one launch (start us, length us, event | category | flops | bytes accessed | tf_op | source)
XLA Modules:
  0.0 35.1 jit_solution(17825784042315063375)
XLA Ops:
  0.6 0.9 %copy-done.1 = f32[1,2,128,128]{3,2,1,0:T(8,128)S(1)} copy-done((f32[1,2,128,128]{3,2,1,0:T(8,128)S(1)}, f32[1,2,128,128]{3,2,1,0:T(8,128)}, u32[]{:S(2)}) %copy-start.1) | copy-done | bytes 131096
  1.6 0.1 shard_map.69.refs_0_
  1.7 3.1 %collective-permute-start = (f32[128,128]{1,0:T(8,128)S(1)}, f32[128,128]{1,0:T(8,128)S(1)}, u32[]{:S(2)}, u32[]{:S(2)}) collective-permute-start(f32[128,128]{1,0:T(8,128)S(1)} %shard_map.69.refs_0_), channel_id=1, source_target_pairs={{0,4},{4,0},{8,12},{12,8},{1,5},{5,1},{9,13},{13,9},{2,6},{6,2},{1... | collective-permute-start | bytes 196616 | tf_op jit(solution)/shard_map/ppermute | solution.py:458
  4.8 2.6 %collective-permute-start.3 = (f32[128,128]{1,0:T(8,128)S(1)}, f32[128,128]{1,0:T(8,128)S(1)}, u32[]{:S(2)}, u32[]{:S(2)}) collective-permute-start(f32[128,128]{1,0:T(8,128)S(1)} %shard_map.69.refs_0_), channel_id=1, source_target_pairs={{0,8},{1,13},{4,12},{5,9},{8,0},{9,5},{12,4},{13,1},{2,10},{3,15},... | collective-permute-start | bytes 196616 | tf_op jit(solution)/shard_map/ppermute | solution.py:477
  7.4 0.3 collective-permute-start.5
  7.7 0.2 collective-permute-start.1
  8.5 0.0 copy-start.2
  9.2 0.1 shard_map.68.pole
  9.3 0.0 collective-permute-done.refs_1_
  9.3 4.1 %shard_map.70.start = f32[2,128,128]{2,1,0:T(8,128)S(1)} custom-call(f32[8,128]{1,0:T(8,128)S(1)} %shard_map.68.pole, f32[128,128]{1,0:T(8,128)S(1)} %shard_map.69.refs_0_, f32[128,128]{1,0:T(8,128)S(1)} %collective-permute-done.refs_1_), custom_call_target="tpu_custom_call" | custom-call | flops 5000000000 | bytes 2000000 | tf_op jit(solution)/shard_map/pallas_call | solution.py:482
  13.4 0.1 collective-permute-start.2
  13.5 1.1 %collective-permute-done.3.refs_0_.refs_2_ = f32[128,128]{1,0:T(8,128)S(1)} collective-permute-done((f32[128,128]{1,0:T(8,128)S(1)}, f32[128,128]{1,0:T(8,128)S(1)}, u32[]{:S(2)}, u32[]{:S(2)}) %collective-permute-start.3) | collective-permute-done | bytes 65568 | tf_op jit(solution)/shard_map/ppermute | solution.py:477
  14.6 0.0 collective-permute-start.4
  14.6 0.2 collective-permute-done.2.refs_4_.refs_6_
  14.7 0.7 %shard_map.72 = (f32[2,128,128]{2,1,0:T(8,128)S(1)}, f32[2,128,128]{2,1,0:T(8,128)S(1)}, f32[2,128,128]{2,1,0:T(8,128)S(1)}) custom-call(f32[8,128]{1,0:T(8,128)S(1)} %shard_map.68.pole, f32[2,128,128]{2,1,0:T(8,128)S(1)} %shard_map.70.start, f32[128,128]{1,0:T(8,128)S(1)} %shard_map.69.refs_0_, f32[128,128]{1,0:T(8,128)S(1)} %collective-permute-done.refs_1_, ...), custom_call_target="tpu_custom_call" | custom-call | flops 1000 | bytes 1000 | tf_op jit(solution)/shard_map/pallas_call | solution.py:501
  15.5 1.2 %collective-permute-done.5.refs_7_ = f32[1,2,128,128]{3,2,1,0:T(8,128)S(1)} collective-permute-done((f32[1,2,128,128]{3,2,1,0:T(8,128)S(1)}, f32[1,2,128,128]{3,2,1,0:T(8,128)S(1)}, u32[]{:S(2)}, u32[]{:S(2)}) %collective-permute-start.5) | collective-permute-done | bytes 131104 | tf_op jit(solution)/shard_map/ppermute | solution.py:477
  16.7 0.0 collective-permute-start.6
  16.7 5.3 %shard_map.73 = (f32[2,128,128]{2,1,0:T(8,128)S(1)}, f32[2,128,128]{2,1,0:T(8,128)S(1)}) custom-call(f32[8,128]{1,0:T(8,128)S(1)} %shard_map.68.pole, f32[2,128,128]{2,1,0:T(8,128)S(1)} %get-tuple-element.15.pivot, f32[128,128]{1,0:T(8,128)S(1)} %collective-permute-done.3.refs_0_.refs_2_, f32[128,128]{1,0:T(8,128)S(1)} %collective-permute-done.4.refs_1_.refs_3_), custom_call_target="tpu_custom_call" | custom-call | flops 5000000000 | bytes 2000000 | tf_op jit(solution)/shard_map/pallas_call | solution.py:511
  22.0 6.0 %shard_map.74 = (f32[2,2,32,128]{3,2,1,0:T(8,128)S(1)}, f32[2,2,32,128]{3,2,1,0:T(8,128)S(1)}, f32[2,2,32,128]{3,2,1,0:T(8,128)S(1)}, f32[2,2,32,128]{3,2,1,0:T(8,128)S(1)}) custom-call(f32[8,128]{1,0:T(8,128)S(1)} %shard_map.68.pole, f32[2,128,128]{2,1,0:T(8,128)S(1)} %shard_map.70.start, f32[2,128,128]{2,1,0:T(8,128)S(1)} %get-tuple-element.17.second, ...), custom_call_target="tpu_custom_call" | custom-call | flops 5000000000 | bytes 2000000 | tf_op jit(solution)/shard_map/pallas_call | solution.py:521
  28.0 0.6 %collective-permute-start.7 = (f32[2,2,32,128]{3,2,1,0:T(8,128)S(1)}, f32[2,2,32,128]{3,2,1,0:T(8,128)S(1)}, u32[]{:S(2)}, u32[]{:S(2)}) collective-permute-start(f32[2,2,32,128]{3,2,1,0:T(8,128)S(1)} %get-tuple-element.23), channel_id=1, source_target_pairs={{0,1},{1,0},{2,3},{3,2},{4,5},{5,4},{6,7},{7,6},{8,9},{9,8},{10,11... | collective-permute-start | bytes 196616 | tf_op jit(solution)/shard_map/ppermute | solution.py:540
  28.6 1.5 %collective-permute-start.8 = (f32[2,2,32,128]{3,2,1,0:T(8,128)S(1)}, f32[2,2,32,128]{3,2,1,0:T(8,128)S(1)}, u32[]{:S(2)}, u32[]{:S(2)}) collective-permute-start(f32[2,2,32,128]{3,2,1,0:T(8,128)S(1)} %get-tuple-element.24), channel_id=1, source_target_pairs={{0,2},{1,3},{2,0},{3,1},{4,6},{5,7},{6,4},{7,5},{8,10},{9,11},{10,... | collective-permute-start | bytes 196616 | tf_op jit(solution)/shard_map/ppermute | solution.py:540
  30.1 2.8 %collective-permute-done.8 = f32[2,2,32,128]{3,2,1,0:T(8,128)S(1)} collective-permute-done((f32[2,2,32,128]{3,2,1,0:T(8,128)S(1)}, f32[2,2,32,128]{3,2,1,0:T(8,128)S(1)}, u32[]{:S(2)}, u32[]{:S(2)}) %collective-permute-start.8) | collective-permute-done | bytes 65568 | tf_op jit(solution)/shard_map/ppermute | solution.py:540
  32.9 1.6 %collective-permute-done.9 = f32[2,2,32,128]{3,2,1,0:T(8,128)S(1)} collective-permute-done((f32[2,2,32,128]{3,2,1,0:T(8,128)S(1)}, f32[2,2,32,128]{3,2,1,0:T(8,128)S(1)}, u32[]{:S(2)}, u32[]{:S(2)}) %collective-permute-start.9) | collective-permute-done | bytes 65568 | tf_op jit(solution)/shard_map/ppermute | solution.py:540
  34.5 0.6 %fusion = (f32[1,2,32,128]{3,2,1,0:T(8,128)}, f32[1,2,32,128]{3,2,1,0:T(8,128)}) fusion(f32[2,2,32,128]{3,2,1,0:T(8,128)S(1)} %add_add_fusion), kind=kLoop, calls=%fused_computation.1 | loop fusion | bytes 131072 | tf_op jit(solution)/shard_map/slice | solution.py:541
  (11 shorter events, 0.0 us)
Async XLA Ops:
  0.6 6.7 %copy-start = (f32[1,2,128,128]{3,2,1,0:T(8,128)S(1)}, f32[1,2,128,128]{3,2,1,0:T(8,128)}, u32[]{:S(2)}) copy-start(f32[1,2,128,128]{3,2,1,0:T(8,128)} %refs_4_.1) | copy-start | bytes 393220
  0.6 0.9 %copy-start.1 = (f32[1,2,128,128]{3,2,1,0:T(8,128)S(1)}, f32[1,2,128,128]{3,2,1,0:T(8,128)}, u32[]{:S(2)}) copy-start(f32[1,2,128,128]{3,2,1,0:T(8,128)} %onsite.1) | copy-start | bytes 393220
  1.7 7.6 %collective-permute-start = (f32[128,128]{1,0:T(8,128)S(1)}, f32[128,128]{1,0:T(8,128)S(1)}, u32[]{:S(2)}, u32[]{:S(2)}) collective-permute-start(f32[128,128]{1,0:T(8,128)S(1)} %shard_map.69.refs_0_), channel_id=1, source_target_pairs={{0,4},{4,0},{8,12},{12,8},{1,5},{5,1},{9,13},{13,9},{2,6},{6,2},{1... | collective-permute-start | bytes 196616 | tf_op jit(solution)/shard_map/ppermute | solution.py:458
  4.8 9.8 %collective-permute-start.3 = (f32[128,128]{1,0:T(8,128)S(1)}, f32[128,128]{1,0:T(8,128)S(1)}, u32[]{:S(2)}, u32[]{:S(2)}) collective-permute-start(f32[128,128]{1,0:T(8,128)S(1)} %shard_map.69.refs_0_), channel_id=1, source_target_pairs={{0,8},{1,13},{4,12},{5,9},{8,0},{9,5},{12,4},{13,1},{2,10},{3,15},... | collective-permute-start | bytes 196616 | tf_op jit(solution)/shard_map/ppermute | solution.py:477
  7.4 9.3 %collective-permute-start.5 = (f32[1,2,128,128]{3,2,1,0:T(8,128)S(1)}, f32[1,2,128,128]{3,2,1,0:T(8,128)S(1)}, u32[]{:S(2)}, u32[]{:S(2)}) collective-permute-start(f32[1,2,128,128]{3,2,1,0:T(8,128)S(1)} %copy-done), channel_id=1, source_target_pairs={{0,8},{1,13},{4,12},{5,9},{8,0},{9,5},{12,4},{13,1},{2,10},{3,15},... | collective-permute-start | bytes 393224 | tf_op jit(solution)/shard_map/ppermute | solution.py:477
  7.7 5.7 %collective-permute-start.1 = (f32[128,128]{1,0:T(8,128)S(1)}, f32[128,128]{1,0:T(8,128)S(1)}, u32[]{:S(2)}, u32[]{:S(2)}) collective-permute-start(f32[128,128]{1,0:T(8,128)S(1)} %shard_map.71), channel_id=1, source_target_pairs={{0,4},{4,0},{8,12},{12,8},{1,5},{5,1},{9,13},{13,9},{2,6},{6,2},{1... | collective-permute-start | bytes 196616 | tf_op jit(solution)/shard_map/ppermute | solution.py:458
  8.5 0.7 %copy-start.2 = (f32[1,2]{1,0:T(1,128)S(1)}, f32[1,2]{1,0:T(1,128)}, u32[]{:S(2)}) copy-start(f32[1,2]{1,0:T(1,128)} %pole_weight.1) | copy-start | bytes 28
  13.4 1.3 %collective-permute-start.2 = (f32[128,128]{1,0:T(8,128)S(1)}, f32[128,128]{1,0:T(8,128)S(1)}, u32[]{:S(2)}, u32[]{:S(2)}) collective-permute-start(f32[128,128]{1,0:T(8,128)S(1)} %collective-permute-done.1.refs_3_.refs_5_), channel_id=1, source_target_pairs={{0,1},{1,0},{2,3},{3,2},{4,5},{5,4},{6,7},{7,6},{8,9},{9,8},{10,11... | collective-permute-start | bytes 196616 | tf_op jit(solution)/shard_map/ppermute | solution.py:496
  14.6 2.1 %collective-permute-start.4 = (f32[128,128]{1,0:T(8,128)S(1)}, f32[128,128]{1,0:T(8,128)S(1)}, u32[]{:S(2)}, u32[]{:S(2)}) collective-permute-start(f32[128,128]{1,0:T(8,128)S(1)} %collective-permute-done.3.refs_0_.refs_2_), channel_id=1, source_target_pairs={{0,1},{1,0},{2,3},{3,2},{4,5},{5,4},{6,7},{7,6},{8,9},{9,8},{10,11... | collective-permute-start | bytes 196616 | tf_op jit(solution)/shard_map/ppermute | solution.py:496
  16.7 5.3 %collective-permute-start.6 = (f32[1,2,128,128]{3,2,1,0:T(8,128)S(1)}, f32[1,2,128,128]{3,2,1,0:T(8,128)S(1)}, u32[]{:S(2)}, u32[]{:S(2)}) collective-permute-start(f32[1,2,128,128]{3,2,1,0:T(8,128)S(1)} %collective-permute-done.5.refs_7_), channel_id=1, source_target_pairs={{0,1},{1,0},{2,3},{3,2},{4,5},{5,4},{6,7},{7,6},{8,9},{9,8},{10,11... | collective-permute-start | bytes 393224 | tf_op jit(solution)/shard_map/ppermute | solution.py:496
  28.0 2.1 %collective-permute-start.7 = (f32[2,2,32,128]{3,2,1,0:T(8,128)S(1)}, f32[2,2,32,128]{3,2,1,0:T(8,128)S(1)}, u32[]{:S(2)}, u32[]{:S(2)}) collective-permute-start(f32[2,2,32,128]{3,2,1,0:T(8,128)S(1)} %get-tuple-element.23), channel_id=1, source_target_pairs={{0,1},{1,0},{2,3},{3,2},{4,5},{5,4},{6,7},{7,6},{8,9},{9,8},{10,11... | collective-permute-start | bytes 196616 | tf_op jit(solution)/shard_map/ppermute | solution.py:540
  28.6 4.3 %collective-permute-start.8 = (f32[2,2,32,128]{3,2,1,0:T(8,128)S(1)}, f32[2,2,32,128]{3,2,1,0:T(8,128)S(1)}, u32[]{:S(2)}, u32[]{:S(2)}) collective-permute-start(f32[2,2,32,128]{3,2,1,0:T(8,128)S(1)} %get-tuple-element.24), channel_id=1, source_target_pairs={{0,2},{1,3},{2,0},{3,1},{4,6},{5,7},{6,4},{7,5},{8,10},{9,11},{10,... | collective-permute-start | bytes 196616 | tf_op jit(solution)/shard_map/ppermute | solution.py:540
  30.1 4.4 %collective-permute-start.9 = (f32[2,2,32,128]{3,2,1,0:T(8,128)S(1)}, f32[2,2,32,128]{3,2,1,0:T(8,128)S(1)}, u32[]{:S(2)}, u32[]{:S(2)}) collective-permute-start(f32[2,2,32,128]{3,2,1,0:T(8,128)S(1)} %get-tuple-element.25), channel_id=1, source_target_pairs={{0,3},{1,2},{2,1},{3,0},{4,7},{5,6},{6,5},{7,4},{8,11},{9,10},{10,... | collective-permute-start | bytes 196616 | tf_op jit(solution)/shard_map/ppermute | solution.py:540

commit v6 on v5

--- a/solution.py
+++ b/solution.py
@@ -9,6 +9,7 @@
 
 ROWS = 8
 PANEL = 2 * ROWS
+SPLIT = 2
 f32, bf16 = jnp.float32, jnp.bfloat16
 PARTS = ((0, 0), (1, 0), (0, 1), (1, 1), (0, 2), (2, 0))
 
@@ -159,21 +160,21 @@
     return [(real[ROWS * t : ROWS * t + ROWS], imag[ROWS * t : ROWS * t + ROWS]) for t in range(len(tiles))]
 
 
-def invert(systems, asides):
+def invert(systems, asides=(), begin=0, end=None):
     order = systems[0][0][0].shape[1]
     count, panels = order // ROWS, order // PANEL
     lane = lax.broadcasted_iota(jnp.int32, (ROWS, order), 1)
     subl = lax.broadcasted_iota(jnp.int32, (ROWS, order), 0)
     systems = [list(tiles) for tiles in systems]
     sweep = sweep_double if len(systems) == 1 else sweep_single
-    for place in range(panels):
+    for place in range(panels)[begin:end]:
         a, b = 2 * place, 2 * place + 1
         in_a = (lane >= ROWS * a) & (lane < ROWS * a + ROWS)
         in_b = (lane >= ROWS * b) & (lane < ROWS * b + ROWS)
         soon = [] if place == panels - 1 else [b + 1, b + 2]
         nexts = [[tiles[i] for tiles in systems] for i in soon]
         second = [tiles[b] for tiles in systems]
-        if place == 0:
+        if place == begin:
             columns = spread([tiles[a] for tiles in systems], ROWS * a)
         second_columns = spread(second, ROWS * a)
         next_columns = [spread(tiles, ROWS * a) for tiles in nexts]
@@ -356,9 +357,15 @@
     zr, zi, _, _ = scalars_of(pole)
     fill_far(me, blocks, block_refs)
     block, _ = chain(slabs, me, blocks, None, zr, zi)
-    own, other = inverses_of(get(pivot), block(False, 0))
-    put(here, own)
-    put(there, other)
+    swept = invert([to_tiles(get(pivot)), to_tiles(block(False, 0))], end=SPLIT)
+    for ref, tiles in zip((here, there), swept):
+        put(ref, from_tiles(tiles))
+
+
+def advance_on(here, there, own, other):
+    swept = invert([to_tiles(get(here)), to_tiles(get(there))], begin=SPLIT)
+    for ref, tiles in zip((own, other), swept):
+        put(ref, from_tiles(tiles))
 
 
 def finish(slabs, poles, pole, start, second, end, outward_1, inward_1, *refs):
@@ -496,8 +503,10 @@
             pairs += [value, lax.ppermute(mine, "sub", [(0, 1), (1, 0)])]
         return pairs
 
-    far_blocks = both(far_blocks, start)
+    arrived = near_links[0]
     near_links = both(near_links, start)
+    after = lax.optimization_barrier((start, arrived))[0]
+    far_blocks = both(far_blocks, after)
     pivot, *factors = pl.pallas_call(
         functools.partial(couple, slabs),
         out_shape=[complex_of] * 3,
@@ -507,16 +516,24 @@
         compiler_params=params,
         cost_estimate=pl.CostEstimate(flops=1000, bytes_accessed=1000, transcendentals=0),
     )(pole, start, *near_blocks, coupling, *near_links)
-    far_links = both(far_links, pivot)
-    second = pl.pallas_call(
+    swept = pl.pallas_call(
         functools.partial(advance, slabs),
         out_shape=[complex_of] * 2,
         in_specs=[vmem] * (2 + middle),
         out_specs=[vmem] * 2,
         scratch_shapes=[scratch(slabs)],
         compiler_params=params,
+        cost_estimate=pl.CostEstimate(flops=1000, bytes_accessed=1000, transcendentals=0),
+    )(pole, pivot, *far_blocks)
+    far_links = both(far_links, swept[0])
+    second = pl.pallas_call(
+        advance_on,
+        out_shape=[complex_of] * 2,
+        in_specs=[vmem] * 2,
+        out_specs=[vmem] * 2,
+        compiler_params=params,
         cost_estimate=cost(2),
-    )(pole, pivot, *far_blocks)
+    )(*swept)
     blocks, links = near_blocks + far_blocks, [coupling] + near_links + far_links
     pieces = pl.pallas_call(
         functools.partial(finish, slabs, poles),

time: 35.3 us -> 34.8 us (0.986)
  waiting for transfers between devices: 6.8 us -> 5.88 us
    pallas_call x0 -> x1, Pallas kernels: none -> 4.11 us  [shards(): pl.pallas_call(advance_on, out_shape=[complex_of] * 2, in_specs=[vmem] *...]
    pallas_call x1, Pallas kernels: 5.28 us -> 1.48 us  [shards(): pl.pallas_call(functools.partial(advance, slabs), out_shape=[complex_of]...]
    ppermute x2, waiting for transfers between devices: 2.25 us -> 1.06 us  [far_swap(): return lax.ppermute(value, ('slab', 'sub'), pairs)]
  transfers between devices with their start and end apart: 10 -> 10, of which waited for: 5 -> 5; matrix products, arithmetic and copies ran while one was open for 0% -> 0% of each run, Pallas kernels for 29% -> 30%
where the time goes in v6:
time: 34.8 us; the launch traced here: 34.6 us
  Pallas kernels  16.6 us (48%)
  starting transfers between devices  8.43 us (24%)
  waiting for transfers between devices  5.88 us (17%)
  between operations  2.06 us (6%)
  local copies, waits for them, and re-layouts  1.57 us (5%)
    pallas_call x1, Pallas kernels, shards(): pl.pallas_call(functools.partial(finish, slabs, poles), out_shape=[jax.Sh...  6.03 us
    ppermute x3, waiting for transfers between devices, shards(): lax.ppermute(pieces[k], ('pole', 'sub'), [(i, i ^ k) for i in range(poles)])  4.3 us
    pallas_call x1, Pallas kernels, shards(): pl.pallas_call(advance_on, out_shape=[complex_of] * 2, in_specs=[vmem] *...  4.11 us
    pallas_call x1, Pallas kernels, shards(): pl.pallas_call(functools.partial(start_chain, slabs), out_shape=complex_o...  4.1 us
    ppermute x2, starting transfers between devices, swap(): return lax.ppermute(value, 'slab', [(i, i ^ k) for i in range(slabs)])  3.27 us
    ppermute x2, starting transfers between devices, far_swap(): return lax.ppermute(value, ('slab', 'sub'), pairs)  2.92 us
    ppermute x3, starting transfers between devices, shards(): lax.ppermute(pieces[k], ('pole', 'sub'), [(i, i ^ k) for i in range(poles)])  1.94 us
    pallas_call x1, Pallas kernels, shards(): pl.pallas_call(functools.partial(advance, slabs), out_shape=[complex_of]...  1.48 us
  transfers between devices with their start and end apart: 10, of which 5 were waited for; matrix products, arithmetic and copies ran while one was open for 0% of the time, Pallas kernels for 30%

profile of v6, /device:TPU:0, one launch (start us, length us, event | category | flops | bytes accessed | tf_op | source)
XLA Modules:
  0.0 34.6 jit_solution(13580481562908548783)
XLA Ops:
  0.6 0.9 %copy-done.1 = f32[1,2,128,128]{3,2,1,0:T(8,128)S(1)} copy-done((f32[1,2,128,128]{3,2,1,0:T(8,128)S(1)}, f32[1,2,128,128]{3,2,1,0:T(8,128)}, u32[]{:S(2)}) %copy-start.1) | copy-done | bytes 131096
  1.6 0.1 shard_map.69.refs_0_
  1.7 3.1 %collective-permute-start = (f32[128,128]{1,0:T(8,128)S(1)}, f32[128,128]{1,0:T(8,128)S(1)}, u32[]{:S(2)}, u32[]{:S(2)}) collective-permute-start(f32[128,128]{1,0:T(8,128)S(1)} %shard_map.69.refs_0_), channel_id=1, source_target_pairs={{0,4},{4,0},{8,12},{12,8},{1,5},{5,1},{9,13},{13,9},{2,6},{6,2},{1... | collective-permute-start | bytes 196616 | tf_op jit(solution)/shard_map/ppermute | solution.py:465
  4.8 2.6 %collective-permute-start.3 = (f32[128,128]{1,0:T(8,128)S(1)}, f32[128,128]{1,0:T(8,128)S(1)}, u32[]{:S(2)}, u32[]{:S(2)}) collective-permute-start(f32[128,128]{1,0:T(8,128)S(1)} %shard_map.69.refs_0_), channel_id=1, source_target_pairs={{0,8},{1,13},{4,12},{5,9},{8,0},{9,5},{12,4},{13,1},{2,10},{3,15},... | collective-permute-start | bytes 196616 | tf_op jit(solution)/shard_map/ppermute | solution.py:484
  7.4 0.3 collective-permute-start.5
  7.7 0.2 collective-permute-start.1
  8.5 0.0 copy-start.2
  9.2 0.1 shard_map.68.pole
  9.3 4.1 %shard_map.70.start = f32[2,128,128]{2,1,0:T(8,128)S(1)} custom-call(f32[8,128]{1,0:T(8,128)S(1)} %shard_map.68.pole, f32[128,128]{1,0:T(8,128)S(1)} %shard_map.69.refs_0_, f32[128,128]{1,0:T(8,128)S(1)} %collective-permute-done.refs_1_), custom_call_target="tpu_custom_call" | custom-call | flops 5000000000 | bytes 2000000 | tf_op jit(solution)/shard_map/pallas_call | solution.py:489
  13.4 0.1 collective-permute-start.2
  13.5 1.1 %collective-permute-done.3.refs_0_.refs_2_ = f32[128,128]{1,0:T(8,128)S(1)} collective-permute-done((f32[128,128]{1,0:T(8,128)S(1)}, f32[128,128]{1,0:T(8,128)S(1)}, u32[]{:S(2)}, u32[]{:S(2)}) %collective-permute-start.3) | collective-permute-done | bytes 65568 | tf_op jit(solution)/shard_map/ppermute | solution.py:484
  14.6 0.2 collective-permute-done.2.refs_4_.refs_6_
  14.7 0.7 %shard_map.72 = (f32[2,128,128]{2,1,0:T(8,128)S(1)}, f32[2,128,128]{2,1,0:T(8,128)S(1)}, f32[2,128,128]{2,1,0:T(8,128)S(1)}) custom-call(f32[8,128]{1,0:T(8,128)S(1)} %shard_map.68.pole, f32[2,128,128]{2,1,0:T(8,128)S(1)} %shard_map.70.start, f32[128,128]{1,0:T(8,128)S(1)} %shard_map.69.refs_0_, f32[128,128]{1,0:T(8,128)S(1)} %collective-permute-done.refs_1_, ...), custom_call_target="tpu_custom_call" | custom-call | flops 1000 | bytes 1000 | tf_op jit(solution)/shard_map/pallas_call | solution.py:510
  15.5 0.3 collective-permute-done.4.refs_1_.refs_3_
  15.8 1.5 %shard_map.73 = (f32[2,128,128]{2,1,0:T(8,128)S(1)}, f32[2,128,128]{2,1,0:T(8,128)S(1)}) custom-call(f32[8,128]{1,0:T(8,128)S(1)} %shard_map.68.pole, f32[2,128,128]{2,1,0:T(8,128)S(1)} %get-tuple-element.16.pivot, f32[128,128]{1,0:T(8,128)S(1)} %collective-permute-done.3.refs_0_.refs_2_, f32[128,128]{1,0:T(8,128)S(1)} %collective-permute-done.4.refs_1_.refs_3_), custom_call_target="tpu_custom_call" | custom-call | flops 1000 | bytes 1000 | tf_op jit(solution)/shard_map/pallas_call | solution.py:519
  17.3 0.2 collective-permute-start.6
  17.5 4.1 %shard_map.74 = (f32[2,128,128]{2,1,0:T(8,128)S(1)}, f32[2,128,128]{2,1,0:T(8,128)S(1)}) custom-call(f32[2,128,128]{2,1,0:T(8,128)S(1)} %get-tuple-element.17.here, f32[2,128,128]{2,1,0:T(8,128)S(1)} %get-tuple-element.18.there), custom_call_target="tpu_custom_call" | custom-call | flops 5000000000 | bytes 2000000 | tf_op jit(solution)/shard_map/pallas_call | solution.py:529
  21.7 6.0 %shard_map.75 = (f32[2,2,32,128]{3,2,1,0:T(8,128)S(1)}, f32[2,2,32,128]{3,2,1,0:T(8,128)S(1)}, f32[2,2,32,128]{3,2,1,0:T(8,128)S(1)}, f32[2,2,32,128]{3,2,1,0:T(8,128)S(1)}) custom-call(f32[8,128]{1,0:T(8,128)S(1)} %shard_map.68.pole, f32[2,128,128]{2,1,0:T(8,128)S(1)} %shard_map.70.start, f32[2,128,128]{2,1,0:T(8,128)S(1)} %get-tuple-element.19.second, ...), custom_call_target="tpu_custom_call" | custom-call | flops 5000000000 | bytes 2000000 | tf_op jit(solution)/shard_map/pallas_call | solution.py:538
  27.7 0.4 %collective-permute-start.7 = (f32[2,2,32,128]{3,2,1,0:T(8,128)S(1)}, f32[2,2,32,128]{3,2,1,0:T(8,128)S(1)}, u32[]{:S(2)}, u32[]{:S(2)}) collective-permute-start(f32[2,2,32,128]{3,2,1,0:T(8,128)S(1)} %get-tuple-element.25), channel_id=1, source_target_pairs={{0,1},{1,0},{2,3},{3,2},{4,5},{5,4},{6,7},{7,6},{8,9},{9,8},{10,11... | collective-permute-start | bytes 196616 | tf_op jit(solution)/shard_map/ppermute | solution.py:557
  28.1 1.5 %collective-permute-start.8 = (f32[2,2,32,128]{3,2,1,0:T(8,128)S(1)}, f32[2,2,32,128]{3,2,1,0:T(8,128)S(1)}, u32[]{:S(2)}, u32[]{:S(2)}) collective-permute-start(f32[2,2,32,128]{3,2,1,0:T(8,128)S(1)} %get-tuple-element.26), channel_id=1, source_target_pairs={{0,2},{1,3},{2,0},{3,1},{4,6},{5,7},{6,4},{7,5},{8,10},{9,11},{10,... | collective-permute-start | bytes 196616 | tf_op jit(solution)/shard_map/ppermute | solution.py:557
  29.6 0.0 collective-permute-start.9
  29.6 2.7 %collective-permute-done.8 = f32[2,2,32,128]{3,2,1,0:T(8,128)S(1)} collective-permute-done((f32[2,2,32,128]{3,2,1,0:T(8,128)S(1)}, f32[2,2,32,128]{3,2,1,0:T(8,128)S(1)}, u32[]{:S(2)}, u32[]{:S(2)}) %collective-permute-start.8) | collective-permute-done | bytes 65568 | tf_op jit(solution)/shard_map/ppermute | solution.py:557
  32.4 1.6 %collective-permute-done.9 = f32[2,2,32,128]{3,2,1,0:T(8,128)S(1)} collective-permute-done((f32[2,2,32,128]{3,2,1,0:T(8,128)S(1)}, f32[2,2,32,128]{3,2,1,0:T(8,128)S(1)}, u32[]{:S(2)}, u32[]{:S(2)}) %collective-permute-start.9) | collective-permute-done | bytes 65568 | tf_op jit(solution)/shard_map/ppermute | solution.py:557
  34.0 0.6 %fusion = (f32[1,2,32,128]{3,2,1,0:T(8,128)}, f32[1,2,32,128]{3,2,1,0:T(8,128)}) fusion(f32[2,2,32,128]{3,2,1,0:T(8,128)S(1)} %add_add_fusion), kind=kLoop, calls=%fused_computation.1 | loop fusion | bytes 131072 | tf_op jit(solution)/shard_map/slice | solution.py:558
  (12 shorter events, 0.0 us)
Async XLA Ops:
  0.6 6.7 %copy-start = (f32[1,2,128,128]{3,2,1,0:T(8,128)S(1)}, f32[1,2,128,128]{3,2,1,0:T(8,128)}, u32[]{:S(2)}) copy-start(f32[1,2,128,128]{3,2,1,0:T(8,128)} %refs_4_.1) | copy-start | bytes 393220
  0.6 0.9 %copy-start.1 = (f32[1,2,128,128]{3,2,1,0:T(8,128)S(1)}, f32[1,2,128,128]{3,2,1,0:T(8,128)}, u32[]{:S(2)}) copy-start(f32[1,2,128,128]{3,2,1,0:T(8,128)} %onsite.1) | copy-start | bytes 393220
  1.7 7.6 %collective-permute-start = (f32[128,128]{1,0:T(8,128)S(1)}, f32[128,128]{1,0:T(8,128)S(1)}, u32[]{:S(2)}, u32[]{:S(2)}) collective-permute-start(f32[128,128]{1,0:T(8,128)S(1)} %shard_map.69.refs_0_), channel_id=1, source_target_pairs={{0,4},{4,0},{8,12},{12,8},{1,5},{5,1},{9,13},{13,9},{2,6},{6,2},{1... | collective-permute-start | bytes 196616 | tf_op jit(solution)/shard_map/ppermute | solution.py:465
  4.8 9.8 %collective-permute-start.3 = (f32[128,128]{1,0:T(8,128)S(1)}, f32[128,128]{1,0:T(8,128)S(1)}, u32[]{:S(2)}, u32[]{:S(2)}) collective-permute-start(f32[128,128]{1,0:T(8,128)S(1)} %shard_map.69.refs_0_), channel_id=1, source_target_pairs={{0,8},{1,13},{4,12},{5,9},{8,0},{9,5},{12,4},{13,1},{2,10},{3,15},... | collective-permute-start | bytes 196616 | tf_op jit(solution)/shard_map/ppermute | solution.py:484
  7.4 9.9 %collective-permute-start.5 = (f32[1,2,128,128]{3,2,1,0:T(8,128)S(1)}, f32[1,2,128,128]{3,2,1,0:T(8,128)S(1)}, u32[]{:S(2)}, u32[]{:S(2)}) collective-permute-start(f32[1,2,128,128]{3,2,1,0:T(8,128)S(1)} %copy-done), channel_id=1, source_target_pairs={{0,8},{1,13},{4,12},{5,9},{8,0},{9,5},{12,4},{13,1},{2,10},{3,15},... | collective-permute-start | bytes 393224 | tf_op jit(solution)/shard_map/ppermute | solution.py:484
  7.7 5.7 %collective-permute-start.1 = (f32[128,128]{1,0:T(8,128)S(1)}, f32[128,128]{1,0:T(8,128)S(1)}, u32[]{:S(2)}, u32[]{:S(2)}) collective-permute-start(f32[128,128]{1,0:T(8,128)S(1)} %shard_map.71), channel_id=1, source_target_pairs={{0,4},{4,0},{8,12},{12,8},{1,5},{5,1},{9,13},{13,9},{2,6},{6,2},{1... | collective-permute-start | bytes 196616 | tf_op jit(solution)/shard_map/ppermute | solution.py:465
  8.5 0.7 %copy-start.2 = (f32[1,2]{1,0:T(1,128)S(1)}, f32[1,2]{1,0:T(1,128)}, u32[]{:S(2)}) copy-start(f32[1,2]{1,0:T(1,128)} %pole_weight.1) | copy-start | bytes 28
  13.4 1.3 %collective-permute-start.2 = (f32[128,128]{1,0:T(8,128)S(1)}, f32[128,128]{1,0:T(8,128)S(1)}, u32[]{:S(2)}, u32[]{:S(2)}) collective-permute-start(f32[128,128]{1,0:T(8,128)S(1)} %collective-permute-done.1.refs_3_.refs_5_), channel_id=1, source_target_pairs={{0,1},{1,0},{2,3},{3,2},{4,5},{5,4},{6,7},{7,6},{8,9},{9,8},{10,11... | collective-permute-start | bytes 196616 | tf_op jit(solution)/shard_map/ppermute | solution.py:503
  14.6 1.3 %collective-permute-start.4 = (f32[128,128]{1,0:T(8,128)S(1)}, f32[128,128]{1,0:T(8,128)S(1)}, u32[]{:S(2)}, u32[]{:S(2)}) collective-permute-start(f32[128,128]{1,0:T(8,128)S(1)} %collective-permute-done.3.refs_0_.refs_2_), channel_id=1, source_target_pairs={{0,1},{1,0},{2,3},{3,2},{4,5},{5,4},{6,7},{7,6},{8,9},{9,8},{10,11... | collective-permute-start | bytes 196616 | tf_op jit(solution)/shard_map/ppermute | solution.py:503
  17.3 4.3 %collective-permute-start.6 = (f32[1,2,128,128]{3,2,1,0:T(8,128)S(1)}, f32[1,2,128,128]{3,2,1,0:T(8,128)S(1)}, u32[]{:S(2)}, u32[]{:S(2)}) collective-permute-start(f32[1,2,128,128]{3,2,1,0:T(8,128)S(1)} %collective-permute-done.5.refs_7_), channel_id=1, source_target_pairs={{0,1},{1,0},{2,3},{3,2},{4,5},{5,4},{6,7},{7,6},{8,9},{9,8},{10,11... | collective-permute-start | bytes 393224 | tf_op jit(solution)/shard_map/ppermute | solution.py:503
  27.7 1.9 %collective-permute-start.7 = (f32[2,2,32,128]{3,2,1,0:T(8,128)S(1)}, f32[2,2,32,128]{3,2,1,0:T(8,128)S(1)}, u32[]{:S(2)}, u32[]{:S(2)}) collective-permute-start(f32[2,2,32,128]{3,2,1,0:T(8,128)S(1)} %get-tuple-element.25), channel_id=1, source_target_pairs={{0,1},{1,0},{2,3},{3,2},{4,5},{5,4},{6,7},{7,6},{8,9},{9,8},{10,11... | collective-permute-start | bytes 196616 | tf_op jit(solution)/shard_map/ppermute | solution.py:557
  28.1 4.3 %collective-permute-start.8 = (f32[2,2,32,128]{3,2,1,0:T(8,128)S(1)}, f32[2,2,32,128]{3,2,1,0:T(8,128)S(1)}, u32[]{:S(2)}, u32[]{:S(2)}) collective-permute-start(f32[2,2,32,128]{3,2,1,0:T(8,128)S(1)} %get-tuple-element.26), channel_id=1, source_target_pairs={{0,2},{1,3},{2,0},{3,1},{4,6},{5,7},{6,4},{7,5},{8,10},{9,11},{10,... | collective-permute-start | bytes 196616 | tf_op jit(solution)/shard_map/ppermute | solution.py:557
  29.6 4.3 %collective-permute-start.9 = (f32[2,2,32,128]{3,2,1,0:T(8,128)S(1)}, f32[2,2,32,128]{3,2,1,0:T(8,128)S(1)}, u32[]{:S(2)}, u32[]{:S(2)}) collective-permute-start(f32[2,2,32,128]{3,2,1,0:T(8,128)S(1)} %get-tuple-element.27), channel_id=1, source_target_pairs={{0,3},{1,2},{2,1},{3,0},{4,7},{5,6},{6,5},{7,4},{8,11},{9,10},{10,... | collective-permute-start | bytes 196616 | tf_op jit(solution)/shard_map/ppermute | solution.py:557

commit v7 on v6

--- a/solution.py
+++ b/solution.py
@@ -9,7 +9,7 @@
 
 ROWS = 8
 PANEL = 2 * ROWS
-SPLIT = 2
+SPLIT = 1
 f32, bf16 = jnp.float32, jnp.bfloat16
 PARTS = ((0, 0), (1, 0), (0, 1), (1, 1), (0, 2), (2, 0))
 

time: 34.8 us -> 34.8 us (level)
    pallas_call x1, Pallas kernels: 4.11 us -> 4.72 us  [shards(): pl.pallas_call(advance_on, out_shape=[complex_of] * 2, in_specs=[vmem] *...]
    pallas_call x1, Pallas kernels: 1.48 us -> 0.9 us  [shards(): pl.pallas_call(functools.partial(advance, slabs), out_shape=[complex_of]...]
where the time goes in v7:
time: 34.8 us; the launch traced here: 34.6 us
  Pallas kernels  16.7 us (48%)
  starting transfers between devices  8.44 us (24%)
  waiting for transfers between devices  5.89 us (17%)
  between operations  2.06 us (6%)
  local copies, waits for them, and re-layouts  1.57 us (5%)
    pallas_call x1, Pallas kernels, shards(): pl.pallas_call(functools.partial(finish, slabs, poles), out_shape=[jax.Sh...  6.03 us
    pallas_call x1, Pallas kernels, shards(): pl.pallas_call(advance_on, out_shape=[complex_of] * 2, in_specs=[vmem] *...  4.72 us
    ppermute x3, waiting for transfers between devices, shards(): lax.ppermute(pieces[k], ('pole', 'sub'), [(i, i ^ k) for i in range(poles)])  4.3 us
    pallas_call x1, Pallas kernels, shards(): pl.pallas_call(functools.partial(start_chain, slabs), out_shape=complex_o...  4.1 us
    ppermute x2, starting transfers between devices, swap(): return lax.ppermute(value, 'slab', [(i, i ^ k) for i in range(slabs)])  3.27 us
    ppermute x2, starting transfers between devices, far_swap(): return lax.ppermute(value, ('slab', 'sub'), pairs)  2.92 us
    ppermute x3, starting transfers between devices, shards(): lax.ppermute(pieces[k], ('pole', 'sub'), [(i, i ^ k) for i in range(poles)])  1.94 us
    ppermute x2, waiting for transfers between devices, far_swap(): return lax.ppermute(value, ('slab', 'sub'), pairs)  1.06 us
  transfers between devices with their start and end apart: 10, of which 5 were waited for; matrix products, arithmetic and copies ran while one was open for 0% of the time, Pallas kernels for 30%

profile of v7, /device:TPU:0, one launch (start us, length us, event | category | flops | bytes accessed | tf_op | source)
XLA Modules:
  0.0 34.6 jit_solution(11217296016417902205)
XLA Ops:
  0.6 0.9 %copy-done.1 = f32[1,2,128,128]{3,2,1,0:T(8,128)S(1)} copy-done((f32[1,2,128,128]{3,2,1,0:T(8,128)S(1)}, f32[1,2,128,128]{3,2,1,0:T(8,128)}, u32[]{:S(2)}) %copy-start.1) | copy-done | bytes 131096
  1.6 0.1 shard_map.69.refs_0_
  1.7 3.1 %collective-permute-start = (f32[128,128]{1,0:T(8,128)S(1)}, f32[128,128]{1,0:T(8,128)S(1)}, u32[]{:S(2)}, u32[]{:S(2)}) collective-permute-start(f32[128,128]{1,0:T(8,128)S(1)} %shard_map.69.refs_0_), channel_id=1, source_target_pairs={{0,4},{4,0},{8,12},{12,8},{1,5},{5,1},{9,13},{13,9},{2,6},{6,2},{1... | collective-permute-start | bytes 196616 | tf_op jit(solution)/shard_map/ppermute | solution.py:465
  4.8 2.6 %collective-permute-start.3 = (f32[128,128]{1,0:T(8,128)S(1)}, f32[128,128]{1,0:T(8,128)S(1)}, u32[]{:S(2)}, u32[]{:S(2)}) collective-permute-start(f32[128,128]{1,0:T(8,128)S(1)} %shard_map.69.refs_0_), channel_id=1, source_target_pairs={{0,8},{1,13},{4,12},{5,9},{8,0},{9,5},{12,4},{13,1},{2,10},{3,15},... | collective-permute-start | bytes 196616 | tf_op jit(solution)/shard_map/ppermute | solution.py:484
  7.4 0.3 collective-permute-start.5
  7.7 0.2 collective-permute-start.1
  8.5 0.0 copy-start.2
  9.2 0.1 shard_map.68.pole
  9.3 4.1 %shard_map.70.start = f32[2,128,128]{2,1,0:T(8,128)S(1)} custom-call(f32[8,128]{1,0:T(8,128)S(1)} %shard_map.68.pole, f32[128,128]{1,0:T(8,128)S(1)} %shard_map.69.refs_0_, f32[128,128]{1,0:T(8,128)S(1)} %collective-permute-done.refs_1_), custom_call_target="tpu_custom_call" | custom-call | flops 5000000000 | bytes 2000000 | tf_op jit(solution)/shard_map/pallas_call | solution.py:489
  13.4 0.1 collective-permute-start.2
  13.5 1.1 %collective-permute-done.3.refs_0_.refs_2_ = f32[128,128]{1,0:T(8,128)S(1)} collective-permute-done((f32[128,128]{1,0:T(8,128)S(1)}, f32[128,128]{1,0:T(8,128)S(1)}, u32[]{:S(2)}, u32[]{:S(2)}) %collective-permute-start.3) | collective-permute-done | bytes 65568 | tf_op jit(solution)/shard_map/ppermute | solution.py:484
  14.6 0.2 collective-permute-done.2.refs_4_.refs_6_
  14.7 0.7 %shard_map.72 = (f32[2,128,128]{2,1,0:T(8,128)S(1)}, f32[2,128,128]{2,1,0:T(8,128)S(1)}, f32[2,128,128]{2,1,0:T(8,128)S(1)}) custom-call(f32[8,128]{1,0:T(8,128)S(1)} %shard_map.68.pole, f32[2,128,128]{2,1,0:T(8,128)S(1)} %shard_map.70.start, f32[128,128]{1,0:T(8,128)S(1)} %shard_map.69.refs_0_, f32[128,128]{1,0:T(8,128)S(1)} %collective-permute-done.refs_1_, ...), custom_call_target="tpu_custom_call" | custom-call | flops 1000 | bytes 1000 | tf_op jit(solution)/shard_map/pallas_call | solution.py:510
  15.5 0.3 collective-permute-done.4.refs_1_.refs_3_
  15.8 0.9 %shard_map.73 = (f32[2,128,128]{2,1,0:T(8,128)S(1)}, f32[2,128,128]{2,1,0:T(8,128)S(1)}) custom-call(f32[8,128]{1,0:T(8,128)S(1)} %shard_map.68.pole, f32[2,128,128]{2,1,0:T(8,128)S(1)} %get-tuple-element.16.pivot, f32[128,128]{1,0:T(8,128)S(1)} %collective-permute-done.3.refs_0_.refs_2_, f32[128,128]{1,0:T(8,128)S(1)} %collective-permute-done.4.refs_1_.refs_3_), custom_call_target="tpu_custom_call" | custom-call | flops 1000 | bytes 1000 | tf_op jit(solution)/shard_map/pallas_call | solution.py:519
  16.7 0.2 collective-permute-start.6
  17.0 4.7 %shard_map.74 = (f32[2,128,128]{2,1,0:T(8,128)S(1)}, f32[2,128,128]{2,1,0:T(8,128)S(1)}) custom-call(f32[2,128,128]{2,1,0:T(8,128)S(1)} %get-tuple-element.17.here, f32[2,128,128]{2,1,0:T(8,128)S(1)} %get-tuple-element.18.there), custom_call_target="tpu_custom_call" | custom-call | flops 5000000000 | bytes 2000000 | tf_op jit(solution)/shard_map/pallas_call | solution.py:529
  21.7 6.0 %shard_map.75 = (f32[2,2,32,128]{3,2,1,0:T(8,128)S(1)}, f32[2,2,32,128]{3,2,1,0:T(8,128)S(1)}, f32[2,2,32,128]{3,2,1,0:T(8,128)S(1)}, f32[2,2,32,128]{3,2,1,0:T(8,128)S(1)}) custom-call(f32[8,128]{1,0:T(8,128)S(1)} %shard_map.68.pole, f32[2,128,128]{2,1,0:T(8,128)S(1)} %shard_map.70.start, f32[2,128,128]{2,1,0:T(8,128)S(1)} %get-tuple-element.19.second, ...), custom_call_target="tpu_custom_call" | custom-call | flops 5000000000 | bytes 2000000 | tf_op jit(solution)/shard_map/pallas_call | solution.py:538
  27.7 0.4 %collective-permute-start.7 = (f32[2,2,32,128]{3,2,1,0:T(8,128)S(1)}, f32[2,2,32,128]{3,2,1,0:T(8,128)S(1)}, u32[]{:S(2)}, u32[]{:S(2)}) collective-permute-start(f32[2,2,32,128]{3,2,1,0:T(8,128)S(1)} %get-tuple-element.25), channel_id=1, source_target_pairs={{0,1},{1,0},{2,3},{3,2},{4,5},{5,4},{6,7},{7,6},{8,9},{9,8},{10,11... | collective-permute-start | bytes 196616 | tf_op jit(solution)/shard_map/ppermute | solution.py:557
  28.2 1.5 %collective-permute-start.8 = (f32[2,2,32,128]{3,2,1,0:T(8,128)S(1)}, f32[2,2,32,128]{3,2,1,0:T(8,128)S(1)}, u32[]{:S(2)}, u32[]{:S(2)}) collective-permute-start(f32[2,2,32,128]{3,2,1,0:T(8,128)S(1)} %get-tuple-element.26), channel_id=1, source_target_pairs={{0,2},{1,3},{2,0},{3,1},{4,6},{5,7},{6,4},{7,5},{8,10},{9,11},{10,... | collective-permute-start | bytes 196616 | tf_op jit(solution)/shard_map/ppermute | solution.py:557
  29.6 0.0 collective-permute-start.9
  29.7 2.7 %collective-permute-done.8 = f32[2,2,32,128]{3,2,1,0:T(8,128)S(1)} collective-permute-done((f32[2,2,32,128]{3,2,1,0:T(8,128)S(1)}, f32[2,2,32,128]{3,2,1,0:T(8,128)S(1)}, u32[]{:S(2)}, u32[]{:S(2)}) %collective-permute-start.8) | collective-permute-done | bytes 65568 | tf_op jit(solution)/shard_map/ppermute | solution.py:557
  32.4 1.6 %collective-permute-done.9 = f32[2,2,32,128]{3,2,1,0:T(8,128)S(1)} collective-permute-done((f32[2,2,32,128]{3,2,1,0:T(8,128)S(1)}, f32[2,2,32,128]{3,2,1,0:T(8,128)S(1)}, u32[]{:S(2)}, u32[]{:S(2)}) %collective-permute-start.9) | collective-permute-done | bytes 65568 | tf_op jit(solution)/shard_map/ppermute | solution.py:557
  34.0 0.6 %fusion = (f32[1,2,32,128]{3,2,1,0:T(8,128)}, f32[1,2,32,128]{3,2,1,0:T(8,128)}) fusion(f32[2,2,32,128]{3,2,1,0:T(8,128)S(1)} %add_add_fusion), kind=kLoop, calls=%fused_computation.1 | loop fusion | bytes 131072 | tf_op jit(solution)/shard_map/slice | solution.py:558
  (12 shorter events, 0.0 us)
Async XLA Ops:
  0.6 6.7 %copy-start = (f32[1,2,128,128]{3,2,1,0:T(8,128)S(1)}, f32[1,2,128,128]{3,2,1,0:T(8,128)}, u32[]{:S(2)}) copy-start(f32[1,2,128,128]{3,2,1,0:T(8,128)} %refs_4_.1) | copy-start | bytes 393220
  0.6 0.9 %copy-start.1 = (f32[1,2,128,128]{3,2,1,0:T(8,128)S(1)}, f32[1,2,128,128]{3,2,1,0:T(8,128)}, u32[]{:S(2)}) copy-start(f32[1,2,128,128]{3,2,1,0:T(8,128)} %onsite.1) | copy-start | bytes 393220
  1.7 7.6 %collective-permute-start = (f32[128,128]{1,0:T(8,128)S(1)}, f32[128,128]{1,0:T(8,128)S(1)}, u32[]{:S(2)}, u32[]{:S(2)}) collective-permute-start(f32[128,128]{1,0:T(8,128)S(1)} %shard_map.69.refs_0_), channel_id=1, source_target_pairs={{0,4},{4,0},{8,12},{12,8},{1,5},{5,1},{9,13},{13,9},{2,6},{6,2},{1... | collective-permute-start | bytes 196616 | tf_op jit(solution)/shard_map/ppermute | solution.py:465
  4.8 9.8 %collective-permute-start.3 = (f32[128,128]{1,0:T(8,128)S(1)}, f32[128,128]{1,0:T(8,128)S(1)}, u32[]{:S(2)}, u32[]{:S(2)}) collective-permute-start(f32[128,128]{1,0:T(8,128)S(1)} %shard_map.69.refs_0_), channel_id=1, source_target_pairs={{0,8},{1,13},{4,12},{5,9},{8,0},{9,5},{12,4},{13,1},{2,10},{3,15},... | collective-permute-start | bytes 196616 | tf_op jit(solution)/shard_map/ppermute | solution.py:484
  7.4 9.4 %collective-permute-start.5 = (f32[1,2,128,128]{3,2,1,0:T(8,128)S(1)}, f32[1,2,128,128]{3,2,1,0:T(8,128)S(1)}, u32[]{:S(2)}, u32[]{:S(2)}) collective-permute-start(f32[1,2,128,128]{3,2,1,0:T(8,128)S(1)} %copy-done), channel_id=1, source_target_pairs={{0,8},{1,13},{4,12},{5,9},{8,0},{9,5},{12,4},{13,1},{2,10},{3,15},... | collective-permute-start | bytes 393224 | tf_op jit(solution)/shard_map/ppermute | solution.py:484
  7.7 5.7 %collective-permute-start.1 = (f32[128,128]{1,0:T(8,128)S(1)}, f32[128,128]{1,0:T(8,128)S(1)}, u32[]{:S(2)}, u32[]{:S(2)}) collective-permute-start(f32[128,128]{1,0:T(8,128)S(1)} %shard_map.71), channel_id=1, source_target_pairs={{0,4},{4,0},{8,12},{12,8},{1,5},{5,1},{9,13},{13,9},{2,6},{6,2},{1... | collective-permute-start | bytes 196616 | tf_op jit(solution)/shard_map/ppermute | solution.py:465
  8.5 0.7 %copy-start.2 = (f32[1,2]{1,0:T(1,128)S(1)}, f32[1,2]{1,0:T(1,128)}, u32[]{:S(2)}) copy-start(f32[1,2]{1,0:T(1,128)} %pole_weight.1) | copy-start | bytes 28
  13.4 1.3 %collective-permute-start.2 = (f32[128,128]{1,0:T(8,128)S(1)}, f32[128,128]{1,0:T(8,128)S(1)}, u32[]{:S(2)}, u32[]{:S(2)}) collective-permute-start(f32[128,128]{1,0:T(8,128)S(1)} %collective-permute-done.1.refs_3_.refs_5_), channel_id=1, source_target_pairs={{0,1},{1,0},{2,3},{3,2},{4,5},{5,4},{6,7},{7,6},{8,9},{9,8},{10,11... | collective-permute-start | bytes 196616 | tf_op jit(solution)/shard_map/ppermute | solution.py:503
  14.6 1.3 %collective-permute-start.4 = (f32[128,128]{1,0:T(8,128)S(1)}, f32[128,128]{1,0:T(8,128)S(1)}, u32[]{:S(2)}, u32[]{:S(2)}) collective-permute-start(f32[128,128]{1,0:T(8,128)S(1)} %collective-permute-done.3.refs_0_.refs_2_), channel_id=1, source_target_pairs={{0,1},{1,0},{2,3},{3,2},{4,5},{5,4},{6,7},{7,6},{8,9},{9,8},{10,11... | collective-permute-start | bytes 196616 | tf_op jit(solution)/shard_map/ppermute | solution.py:503
  16.7 5.0 %collective-permute-start.6 = (f32[1,2,128,128]{3,2,1,0:T(8,128)S(1)}, f32[1,2,128,128]{3,2,1,0:T(8,128)S(1)}, u32[]{:S(2)}, u32[]{:S(2)}) collective-permute-start(f32[1,2,128,128]{3,2,1,0:T(8,128)S(1)} %collective-permute-done.5.refs_7_), channel_id=1, source_target_pairs={{0,1},{1,0},{2,3},{3,2},{4,5},{5,4},{6,7},{7,6},{8,9},{9,8},{10,11... | collective-permute-start | bytes 393224 | tf_op jit(solution)/shard_map/ppermute | solution.py:503
  27.7 1.9 %collective-permute-start.7 = (f32[2,2,32,128]{3,2,1,0:T(8,128)S(1)}, f32[2,2,32,128]{3,2,1,0:T(8,128)S(1)}, u32[]{:S(2)}, u32[]{:S(2)}) collective-permute-start(f32[2,2,32,128]{3,2,1,0:T(8,128)S(1)} %get-tuple-element.25), channel_id=1, source_target_pairs={{0,1},{1,0},{2,3},{3,2},{4,5},{5,4},{6,7},{7,6},{8,9},{9,8},{10,11... | collective-permute-start | bytes 196616 | tf_op jit(solution)/shard_map/ppermute | solution.py:557
  28.2 4.3 %collective-permute-start.8 = (f32[2,2,32,128]{3,2,1,0:T(8,128)S(1)}, f32[2,2,32,128]{3,2,1,0:T(8,128)S(1)}, u32[]{:S(2)}, u32[]{:S(2)}) collective-permute-start(f32[2,2,32,128]{3,2,1,0:T(8,128)S(1)} %get-tuple-element.26), channel_id=1, source_target_pairs={{0,2},{1,3},{2,0},{3,1},{4,6},{5,7},{6,4},{7,5},{8,10},{9,11},{10,... | collective-permute-start | bytes 196616 | tf_op jit(solution)/shard_map/ppermute | solution.py:557
  29.6 4.3 %collective-permute-start.9 = (f32[2,2,32,128]{3,2,1,0:T(8,128)S(1)}, f32[2,2,32,128]{3,2,1,0:T(8,128)S(1)}, u32[]{:S(2)}, u32[]{:S(2)}) collective-permute-start(f32[2,2,32,128]{3,2,1,0:T(8,128)S(1)} %get-tuple-element.27), channel_id=1, source_target_pairs={{0,3},{1,2},{2,1},{3,0},{4,7},{5,6},{6,5},{7,4},{8,11},{9,10},{10,... | collective-permute-start | bytes 196616 | tf_op jit(solution)/shard_map/ppermute | solution.py:557
